TPU v7x, 32 devices: a whole 2x2x4 slice. The times are simulated.
32 devices in a mesh: space: 16 (over z, y, core), bead: 2 (over x).
Axes of the slice: x: 2, y: 2, z: 4, core: 2. Of those that a mesh axis runs over, the one named last changes fastest.
Arguments:
- positions: float32 [8, 3, 1536], P('bead', None, 'space'), may hold values from -6 to 6
- momenta: float32 [8, 3, 1536], P('bead', None, 'space'), may hold values from -6 to 6
- neighbours: int32 [1536, 64], P('space'), may hold values from 0 to 479, as said below
- nbr_count: int32 [1536], P('space'), may hold values from 32 to 64
- send_rows: int32 [16, 4, 96], P('space'), may hold values from -1 to 95, as said below
- embed_first: float32 [2, 128], replicated, may hold values from -6 to 6
- embed_weight: bfloat16 [128, 128], replicated, may hold values from -0.5 to 0.5
- embed_bias: float32 [128], replicated, may hold values from -3 to 3
- fit_weight: bfloat16 [2048, 240], replicated, may hold values from -0.125 to 0.125
- fit_bias: float32 [240], replicated, may hold values from -3 to 3
- fit_weight2: bfloat16 [240, 240], replicated, may hold values from -0.375 to 0.375
- fit_bias2: float32 [240], replicated, may hold values from -3 to 3
- fit_out: float32 [240], replicated, may hold values from -0.375 to 0.375
Outputs:
- new_positions: float32 [8, 3, 1536], P('bead', None, 'space')
- new_momenta: float32 [8, 3, 1536], P('bead', None, 'space')
Inputs may be any that keep to these rules, and one draw needn't show every extreme that they name: `neighbours`: an entry below 96 names another own atom of the domain; an entry 96 + j * 96 + s names ghost slot s of block j, and that slot holds an atom. Entries past nbr_count are padding of the same kind. `send_rows`: -1 marks an empty slot. In each block the filled slots come first and name distinct atoms; blocks toward a domain that does not exist are empty; in every draw some block is full.
All inputs are finite; a program needn't handle non-finite values.
Results may differ from a plain program's by a relative error of at most 0.03.
Values sent between devices are 32-bit elements; how exact they have to be, the bound alone decides.
No kernel may reach another device: no remote copies, remote signals or barrier semaphores. Data moves between devices by JAX's collectives and lax.ppermute only.
A program may use at most 64 MiB of HBM per device.

v0:
```python
import jax
import jax.numpy as jnp
import numpy as np
from jax import lax
from jax.sharding import PartitionSpec as P

AXIS = 16


cycle_freq = 0.5
time_step = 1.0
soften = 0.25
force_gain = 64.0


def passed_along(value, axis, steps):
    count = lax.axis_size(axis)
    first, last = (max(0, -steps), min(count, count - steps))
    return lax.ppermute(value, axis, [(source, source + steps) for source in range(first, last)])


def mode_maps(beads):
    column = np.arange(beads)[None, :]
    bead_row = np.arange(beads)[:, None]
    phases = 2.0 * np.pi * bead_row * column / beads
    mode_basis = np.where(
        column == 0,
        1.0 / np.sqrt(beads),
        np.where(
            2 * column < beads,
            np.sqrt(2.0 / beads) * np.cos(phases),
            np.where(
                2 * column == beads,
                np.cos(phases) / np.sqrt(beads),
                np.sqrt(2.0 / beads) * np.sin(phases),
            ),
        ),
    )
    frequency = 2.0 * cycle_freq * np.sin(np.pi * np.arange(beads) / beads)
    angles = frequency * time_step
    safe_freq = np.where(frequency > 0, frequency, 1.0)
    cosine = np.cos(angles)
    drift = np.where(frequency > 0, np.sin(angles) / safe_freq, time_step)
    pull = -frequency * np.sin(angles)
    keep_map = mode_basis * cosine[None, :] @ mode_basis.T
    drift_map = mode_basis * drift[None, :] @ mode_basis.T
    pull_map = mode_basis * pull[None, :] @ mode_basis.T
    return (
        jnp.asarray(keep_map, jnp.float32),
        jnp.asarray(drift_map, jnp.float32),
        jnp.asarray(pull_map, jnp.float32),
    )


def site_energy(
    coord_table,
    neighbours,
    nbr_count,
    embed_first,
    embed_weight,
    embed_bias,
    fit_weight,
    fit_bias,
    fit_weight2,
    fit_bias2,
    fit_out,
):
    owned = neighbours.shape[0]
    listed = neighbours.shape[1]
    centre = coord_table[:, :owned]
    nearby = jnp.take(coord_table, neighbours, axis=1)
    offset_vec = nearby - centre[:, :, None]
    inverse = lax.rsqrt(jnp.sum(offset_vec * offset_vec, axis=0) + soften)
    active = (jnp.arange(listed)[None, :] < nbr_count[:, None]).astype(jnp.float32)
    smooth = inverse * active
    radial = jnp.concatenate([smooth[None], smooth[None] * inverse[None] * offset_vec], axis=0)
    embed_one = jnp.tanh(smooth[:, :, None] * embed_first[0] + embed_first[1])
    embed_low = embed_one.astype(jnp.bfloat16).reshape(owned * listed, -1)
    product = jnp.dot(embed_low, embed_weight, preferred_element_type=jnp.float32)
    second = embed_one + jnp.tanh(product.reshape(owned, listed, -1) + embed_bias)
    moment = jnp.einsum("xan,ane->axe", radial, second, precision=lax.Precision.HIGHEST) / listed
    descriptor = jnp.einsum(
        "axe,axf->aef", moment, moment[:, :, :AXIS], precision=lax.Precision.HIGHEST
    ).reshape(owned, -1)
    hidden = jnp.tanh(
        jnp.dot(descriptor.astype(jnp.bfloat16), fit_weight, preferred_element_type=jnp.float32)
        + fit_bias
    )
    hidden_two = hidden + jnp.tanh(
        jnp.dot(hidden.astype(jnp.bfloat16), fit_weight2, preferred_element_type=jnp.float32)
        + fit_bias2
    )
    return jnp.sum(hidden_two * fit_out)


def bead_forces(coord_table, neighbours, nbr_count, *params):
    return -jax.grad(site_energy)(coord_table, neighbours, nbr_count, *params)


def apply_maps(keep_map, drift_map, pull_map, stacked):
    highest = lax.Precision.HIGHEST
    moved = jnp.dot(keep_map, stacked[0], precision=highest) + jnp.dot(
        drift_map, stacked[1], precision=highest
    )
    pulled = jnp.dot(pull_map, stacked[0], precision=highest) + jnp.dot(
        keep_map, stacked[1], precision=highest
    )
    return jnp.stack([moved, pulled])


def on_device(
    positions,
    momenta,
    neighbours,
    nbr_count,
    send_rows,
    embed_first,
    embed_weight,
    embed_bias,
    fit_weight,
    fit_bias,
    fit_weight2,
    fit_bias2,
    fit_out,
):
    params = (
        embed_first,
        embed_weight,
        embed_bias,
        fit_weight,
        fit_bias,
        fit_weight2,
        fit_bias2,
        fit_out,
    )
    bead_dev, components, owned = positions.shape
    blocks = send_rows.shape[1]
    half_blocks = blocks // 2
    slot_count = send_rows.shape[2]
    strides = list(range(-half_blocks, 0)) + list(range(1, half_blocks + 1))
    flat_coords = positions.reshape(bead_dev * components, owned)
    filled = (send_rows[0] >= 0).astype(jnp.float32)
    picked = jnp.maximum(send_rows[0], 0)
    packet = jnp.take(flat_coords, picked, axis=1) * filled[None]
    ghosts = jnp.stack(
        [passed_along(packet[:, column], "space", stride) for column, stride in enumerate(strides)],
        axis=1,
    )
    coord_table = jnp.concatenate([flat_coords, ghosts.reshape(bead_dev * components, -1)], axis=1)
    coord_table = coord_table.reshape(bead_dev, components, -1)

    def per_bead(single):
        return bead_forces(single, neighbours, nbr_count, *params)

    forces = lax.map(per_bead, coord_table).reshape(bead_dev * components, -1)
    own_force = forces[:, :owned]
    ghost_force = forces[:, owned:].reshape(bead_dev * components, blocks, slot_count)
    returned = jnp.stack(
        [
            passed_along(ghost_force[:, column], "space", -stride)
            for column, stride in enumerate(strides)
        ],
        axis=1,
    )
    returned = returned * filled[None]
    own_force = own_force.at[:, picked.reshape(-1)].add(returned.reshape(bead_dev * components, -1))
    kicked = momenta + time_step * force_gain * own_force.reshape(positions.shape)
    beads = lax.axis_size("bead") * bead_dev
    keep_map, drift_map, pull_map = mode_maps(beads)
    width = components * owned
    stacked = jnp.stack([positions.reshape(bead_dev, width), kicked.reshape(bead_dev, width)])
    spread = lax.all_to_all(stacked, "bead", split_axis=2, concat_axis=1, tiled=True)
    mapped = apply_maps(keep_map, drift_map, pull_map, spread)
    result = lax.all_to_all(mapped, "bead", split_axis=1, concat_axis=2, tiled=True)
    return (result[0].reshape(positions.shape), result[1].reshape(positions.shape))


def solution(mesh):
    in_specs = (
        P("bead", None, "space"),
        P("bead", None, "space"),
        P("space", None),
        P("space"),
        P("space", None, None),
        P(),
        P(),
        P(),
        P(),
        P(),
        P(),
        P(),
        P(),
    )
    out_specs = (P("bead", None, "space"), P("bead", None, "space"))
    return jax.shard_map(
        on_device, mesh=mesh, in_specs=in_specs, out_specs=out_specs, check_vma=False
    )
```

profile of v0, /device:TPU:8, one launch (start us, length us, event | category | flops | bytes accessed | tf_op | source)
XLA Modules:
  0.0 446.2 jit_solution(10828528761699792861)
XLA Ops:
  7.2 4.5 %collective-permute-start.1 = (f32[12,96]{1,0:T(8,128)S(1)}, f32[12,96]{1,0:T(8,128)S(1)}, u32[]{:S(2)}, u32[]{:S(2)}) collective-permute-start(f32[12,96]{1,0:T(8,128)S(1)} %get-tuple-element.165), channel_id=1, source_target_pairs={{2,0},{4,2},{6,4},{8,6},{10,8},{12,10},{14,12},{16,14},{18,16},{20... | collective-permute-start | bytes 13832 | tf_op jit(solution)/shard_map/ppermute | solution.py:19
  21.5 387.2 %while.10 = (s32[]{:T(128)}, f32[4,3,480]{2,1,0:T(4,128)}, s32[96]{0:T(128)}, s32[96,64]{1,0:T(8,128)S(1)}, f32[4,3,480]{2,1,0:T(4,128)}, /*index=5*/f32[2,128]{...) while((s32[]{:T(128)}, f32[4,3,480]{2,1,0:T(4,128)}, ...), condition=%wide.region_6.7_spmd, body=%wide.region_0.6_spmd.sunk | while | flops 777730432 | bytes 38690104 | solution.py:155
  23.8 16.1 %gather_fusion = f32[6144,3]{1,0:T(8,128)S(1)} fusion(f32[3,480]{0,1:T(8,128)S(1)} %bitcast.182, s32[6144]{0:T(1024)S(1)} %broadcast_clamp_fusion.2), kind=kCustom, calls=%fused_computation.clone.1 | custom fusion | bytes 172032 | tf_op jit(solution)/shard_map/while/body/eval_jaxpr/jvp(jit(_take))/gather | solution.py:71
  43.6 3.9 fusion.155
  66.6 6.0 %fusion.160 = f32[4,96,64]{2,0,1:T(4,128)S(1)} fusion(f32[96,4,128]{2,1,0:T(4,128)S(1)} %fusion.159, f32[96,64,128]{2,1,0:T(8,128)S(1)} %fusion.153, f32[128]{0:T(128)} %get-tuple-element.309, f32[128]{0:T(128)} %copy-done.23, f32[128]{0:T(128)} %copy-done.21, f32[96,64]{1,0:T(8,128)} %copy-done.7), kind=kOutput, calls=%fused_computation.32.clone.1 | convolution fusion | flops 40894464 | bytes 3466752 | tf_op jit(solution)/shard_map/while/body/eval_jaxpr/transpose(jvp(xan,ane->axe))/dot_general | solution.py:81
  72.7 5.2 %multiply_multiply_fusion.2 = (bf16[96,64,128]{2,1,0:T(8,128)(2,1)S(1)}, f32[96,64,128]{2,1,0:T(8,128)S(1)}) fusion(f32[96,64,128]{2,1,0:T(8,128)S(1)} %fusion.153, f32[128]{0:T(128)S(1)} %copy-done.26, f32[96,4,128]{2,1,0:T(4,128)S(1)} %fusion.159, f32[3,96,64]{2,0,1:T(4,128)S(1)} %copy-done.6, f32[1,96,64]{2,0,1:T(1,128)S(1)} %bitcast.191), kind=kOutput, calls=%fused_computation.9.clone.1 | convolution fusion | flops 42491904 | bytes 8159744 | tf_op jit(solution)/shard_map/while/body/eval_jaxpr/transpose(jvp(xan,ane->axe))/dot_general | solution.py:81
  84.2 33.3 %scatter_fusion = f32[3,480]{0,1:T(8,128)S(1)} fusion(f32[3,480]{0,1:T(8,128)S(1)} %pad.61, s32[6144]{0:T(1024)S(1)} %copy-done.12, f32[6144,3]{1,0:T(8,128)S(1)} %bitcast.185), kind=kCustom, calls=%fused_computation.2.clone.1 | custom fusion | flops 18432 | bytes 245760 | tf_op jit(solution)/shard_map/while/body/eval_jaxpr/transpose(jvp(jit(_take)))/scatter-add | solution.py:71
  120.6 16.1 %gather_fusion = f32[6144,3]{1,0:T(8,128)S(1)} fusion(f32[3,480]{0,1:T(8,128)S(1)} %bitcast.182, s32[6144]{0:T(1024)S(1)} %broadcast_clamp_fusion.2), kind=kCustom, calls=%fused_computation.clone.1 | custom fusion | bytes 172032 | tf_op jit(solution)/shard_map/while/body/eval_jaxpr/jvp(jit(_take))/gather | solution.py:71
  140.4 3.9 fusion.155
  163.4 6.0 %fusion.160 = f32[4,96,64]{2,0,1:T(4,128)S(1)} fusion(f32[96,4,128]{2,1,0:T(4,128)S(1)} %fusion.159, f32[96,64,128]{2,1,0:T(8,128)S(1)} %fusion.153, f32[128]{0:T(128)} %get-tuple-element.309, f32[128]{0:T(128)} %copy-done.23, f32[128]{0:T(128)} %copy-done.21, f32[96,64]{1,0:T(8,128)} %copy-done.7), kind=kOutput, calls=%fused_computation.32.clone.1 | convolution fusion | flops 40894464 | bytes 3466752 | tf_op jit(solution)/shard_map/while/body/eval_jaxpr/transpose(jvp(xan,ane->axe))/dot_general | solution.py:81
  169.5 5.2 %multiply_multiply_fusion.2 = (bf16[96,64,128]{2,1,0:T(8,128)(2,1)S(1)}, f32[96,64,128]{2,1,0:T(8,128)S(1)}) fusion(f32[96,64,128]{2,1,0:T(8,128)S(1)} %fusion.153, f32[128]{0:T(128)S(1)} %copy-done.26, f32[96,4,128]{2,1,0:T(4,128)S(1)} %fusion.159, f32[3,96,64]{2,0,1:T(4,128)S(1)} %copy-done.6, f32[1,96,64]{2,0,1:T(1,128)S(1)} %bitcast.191), kind=kOutput, calls=%fused_computation.9.clone.1 | convolution fusion | flops 42491904 | bytes 8159744 | tf_op jit(solution)/shard_map/while/body/eval_jaxpr/transpose(jvp(xan,ane->axe))/dot_general | solution.py:81
  181.0 33.3 %scatter_fusion = f32[3,480]{0,1:T(8,128)S(1)} fusion(f32[3,480]{0,1:T(8,128)S(1)} %pad.61, s32[6144]{0:T(1024)S(1)} %copy-done.12, f32[6144,3]{1,0:T(8,128)S(1)} %bitcast.185), kind=kCustom, calls=%fused_computation.2.clone.1 | custom fusion | flops 18432 | bytes 245760 | tf_op jit(solution)/shard_map/while/body/eval_jaxpr/transpose(jvp(jit(_take)))/scatter-add | solution.py:71
  217.4 16.1 %gather_fusion = f32[6144,3]{1,0:T(8,128)S(1)} fusion(f32[3,480]{0,1:T(8,128)S(1)} %bitcast.182, s32[6144]{0:T(1024)S(1)} %broadcast_clamp_fusion.2), kind=kCustom, calls=%fused_computation.clone.1 | custom fusion | bytes 172032 | tf_op jit(solution)/shard_map/while/body/eval_jaxpr/jvp(jit(_take))/gather | solution.py:71
  237.2 3.9 fusion.155
  260.2 6.0 %fusion.160 = f32[4,96,64]{2,0,1:T(4,128)S(1)} fusion(f32[96,4,128]{2,1,0:T(4,128)S(1)} %fusion.159, f32[96,64,128]{2,1,0:T(8,128)S(1)} %fusion.153, f32[128]{0:T(128)} %get-tuple-element.309, f32[128]{0:T(128)} %copy-done.23, f32[128]{0:T(128)} %copy-done.21, f32[96,64]{1,0:T(8,128)} %copy-done.7), kind=kOutput, calls=%fused_computation.32.clone.1 | convolution fusion | flops 40894464 | bytes 3466752 | tf_op jit(solution)/shard_map/while/body/eval_jaxpr/transpose(jvp(xan,ane->axe))/dot_general | solution.py:81
  266.3 5.2 %multiply_multiply_fusion.2 = (bf16[96,64,128]{2,1,0:T(8,128)(2,1)S(1)}, f32[96,64,128]{2,1,0:T(8,128)S(1)}) fusion(f32[96,64,128]{2,1,0:T(8,128)S(1)} %fusion.153, f32[128]{0:T(128)S(1)} %copy-done.26, f32[96,4,128]{2,1,0:T(4,128)S(1)} %fusion.159, f32[3,96,64]{2,0,1:T(4,128)S(1)} %copy-done.6, f32[1,96,64]{2,0,1:T(1,128)S(1)} %bitcast.191), kind=kOutput, calls=%fused_computation.9.clone.1 | convolution fusion | flops 42491904 | bytes 8159744 | tf_op jit(solution)/shard_map/while/body/eval_jaxpr/transpose(jvp(xan,ane->axe))/dot_general | solution.py:81
  277.8 33.3 %scatter_fusion = f32[3,480]{0,1:T(8,128)S(1)} fusion(f32[3,480]{0,1:T(8,128)S(1)} %pad.61, s32[6144]{0:T(1024)S(1)} %copy-done.12, f32[6144,3]{1,0:T(8,128)S(1)} %bitcast.185), kind=kCustom, calls=%fused_computation.2.clone.1 | custom fusion | flops 18432 | bytes 245760 | tf_op jit(solution)/shard_map/while/body/eval_jaxpr/transpose(jvp(jit(_take)))/scatter-add | solution.py:71
  314.2 16.1 %gather_fusion = f32[6144,3]{1,0:T(8,128)S(1)} fusion(f32[3,480]{0,1:T(8,128)S(1)} %bitcast.182, s32[6144]{0:T(1024)S(1)} %broadcast_clamp_fusion.2), kind=kCustom, calls=%fused_computation.clone.1 | custom fusion | bytes 172032 | tf_op jit(solution)/shard_map/while/body/eval_jaxpr/jvp(jit(_take))/gather | solution.py:71
  334.0 3.9 fusion.155
  357.0 6.0 %fusion.160 = f32[4,96,64]{2,0,1:T(4,128)S(1)} fusion(f32[96,4,128]{2,1,0:T(4,128)S(1)} %fusion.159, f32[96,64,128]{2,1,0:T(8,128)S(1)} %fusion.153, f32[128]{0:T(128)} %get-tuple-element.309, f32[128]{0:T(128)} %copy-done.23, f32[128]{0:T(128)} %copy-done.21, f32[96,64]{1,0:T(8,128)} %copy-done.7), kind=kOutput, calls=%fused_computation.32.clone.1 | convolution fusion | flops 40894464 | bytes 3466752 | tf_op jit(solution)/shard_map/while/body/eval_jaxpr/transpose(jvp(xan,ane->axe))/dot_general | solution.py:81
  363.1 5.2 %multiply_multiply_fusion.2 = (bf16[96,64,128]{2,1,0:T(8,128)(2,1)S(1)}, f32[96,64,128]{2,1,0:T(8,128)S(1)}) fusion(f32[96,64,128]{2,1,0:T(8,128)S(1)} %fusion.153, f32[128]{0:T(128)S(1)} %copy-done.26, f32[96,4,128]{2,1,0:T(4,128)S(1)} %fusion.159, f32[3,96,64]{2,0,1:T(4,128)S(1)} %copy-done.6, f32[1,96,64]{2,0,1:T(1,128)S(1)} %bitcast.191), kind=kOutput, calls=%fused_computation.9.clone.1 | convolution fusion | flops 42491904 | bytes 8159744 | tf_op jit(solution)/shard_map/while/body/eval_jaxpr/transpose(jvp(xan,ane->axe))/dot_general | solution.py:81
  374.6 33.3 %scatter_fusion = f32[3,480]{0,1:T(8,128)S(1)} fusion(f32[3,480]{0,1:T(8,128)S(1)} %pad.61, s32[6144]{0:T(1024)S(1)} %copy-done.12, f32[6144,3]{1,0:T(8,128)S(1)} %bitcast.185), kind=kCustom, calls=%fused_computation.2.clone.1 | custom fusion | flops 18432 | bytes 245760 | tf_op jit(solution)/shard_map/while/body/eval_jaxpr/transpose(jvp(jit(_take)))/scatter-add | solution.py:71
  427.1 6.4 %all_to_all.30 = f32[2,1,1152]{2,1,0:T(1,128)S(1)} all-to-all(f32[2,1,1152]{2,1,0:T(1,128)S(1)} %reshape.285), channel_id=1, replica_groups=mesh['space'=16,'bead'=2] {'bead'}, dimensions={0} | all-to-all | bytes 18432 | tf_op jit(solution)/shard_map/all_to_all | solution.py:172
  438.7 6.2 %all_to_all.31 = f32[2,8,144]{2,0,1:T(2,128)S(1)} all-to-all(f32[2,8,144]{2,0,1:T(2,128)S(1)} %copy.119), channel_id=1, replica_groups=mesh['space'=16,'bead'=2] {'bead'}, dimensions={1} | all-to-all | bytes 18432 | tf_op jit(solution)/shard_map/all_to_all | solution.py:174
  (430 shorter events, 168.3 us)
Async XLA Ops:
  5.3 13.2 %collective-permute-start.2 = (f32[12,96]{1,0:T(8,128)S(1)}, f32[12,96]{1,0:T(8,128)S(1)}, u32[]{:S(2)}, u32[]{:S(2)}) collective-permute-start(f32[12,96]{1,0:T(8,128)S(1)} %get-tuple-element.164), channel_id=1, source_target_pairs={{0,2},{2,4},{4,6},{6,8},{8,10},{10,12},{12,14},{14,16},{16,18},{18... | collective-permute-start | bytes 13832 | tf_op jit(solution)/shard_map/ppermute | solution.py:19
  7.2 11.3 %collective-permute-start.1 = (f32[12,96]{1,0:T(8,128)S(1)}, f32[12,96]{1,0:T(8,128)S(1)}, u32[]{:S(2)}, u32[]{:S(2)}) collective-permute-start(f32[12,96]{1,0:T(8,128)S(1)} %get-tuple-element.165), channel_id=1, source_target_pairs={{2,0},{4,2},{6,4},{8,6},{10,8},{12,10},{14,12},{16,14},{18,16},{20... | collective-permute-start | bytes 13832 | tf_op jit(solution)/shard_map/ppermute | solution.py:19
  11.8 6.8 %collective-permute-start = (f32[12,96]{1,0:T(8,128)S(1)}, f32[12,96]{1,0:T(8,128)S(1)}, u32[]{:S(2)}, u32[]{:S(2)}) collective-permute-start(f32[12,96]{1,0:T(8,128)S(1)} %get-tuple-element.162), channel_id=1, source_target_pairs={{4,0},{6,2},{8,4},{10,6},{12,8},{14,10},{16,12},{18,14},{20,16},{2... | collective-permute-start | bytes 13832 | tf_op jit(solution)/shard_map/ppermute | solution.py:19
  14.2 6.4 %collective-permute-start.3 = (f32[12,96]{1,0:T(8,128)S(1)}, f32[12,96]{1,0:T(8,128)S(1)}, u32[]{:S(2)}, u32[]{:S(2)}) collective-permute-start(f32[12,96]{1,0:T(8,128)S(1)} %get-tuple-element.163), channel_id=1, source_target_pairs={{0,4},{2,6},{4,8},{6,10},{8,12},{10,14},{12,16},{14,18},{16,20},{1... | collective-permute-start | bytes 13832 | tf_op jit(solution)/shard_map/ppermute | solution.py:19
  21.5 21.2 %copy-start.13 = (s32[96,64]{1,0:T(8,128)}, s32[96,64]{1,0:T(8,128)S(1)}, u32[]{:S(2)}) copy-start(s32[96,64]{1,0:T(8,128)S(1)} %get-tuple-element.305) | copy-start | bytes 73732 | tf_op jit(solution)/shard_map/while
  22.2 20.4 %copy-start.21 = (f32[128]{0:T(128)}, f32[128]{0:T(128)S(1)}, u32[]{:S(2)}) copy-start(f32[128]{0:T(128)S(1)} %get-tuple-element.265) | copy-start | bytes 1540 | tf_op jit(solution)/shard_map/while
  22.3 20.4 %copy-start.23 = (f32[128]{0:T(128)}, f32[128]{0:T(128)S(1)}, u32[]{:S(2)}) copy-start(f32[128]{0:T(128)S(1)} %get-tuple-element.264) | copy-start | bytes 1540 | tf_op jit(solution)/shard_map/while
  82.2 36.1 %copy-start.14 = (s32[96,64]{1,0:T(8,128)S(1)}, s32[96,64]{1,0:T(8,128)}, u32[]{:S(2)}) copy-start(s32[96,64]{1,0:T(8,128)} %copy-done.13) | copy-start | bytes 73732 | tf_op jit(solution)/shard_map/while
  118.3 21.2 %copy-start.13 = (s32[96,64]{1,0:T(8,128)}, s32[96,64]{1,0:T(8,128)S(1)}, u32[]{:S(2)}) copy-start(s32[96,64]{1,0:T(8,128)S(1)} %get-tuple-element.305) | copy-start | bytes 73732 | tf_op jit(solution)/shard_map/while
  119.0 20.4 %copy-start.21 = (f32[128]{0:T(128)}, f32[128]{0:T(128)S(1)}, u32[]{:S(2)}) copy-start(f32[128]{0:T(128)S(1)} %get-tuple-element.265) | copy-start | bytes 1540 | tf_op jit(solution)/shard_map/while
  119.0 20.4 %copy-start.23 = (f32[128]{0:T(128)}, f32[128]{0:T(128)S(1)}, u32[]{:S(2)}) copy-start(f32[128]{0:T(128)S(1)} %get-tuple-element.264) | copy-start | bytes 1540 | tf_op jit(solution)/shard_map/while
  179.0 36.1 %copy-start.14 = (s32[96,64]{1,0:T(8,128)S(1)}, s32[96,64]{1,0:T(8,128)}, u32[]{:S(2)}) copy-start(s32[96,64]{1,0:T(8,128)} %copy-done.13) | copy-start | bytes 73732 | tf_op jit(solution)/shard_map/while
  215.1 21.2 %copy-start.13 = (s32[96,64]{1,0:T(8,128)}, s32[96,64]{1,0:T(8,128)S(1)}, u32[]{:S(2)}) copy-start(s32[96,64]{1,0:T(8,128)S(1)} %get-tuple-element.305) | copy-start | bytes 73732 | tf_op jit(solution)/shard_map/while
  215.8 20.4 %copy-start.21 = (f32[128]{0:T(128)}, f32[128]{0:T(128)S(1)}, u32[]{:S(2)}) copy-start(f32[128]{0:T(128)S(1)} %get-tuple-element.265) | copy-start | bytes 1540 | tf_op jit(solution)/shard_map/while
  215.8 20.4 %copy-start.23 = (f32[128]{0:T(128)}, f32[128]{0:T(128)S(1)}, u32[]{:S(2)}) copy-start(f32[128]{0:T(128)S(1)} %get-tuple-element.264) | copy-start | bytes 1540 | tf_op jit(solution)/shard_map/while
  275.8 36.1 %copy-start.14 = (s32[96,64]{1,0:T(8,128)S(1)}, s32[96,64]{1,0:T(8,128)}, u32[]{:S(2)}) copy-start(s32[96,64]{1,0:T(8,128)} %copy-done.13) | copy-start | bytes 73732 | tf_op jit(solution)/shard_map/while
  311.9 21.2 %copy-start.13 = (s32[96,64]{1,0:T(8,128)}, s32[96,64]{1,0:T(8,128)S(1)}, u32[]{:S(2)}) copy-start(s32[96,64]{1,0:T(8,128)S(1)} %get-tuple-element.305) | copy-start | bytes 73732 | tf_op jit(solution)/shard_map/while
  312.6 20.4 %copy-start.21 = (f32[128]{0:T(128)}, f32[128]{0:T(128)S(1)}, u32[]{:S(2)}) copy-start(f32[128]{0:T(128)S(1)} %get-tuple-element.265) | copy-start | bytes 1540 | tf_op jit(solution)/shard_map/while
  312.6 20.4 %copy-start.23 = (f32[128]{0:T(128)}, f32[128]{0:T(128)S(1)}, u32[]{:S(2)}) copy-start(f32[128]{0:T(128)S(1)} %get-tuple-element.264) | copy-start | bytes 1540 | tf_op jit(solution)/shard_map/while
  372.6 36.1 %copy-start.14 = (s32[96,64]{1,0:T(8,128)S(1)}, s32[96,64]{1,0:T(8,128)}, u32[]{:S(2)}) copy-start(s32[96,64]{1,0:T(8,128)} %copy-done.13) | copy-start | bytes 73732 | tf_op jit(solution)/shard_map/while
  409.7 11.9 %collective-permute-start.7 = (f32[12,96]{1,0:T(8,128)S(1)}, f32[12,96]{1,0:T(8,128)S(1)}, u32[]{:S(2)}, u32[]{:S(2)}) collective-permute-start(f32[12,96]{1,0:T(8,128)S(1)} %bitcast.199), channel_id=1, source_target_pairs={{4,0},{6,2},{8,4},{10,6},{12,8},{14,10},{16,12},{18,14},{20,16},{2... | collective-permute-start | bytes 13832 | tf_op jit(solution)/shard_map/ppermute | solution.py:19
  411.6 10.0 %collective-permute-start.6 = (f32[12,96]{1,0:T(8,128)S(1)}, f32[12,96]{1,0:T(8,128)S(1)}, u32[]{:S(2)}, u32[]{:S(2)}) collective-permute-start(f32[12,96]{1,0:T(8,128)S(1)} %bitcast.200), channel_id=1, source_target_pairs={{2,0},{4,2},{6,4},{8,6},{10,8},{12,10},{14,12},{16,14},{18,16},{20... | collective-permute-start | bytes 13832 | tf_op jit(solution)/shard_map/ppermute | solution.py:19
  413.5 8.0 %collective-permute-start.5 = (f32[12,96]{1,0:T(8,128)S(1)}, f32[12,96]{1,0:T(8,128)S(1)}, u32[]{:S(2)}, u32[]{:S(2)}) collective-permute-start(f32[12,96]{1,0:T(8,128)S(1)} %bitcast.201), channel_id=1, source_target_pairs={{0,2},{2,4},{4,6},{6,8},{8,10},{10,12},{12,14},{14,16},{16,18},{18... | collective-permute-start | bytes 13832 | tf_op jit(solution)/shard_map/ppermute | solution.py:19
  416.0 6.4 %collective-permute-start.4 = (f32[12,96]{1,0:T(8,128)S(1)}, f32[12,96]{1,0:T(8,128)S(1)}, u32[]{:S(2)}, u32[]{:S(2)}) collective-permute-start(f32[12,96]{1,0:T(8,128)S(1)} %bitcast.203), channel_id=1, source_target_pairs={{0,4},{2,6},{4,8},{6,10},{8,12},{10,14},{12,16},{14,18},{16,20},{1... | collective-permute-start | bytes 13832 | tf_op jit(solution)/shard_map/ppermute | solution.py:19
  (90 other events, 439.7 us)
where the time goes:
time: 450 us; the launch traced here: 446 us
  other arithmetic  156 us (35%)
  local copies, waits for them, and re-layouts  133 us (30%)
  matrix products  117 us (26%)
  starting transfers between devices  22.5 us (5%)
  blocking collectives  12.6 us (3%)
    scatter-add x4, other arithmetic, site_energy(): nearby = jnp.take(coord_table, neighbours, axis=1)  133 us
    gather x8, local copies, waits for them, and re-layouts, site_energy(): nearby = jnp.take(coord_table, neighbours, axis=1)  69.5 us
    dot_general x12, matrix products, site_energy(): jnp.einsum('xan,ane->axe', radial, second, precision=lax.Precision.HIGHEST)  60.5 us
    ppermute x8, starting transfers between devices, passed_along(): lax.ppermute(value, axis, [(source, source + steps) for source in range(f...  22.5 us
    dot_general x12, matrix products, site_energy(): jnp.einsum('axe,axf->aef', moment, moment[:, :, :AXIS], precision=lax.Pre...  21.8 us
    dot_general x8, matrix products, site_energy(): jnp.dot(descriptor.astype(jnp.bfloat16), fit_weight, preferred_element_ty...  17.8 us
    reshape x4, local copies, waits for them, and re-layouts, site_energy(): descriptor = jnp.einsum('axe,axf->aef', moment, moment[:, :, :AXIS], prec...  9.73 us
    convert_element_type x4, local copies, waits for them, and re-layouts, site_energy(): descriptor.astype(jnp.bfloat16)  9.56 us
  transfers between devices with their start and end apart: 8, of which 2 were waited for; matrix products, arithmetic and copies ran while one was open for 1% of the time, Pallas kernels for 0%

commit v1 on v0

v1 whole, which is shorter than its diff:
```python
import functools

import jax
import jax.numpy as jnp
import numpy as np
from jax import lax
from jax.experimental import pallas as pl
from jax.experimental.pallas import tpu as pltpu
from jax.sharding import PartitionSpec as P

AXIS = 16
LANES = 128
GROUP = 8

cycle_freq = 0.5
time_step = 1.0
soften = 0.25
force_gain = 64.0

f32 = jnp.float32
bf16 = jnp.bfloat16


def passed_along(value, axis, steps):
    count = lax.axis_size(axis)
    first, last = (max(0, -steps), min(count, count - steps))
    return lax.ppermute(value, axis, [(source, source + steps) for source in range(first, last)])


def mode_maps(beads):
    column = np.arange(beads)[None, :]
    bead_row = np.arange(beads)[:, None]
    phases = 2.0 * np.pi * bead_row * column / beads
    mode_basis = np.where(
        column == 0,
        1.0 / np.sqrt(beads),
        np.where(
            2 * column < beads,
            np.sqrt(2.0 / beads) * np.cos(phases),
            np.where(
                2 * column == beads,
                np.cos(phases) / np.sqrt(beads),
                np.sqrt(2.0 / beads) * np.sin(phases),
            ),
        ),
    )
    frequency = 2.0 * cycle_freq * np.sin(np.pi * np.arange(beads) / beads)
    angles = frequency * time_step
    safe_freq = np.where(frequency > 0, frequency, 1.0)
    cosine = np.cos(angles)
    drift = np.where(frequency > 0, np.sin(angles) / safe_freq, time_step)
    pull = -frequency * np.sin(angles)
    keep_map = mode_basis * cosine[None, :] @ mode_basis.T
    drift_map = mode_basis * drift[None, :] @ mode_basis.T
    pull_map = mode_basis * pull[None, :] @ mode_basis.T
    return keep_map, drift_map, pull_map


def propagation_table(groups, bead_dev):
    keep, drift, pull = mode_maps(groups * bead_dev)
    table = np.zeros((groups, groups, 2, bead_dev, 3, 2, 3, bead_dev))
    for source in range(groups):
        cols = slice(source * bead_dev, (source + 1) * bead_dev)
        for target in range(groups):
            rows = slice(target * bead_dev, (target + 1) * bead_dev)
            for c in range(3):
                table[source, target, 0, :, c, 0, c, :] = keep[rows, cols]
                table[source, target, 0, :, c, 1, c, :] = drift[rows, cols]
                table[source, target, 1, :, c, 0, c, :] = pull[rows, cols]
                table[source, target, 1, :, c, 1, c, :] = keep[rows, cols]
    if groups == 2:
        table[1] = table[1, ::-1].copy()
    return table.reshape(groups, groups * 6 * bead_dev, 6 * bead_dev).astype(np.float32)


def lane_take(values, picked):
    numbers = lax.GatherDimensionNumbers(
        offset_dims=(),
        collapsed_slice_dims=(1,),
        start_index_map=(1,),
        operand_batching_dims=(0,),
        start_indices_batching_dims=(0,),
    )
    return lax.gather(
        values,
        picked[..., None],
        numbers,
        (1, 1),
        mode=lax.GatherScatterMode.PROMISE_IN_BOUNDS,
    )


def dot(a, b):
    return jnp.dot(a, b, preferred_element_type=f32)


def dot_nt(a, b):
    return lax.dot_general(a, b, (((1,), (1,)), ((), ())), preferred_element_type=f32)


def packet_kernel(pos, send, own, *outs_and_scratch):
    outs, table = outs_and_scratch[:-1], outs_and_scratch[-1]
    beads, comps, atoms = pos.shape
    table[...] = jnp.zeros_like(table)
    for b in range(beads):
        for c in range(comps):
            row = c * beads + b
            table[row : row + 1, 0:atoms] = pos[b, c : c + 1, :]
    own[...] = table[0 : beads * comps, 0:atoms]
    for j, out in enumerate(outs):
        picked = send[0, j : j + 1, :]
        for first in range(0, beads * comps, 8):
            rows = min(8, beads * comps - first)
            wide = jnp.concatenate([picked, jnp.full((1, LANES - atoms), -1, jnp.int32)], axis=1)
            wide = jnp.broadcast_to(wide, (8, LANES))
            got = lane_take(table[first : first + 8, :], jnp.maximum(wide, 0))
            got = jnp.where(wide >= 0, got, 0.0)
            out[first : first + rows, :] = got[0:rows, 0:atoms]


def column_of(row, rows):
    wide = jnp.broadcast_to(row, (LANES, rows))
    return jnp.transpose(wide)


def wide_columns(column, width):
    return jnp.concatenate([column] * (width // LANES), axis=1)


def force_kernel(
    own, g0, g1, g2, g3, idx, cnt, first, w_embed_t, e_bias,
    fit_w, fit_wt, f_bias, fit_w2, fit_w2t, f_bias2, f_out,
    own_f, o0, o1, o2, o3,
    table, counts, columns, fit_columns, radial, inverse, offset, second, slope,
    moment, moment_t, desc, d_desc, d_moment_t, d_moment, pair_grad, totals, index,
):
    beads = 4
    comps = 3
    atoms = own.shape[1]
    blocks, width = idx.shape
    listed = width // GROUP
    emb = w_embed_t.shape[0]
    fit = f_bias.shape[1]
    fit_pad = fit_w.shape[1]
    sources = (own, g0, g1, g2, g3)

    table[...] = jnp.zeros_like(table)
    for j, source in enumerate(sources):
        for c in range(comps):
            table[j, c, 0:beads, 0:atoms] = source[c * beads : (c + 1) * beads, :]
    counts[...] = jnp.zeros_like(counts)
    counts[:, 0:atoms] = jnp.broadcast_to(cnt[...], (8, atoms))
    columns[0] = column_of(first[0:1, :], emb)
    columns[1] = column_of(first[1:2, :], emb)
    columns[2] = column_of(e_bias[...], emb)
    pad = jnp.zeros((1, fit_pad - fit), f32)
    for at, vector in enumerate((f_bias, f_bias2, f_out)):
        fit_columns[at] = column_of(jnp.concatenate([vector[...], pad], axis=1), fit_pad)
    pair_grad[...] = jnp.zeros_like(pair_grad)
    totals[...] = jnp.zeros_like(totals)
    for i in range(blocks):
        index[i] = jnp.broadcast_to(idx[i : i + 1, :], (8, width))

    lane = lax.broadcasted_iota(jnp.int32, (8, LANES), 1)

    def pairs(i, carry):
        for part in range(width // LANES):
            cols = slice(part * LANES, (part + 1) * LANES)
            ix = index[i, :, cols]
            atom = GROUP * i + part * (LANES // listed) + lane // listed
            entry = lane % listed
            domain = (ix >= atoms).astype(jnp.int32)
            for j in range(2, len(sources)):
                domain += (ix >= j * atoms).astype(jnp.int32)
            local = ix - atoms * domain
            active = entry < lane_take(counts[...], atom)
            offs = []
            for c in range(comps):
                near = lane_take(table[0, c], local)
                for j in range(1, len(sources)):
                    near = jnp.where(domain == j, lane_take(table[j, c], local), near)
                offs.append(near - lane_take(table[0, c], atom))
            square = offs[0] * offs[0] + offs[1] * offs[1] + offs[2] * offs[2]
            inv = lax.rsqrt(square + soften)
            smooth = jnp.where(active, inv, 0.0)
            scaled = smooth * inv
            inverse[i, :, cols] = inv
            radial[0, i, :, cols] = smooth
            for c in range(comps):
                offset[c, i, :, cols] = offs[c]
                radial[c + 1, i, :, cols] = scaled * offs[c]
        return carry

    lax.fori_loop(0, blocks, pairs, 0)

    segment = (
        lax.broadcasted_iota(jnp.int32, (GROUP, width), 1) // listed
        == lax.broadcasted_iota(jnp.int32, (GROUP, width), 0)
    )

    def embed(i, carry):
        for b in range(beads):
            w_first = wide_columns(columns[0], width)
            smooth = radial[0, i, b : b + 1, :]
            one = jnp.tanh(smooth * w_first + wide_columns(columns[1], width))
            one_slope = (1.0 - one * one) * w_first
            low = jnp.concatenate([one.astype(bf16), one_slope.astype(bf16)], axis=1)
            product = dot(w_embed_t[...], low)
            two = jnp.tanh(product[:, 0:width] + wide_columns(columns[2], width))
            total = (one + two).astype(bf16)
            second[b * blocks + i] = total
            slope[b * blocks + i] = (one_slope + (1.0 - two * two) * product[:, width:]).astype(bf16)
            spread = jnp.concatenate(
                [jnp.where(segment, radial[x, i, b : b + 1, :], 0.0) for x in range(4)], axis=0
            )
            part = dot_nt(spread.astype(bf16), total) * (1.0 / listed)
            start = pl.multiple_of(b * atoms + GROUP * i, GROUP)
            for x in range(4):
                moment[x, pl.ds(start, GROUP), :] = part[x * GROUP : (x + 1) * GROUP, :]
        return carry

    lax.fori_loop(0, blocks, embed, 0)

    for x in range(4):
        moment_t[x] = jnp.transpose(moment[x])
    for f in range(AXIS):
        value = moment_t[0] * moment_t[0, f : f + 1, :]
        for x in range(1, 4):
            value += moment_t[x] * moment_t[x, f : f + 1, :]
        desc[f * emb : (f + 1) * emb, :] = value.astype(bf16)
    many = beads * atoms
    bias, bias2, out_col = (wide_columns(fit_columns[at], many) for at in range(3))
    hidden = jnp.tanh(dot(fit_wt[...], desc[...]) + bias)
    more = jnp.tanh(dot(fit_w2t[...], hidden.astype(bf16)) + bias2)
    d_more = out_col * (1.0 - more * more)
    d_hidden = out_col + dot(fit_w2[...], d_more.astype(bf16))
    d_pre = (d_hidden * (1.0 - hidden * hidden)).astype(bf16)
    d_desc[...] = dot(fit_w[...], d_pre)

    def left(e, carry):
        rows = pl.ds(pl.multiple_of(e * 8, 8), 8)
        sums = [None] * 4
        for f in range(AXIS):
            grad = d_desc[pl.ds(pl.multiple_of(f * emb + e * 8, 8), 8), :]
            for x in range(4):
                term = grad * moment_t[x, f : f + 1, :]
                sums[x] = term if f == 0 else sums[x] + term
        for x in range(4):
            d_moment_t[x, rows, :] = sums[x]
        return carry

    lax.fori_loop(0, emb // 8, left, 0)
    for f in range(AXIS):
        for x in range(4):
            terms = jnp.sum(d_desc[f * emb : (f + 1) * emb, :] * moment_t[x], axis=0, keepdims=True)
            d_moment_t[x, f : f + 1, :] += terms
    for x in range(4):
        d_moment[x] = jnp.transpose(d_moment_t[x]) * (1.0 / listed)

    row_of = lax.broadcasted_iota(jnp.int32, (atoms, width), 0)
    lane_of = lax.broadcasted_iota(jnp.int32, (atoms, width), 1)

    def backward(i, carry):
        for b in range(beads):
            start = pl.multiple_of(b * atoms + GROUP * i, GROUP)
            left_side = jnp.concatenate(
                [d_moment[x, pl.ds(start, GROUP), :] for x in range(4)], axis=0
            ).astype(bf16)
            by_second = dot(left_side, second[b * blocks + i])
            by_slope = dot(left_side, slope[b * blocks + i])
            along = None
            for x in range(4):
                rows = slice(x * GROUP, (x + 1) * GROUP)
                pair_grad[x, b : b + 1, :] = jnp.sum(
                    jnp.where(segment, by_second[rows, :], 0.0), axis=0, keepdims=True
                )
                term = by_slope[rows, :] * radial[x, i, b : b + 1, :]
                along = term if along is None else along + term
            pair_grad[4, b : b + 1, :] = jnp.sum(
                jnp.where(segment, along, 0.0), axis=0, keepdims=True
            )
        inv = inverse[i]
        smooth = radial[0, i]
        offs = [offset[c, i] for c in range(comps)]
        along = pair_grad[1] * offs[0] + pair_grad[2] * offs[1] + pair_grad[3] * offs[2]
        live = jnp.where(smooth > 0.0, 1.0, 0.0)
        d_inv = live * (pair_grad[0] + pair_grad[4]) + 2.0 * smooth * along
        pull = d_inv * inv * inv * inv
        scaled = smooth * inv
        grads = [pair_grad[c + 1] * scaled - pull * offs[c] for c in range(comps)]
        high = [g.astype(bf16) for g in grads]
        low = [(g - h.astype(f32)) for g, h in zip(grads, high)]
        sides = jnp.concatenate(
            [h.astype(f32) for h in high] + low, axis=0
        ).astype(bf16)
        ix = index[i, 0:1, :]
        for j in range(len(sources)):
            hot = jnp.where(row_of == ix - j * atoms, 1.0, 0.0)
            if j == 0:
                hot = hot - jnp.where(row_of == GROUP * i + lane_of // listed, 1.0, 0.0)
            totals[j * LANES : j * LANES + atoms, 0 : 6 * 8] += dot_nt(hot.astype(bf16), sides)
        return carry

    lax.fori_loop(0, blocks, backward, 0)

    for j, out in enumerate((own_f, o0, o1, o2, o3)):
        turned = jnp.transpose(totals[j * LANES : (j + 1) * LANES, :])
        whole = turned[0:24, :] + turned[24:48, :]
        for c in range(comps):
            out[c * beads : (c + 1) * beads, :] = -whole[c * 8 : c * 8 + beads, 0:atoms]


def finish_kernel(pos, mom, own_f, r0, r1, r2, r3, send, maps, out, stacked):
    beads, comps, atoms = pos.shape
    rows = beads * comps
    force = own_f[...]
    row_of = lax.broadcasted_iota(jnp.int32, (atoms, send.shape[2]), 0)
    for j, back in enumerate((r0, r1, r2, r3)):
        hot = jnp.where(row_of == send[0, j : j + 1, :], 1.0, 0.0).astype(bf16)
        value = back[...]
        high = value.astype(bf16)
        rest = value - high.astype(f32)
        low = rest.astype(bf16)
        force += dot_nt(high, hot) + dot_nt(low, hot)
    stacked[rows:, :] = force * (time_step * force_gain)
    for b in range(beads):
        for c in range(comps):
            at = c * beads + b
            stacked[at : at + 1, :] = pos[b, c : c + 1, :]
            stacked[rows + at : rows + at + 1, :] += mom[b, c : c + 1, :]
    out[...] = jnp.dot(
        maps[lax.axis_index("bead")],
        stacked[...],
        precision=lax.Precision.HIGHEST,
        preferred_element_type=f32,
    )


def on_device(
    positions, momenta, neighbours, nbr_count, send_rows, embed_first, embed_weight,
    embed_bias, fit_weight, fit_bias, fit_weight2, fit_bias2, fit_out,
):
    bead_dev, comps, atoms = positions.shape
    listed = neighbours.shape[1]
    fit = fit_weight.shape[1]
    emb = embed_weight.shape[0]
    fit_pad = -(-fit // LANES) * LANES
    rows = bead_dev * comps
    blocks = atoms // GROUP
    width = GROUP * listed
    many = bead_dev * atoms
    piece = jax.ShapeDtypeStruct((rows, atoms), f32)
    strides = (-2, -1, 1, 2)

    own, *packets = pl.pallas_call(
        packet_kernel,
        out_shape=[piece] * 5,
        scratch_shapes=[pltpu.VMEM((16, LANES), f32)],
        name="packets",
    )(positions, send_rows)
    ghosts = [passed_along(packet, "space", stride) for packet, stride in zip(packets, strides)]

    by_axis = fit_weight.reshape(emb, AXIS, fit).transpose(1, 0, 2).reshape(emb * AXIS, fit)
    fit_w = jnp.pad(by_axis, ((0, 0), (0, fit_pad - fit)))
    fit_wt = fit_w.T
    fit_w2 = jnp.pad(fit_weight2, ((0, fit_pad - fit), (0, fit_pad - fit)))
    own_f, *ghost_f = pl.pallas_call(
        force_kernel,
        out_shape=[piece] * 5,
        scratch_shapes=[
            pltpu.VMEM((5, comps, 8, LANES), f32),
            pltpu.VMEM((8, LANES), jnp.int32),
            pltpu.VMEM((3, emb, LANES), f32),
            pltpu.VMEM((3, fit_pad, LANES), f32),
            pltpu.VMEM((4, blocks, 8, width), f32),
            pltpu.VMEM((blocks, 8, width), f32),
            pltpu.VMEM((comps, blocks, 8, width), f32),
            pltpu.VMEM((bead_dev * blocks, emb, width), bf16),
            pltpu.VMEM((bead_dev * blocks, emb, width), bf16),
            pltpu.VMEM((4, many, emb), f32),
            pltpu.VMEM((4, emb, many), f32),
            pltpu.VMEM((emb * AXIS, many), bf16),
            pltpu.VMEM((emb * AXIS, many), f32),
            pltpu.VMEM((4, emb, many), f32),
            pltpu.VMEM((4, many, emb), f32),
            pltpu.VMEM((5, 8, width), f32),
            pltpu.VMEM((5 * LANES, LANES), f32),
            pltpu.VMEM((blocks, 8, width), jnp.int32),
        ],
        compiler_params=pltpu.CompilerParams(vmem_limit_bytes=50 * 1024 * 1024),
        name="forces",
    )(
        own, *ghosts, neighbours.reshape(blocks, width), nbr_count.reshape(1, atoms),
        embed_first, embed_weight.T, embed_bias.reshape(1, emb),
        fit_w, fit_wt, fit_bias.reshape(1, fit), fit_w2, fit_w2.T,
        fit_bias2.reshape(1, fit), fit_out.reshape(1, fit),
    )
    returned = [passed_along(part, "space", -stride) for part, stride in zip(ghost_f, strides)]

    groups = lax.axis_size("bead")
    maps = jnp.asarray(propagation_table(groups, bead_dev))
    shares = pl.pallas_call(
        finish_kernel,
        out_shape=jax.ShapeDtypeStruct((groups * 2 * rows, atoms), f32),
        scratch_shapes=[pltpu.VMEM((2 * rows, atoms), f32)],
        name="propagate",
    )(positions, momenta, own_f, *returned, send_rows, maps)
    if groups == 2:
        other = lax.ppermute(shares[2 * rows :], "bead", [(0, 1), (1, 0)])
        result = shares[: 2 * rows] + other
    else:
        parts = lax.all_to_all(
            shares.reshape(groups, 2 * rows, atoms), "bead", split_axis=0, concat_axis=0, tiled=True
        )
        result = parts.sum(axis=0)
    return (result[:rows].reshape(positions.shape), result[rows:].reshape(positions.shape))


def solution(mesh):
    in_specs = (
        P("bead", None, "space"),
        P("bead", None, "space"),
        P("space", None),
        P("space"),
        P("space", None, None),
    ) + (P(),) * 8
    out_specs = (P("bead", None, "space"), P("bead", None, "space"))
    return jax.shard_map(
        on_device, mesh=mesh, in_specs=in_specs, out_specs=out_specs, check_vma=False
    )
```

time: 450 us -> 73.8 us (0.16)
  other arithmetic: 156 us -> 0.01 us
  local copies, waits for them, and re-layouts: 133 us -> 13.1 us
  matrix products: 117 us -> 0 us
  Pallas kernels: 0 us -> 29.3 us
  blocking collectives: 12.6 us -> 0 us
    scatter-add x5 -> x0, other arithmetic: 136 us -> none  [the longest x4 133 us: site_energy(): nearby = jnp.take(coord_table, neighbours, axis=1)]
    dot_general x48 -> x0, matrix products: 117 us -> none  [the longest x12 60.5 us: site_energy(): jnp.einsum('xan,ane->axe', radial, second, precision=lax.Precision.HIGHEST)]
    gather x10 -> x0, local copies, waits for them, and re-layouts: 70.7 us -> none  [the longest x8 69.5 us: site_energy(): nearby = jnp.take(coord_table, neighbours, axis=1)]
    pallas_call x0 -> x3, Pallas kernels: none -> 29.3 us  [the longest x1 26 us: on_device(): pl.pallas_call(force_kernel, out_shape=[piece] * 5, scratch_shapes=[pltpu...]
    convert_element_type x8 -> x0, local copies, waits for them, and re-layouts: 17.6 us -> none  [the longest x4 9.56 us: site_energy(): descriptor.astype(jnp.bfloat16)]
    reduce_sum x16 -> x0, other arithmetic: 14.1 us -> none  [the longest x4 8.32 us: site_energy(): embed_one = jnp.tanh(smooth[:, :, None] * embed_first[0] + embed_first[1])]
    all_to_all x2 -> x0, blocking collectives: 12.6 us -> none  [the longest x1 6.38 us: on_device(): lax.all_to_all(stacked, 'bead', split_axis=2, concat_axis=1, tiled=True)]
    reshape x8 -> x3, local copies, waits for them, and re-layouts: 10.7 us -> 0.1 us  [the longest x1 0.08 us: on_device(): neighbours.reshape(blocks, width)]
  transfers between devices with their start and end apart: 8 -> 9, of which waited for: 2 -> 2; matrix products, arithmetic and copies ran while one was open for 1% -> 8% of each run, Pallas kernels for 0% -> 0%
where the time goes in v1:
time: 73.8 us; the launch traced here: 73.1 us
  Pallas kernels  29.3 us (40%)
  starting transfers between devices  24.5 us (33%)
  local copies, waits for them, and re-layouts  13.1 us (18%)
  waiting for transfers between devices  5.2 us (7%)
  between operations  0.96 us (1%)
    pallas_call x1, Pallas kernels, on_device(): pl.pallas_call(force_kernel, out_shape=[piece] * 5, scratch_shapes=[pltpu...  26 us
    ppermute x8, starting transfers between devices, passed_along(): lax.ppermute(value, axis, [(source, source + steps) for source in range(f...  23 us
    unnamed x47, local copies, waits for them, and re-layouts  10.5 us
    ppermute x8, waiting for transfers between devices, passed_along(): lax.ppermute(value, axis, [(source, source + steps) for source in range(f...  2.98 us
    ppermute x1, waiting for transfers between devices, on_device(): other = lax.ppermute(shares[2 * rows:], 'bead', [(0, 1), (1, 0)])  2.21 us
    pallas_call x1, Pallas kernels, on_device(): pl.pallas_call(finish_kernel, out_shape=jax.ShapeDtypeStruct((groups * 2...  1.95 us
    ppermute x1, starting transfers between devices, on_device(): other = lax.ppermute(shares[2 * rows:], 'bead', [(0, 1), (1, 0)])  1.48 us
  transfers between devices with their start and end apart: 9, of which 2 were waited for; matrix products, arithmetic and copies ran while one was open for 8% of the time, Pallas kernels for 0%

profile of v1, /device:TPU:8, one launch (start us, length us, event | category | flops | bytes accessed | tf_op | source)
XLA Modules:
  0.0 73.1 jit_solution(16310166344809142049)
XLA Ops:
  0.6 1.3 %copy.35.pos = f32[4,3,96]{2,1,0:T(4,128)} copy(f32[4,3,96]{2,0,1:T(4,128)} %param.14) | data formatting | bytes 9216 | tf_op args[0]
  1.9 1.4 %packets.1 = (f32[12,96]{1,0:T(8,128)}, f32[12,96]{1,0:T(8,128)}, f32[12,96]{1,0:T(8,128)}, f32[12,96]{1,0:T(8,128)}, f32[12,96]{1,0:T(8,128)}) custom-call(f32[4,3,96]{2,1,0:T(4,128)} %copy.35.pos, s32[1,4,96]{2,1,0:T(4,128)} %send.3), custom_call_target="tpu_custom_call" | custom-call | tf_op jit(solution)/shard_map/packets/pallas_call | solution.py:355
  3.3 3.3 %collective-permute-start = (f32[12,96]{1,0:T(8,128)}, f32[12,96]{1,0:T(8,128)S(1)}, u32[]{:S(2)}, u32[]{:S(2)}) collective-permute-start(f32[12,96]{1,0:T(8,128)} %get-tuple-element.13), channel_id=1, source_target_pairs={{4,0},{6,2},{8,4},{10,6},{12,8},{14,10},{16,12},{18,14},{20,16},{2... | collective-permute-start | bytes 13832 | tf_op jit(solution)/shard_map/ppermute | solution.py:27
  6.6 1.9 %collective-permute-start.1 = (f32[12,96]{1,0:T(8,128)}, f32[12,96]{1,0:T(8,128)S(1)}, u32[]{:S(2)}, u32[]{:S(2)}) collective-permute-start(f32[12,96]{1,0:T(8,128)} %get-tuple-element.14), channel_id=1, source_target_pairs={{2,0},{4,2},{6,4},{8,6},{10,8},{12,10},{14,12},{16,14},{18,16},{20... | collective-permute-start | bytes 13832 | tf_op jit(solution)/shard_map/ppermute | solution.py:27
  8.5 2.4 %collective-permute-start.2 = (f32[12,96]{1,0:T(8,128)}, f32[12,96]{1,0:T(8,128)S(1)}, u32[]{:S(2)}, u32[]{:S(2)}) collective-permute-start(f32[12,96]{1,0:T(8,128)} %get-tuple-element.15), channel_id=1, source_target_pairs={{0,2},{2,4},{4,6},{6,8},{8,10},{10,12},{12,14},{14,16},{16,18},{18... | collective-permute-start | bytes 13832 | tf_op jit(solution)/shard_map/ppermute | solution.py:27
  11.0 2.6 %collective-permute-start.3 = (f32[12,96]{1,0:T(8,128)}, f32[12,96]{1,0:T(8,128)S(1)}, u32[]{:S(2)}, u32[]{:S(2)}) collective-permute-start(f32[12,96]{1,0:T(8,128)} %get-tuple-element.16), channel_id=1, source_target_pairs={{0,4},{2,6},{4,8},{6,10},{8,12},{10,14},{12,16},{14,18},{16,20},{1... | collective-permute-start | bytes 13832 | tf_op jit(solution)/shard_map/ppermute | solution.py:27
  13.6 1.5 %copy.30 = bf16[2048,240]{1,0:T(8,128)(2,1)S(1)} copy(bf16[2048,240]{0,1:T(8,128)(2,1)} %param.22) | data formatting | bytes 1966080 | tf_op args[8]
  15.0 1.4 %copy.31 = bf16[16,128,240]{1,0,2:T(8,128)(2,1)S(1)} copy(bf16[16,128,240]{2,0,1:T(8,128)(2,1)S(1)} %bitcast.27) | data formatting | bytes 1966080 | tf_op jit(solution)/shard_map/transpose | solution.py:363
  16.8 0.8 %copy-done.9 = bf16[240,240]{1,0:T(8,128)(2,1)S(1)} copy-done((bf16[240,240]{1,0:T(8,128)(2,1)S(1)}, bf16[240,240]{1,0:T(8,128)(2,1)}, u32[]{:S(2)}) %copy-start.9) | copy-done | bytes 115224
  18.3 0.8 %copy.42 = bf16[240,240]{1,0:T(8,128)(2,1)} copy(bf16[240,240]{0,1:T(8,128)(2,1)S(1)} %copy.32) | data formatting | bytes 230400
  19.2 0.7 copy-done.8
  20.0 0.7 %copy-done.11 = s32[96,64]{0,1:T(8,128)S(1)} copy-done((s32[96,64]{0,1:T(8,128)S(1)}, s32[96,64]{0,1:T(8,128)}, u32[]{:S(2)}) %copy-start.11) | copy-done | bytes 24600
  20.9 0.6 copy-done.12
  22.4 26.0 %forces.1 = (f32[12,96]{1,0:T(8,128)S(1)}, f32[12,96]{1,0:T(8,128)S(1)}, f32[12,96]{1,0:T(8,128)S(1)}, f32[12,96]{1,0:T(8,128)S(1)}, f32[12,96]{1,0:T(8,128)S(1)}) custom-call(f32[12,96]{1,0:T(8,128)S(1)} %copy-done, f32[12,96]{1,0:T(8,128)S(1)} %collective-permute-done.g0, f32[12,96]{1,0:T(8,128)S(1)} %collective-permute-done.1.g1, ...), custom_call_target="tpu_custom_call" | custom-call | tf_op jit(solution)/shard_map/forces/pallas_call | solution.py:367
  48.4 4.4 %collective-permute-start.4 = (f32[12,96]{1,0:T(8,128)S(1)}, f32[12,96]{1,0:T(8,128)S(1)}, u32[]{:S(2)}, u32[]{:S(2)}) collective-permute-start(f32[12,96]{1,0:T(8,128)S(1)} %get-tuple-element.18), channel_id=1, source_target_pairs={{0,4},{2,6},{4,8},{6,10},{8,12},{10,14},{12,16},{14,18},{16,20},{1... | collective-permute-start | bytes 13832 | tf_op jit(solution)/shard_map/ppermute | solution.py:27
  52.8 2.1 %collective-permute-start.5 = (f32[12,96]{1,0:T(8,128)S(1)}, f32[12,96]{1,0:T(8,128)S(1)}, u32[]{:S(2)}, u32[]{:S(2)}) collective-permute-start(f32[12,96]{1,0:T(8,128)S(1)} %get-tuple-element.19), channel_id=1, source_target_pairs={{0,2},{2,4},{4,6},{6,8},{8,10},{10,12},{12,14},{14,16},{16,18},{18... | collective-permute-start | bytes 13832 | tf_op jit(solution)/shard_map/ppermute | solution.py:27
  54.9 4.3 %collective-permute-start.6 = (f32[12,96]{1,0:T(8,128)S(1)}, f32[12,96]{1,0:T(8,128)S(1)}, u32[]{:S(2)}, u32[]{:S(2)}) collective-permute-start(f32[12,96]{1,0:T(8,128)S(1)} %get-tuple-element.20), channel_id=1, source_target_pairs={{2,0},{4,2},{6,4},{8,6},{10,8},{12,10},{14,12},{16,14},{18,16},{20... | collective-permute-start | bytes 13832 | tf_op jit(solution)/shard_map/ppermute | solution.py:27
  59.3 1.9 %collective-permute-start.7 = (f32[12,96]{1,0:T(8,128)S(1)}, f32[12,96]{1,0:T(8,128)S(1)}, u32[]{:S(2)}, u32[]{:S(2)}) collective-permute-start(f32[12,96]{1,0:T(8,128)S(1)} %get-tuple-element.21), channel_id=1, source_target_pairs={{4,0},{6,2},{8,4},{10,6},{12,8},{14,10},{16,12},{18,14},{20,16},{2... | collective-permute-start | bytes 13832 | tf_op jit(solution)/shard_map/ppermute | solution.py:27
  61.8 3.0 %collective-permute-done.7.r3 = f32[12,96]{1,0:T(8,128)S(1)} collective-permute-done((f32[12,96]{1,0:T(8,128)S(1)}, f32[12,96]{1,0:T(8,128)S(1)}, u32[]{:S(2)}, u32[]{:S(2)}) %collective-permute-start.7) | collective-permute-done | bytes 4640 | tf_op jit(solution)/shard_map/ppermute | solution.py:27
  65.4 2.0 %propagate.1 = f32[48,96]{1,0:T(8,128)} custom-call(f32[4,3,96]{2,1,0:T(4,128)} %copy.35.pos, f32[4,3,96]{2,1,0:T(4,128)} %copy.36.mom, f32[12,96]{1,0:T(8,128)} %copy-done.1, f32[12,96]{1,0:T(8,128)} %copy-done.13, f32[12,96]{1,0:T(8,128)} %copy-done.14, f32[12,96]{1,0:T(8,128)} %copy-done.15, f32[12,96]{1,0:T(8,128)} %copy-done.16, s32[1,4,96]{2,1,0:T(4,128)} %send.3, ...), custom_call_target="tpu_custom_call" | custom-call | tf_op jit(solution)/shard_map/propagate/pallas_call | solution.py:402
  67.3 0.8 %slice.17 = f32[24,96]{1,0:T(8,128)S(1)} slice(f32[48,96]{1,0:T(8,128)} %propagate.1), slice={[24:48], [0:96]} | slice | bytes 18432 | tf_op jit(solution)/shard_map/slice | solution.py:409
  68.1 1.5 %collective-permute-start.8 = (f32[24,96]{1,0:T(8,128)S(1)}, f32[24,96]{1,0:T(8,128)S(1)}, u32[]{:S(2)}, u32[]{:S(2)}) collective-permute-start(f32[24,96]{1,0:T(8,128)S(1)} %slice.17), channel_id=1, source_target_pairs={{0,1},{1,0},{2,3},{3,2},{4,5},{5,4},{6,7},{7,6},{8,9},{9,8},{10,11... | collective-permute-start | bytes 27656 | tf_op jit(solution)/shard_map/ppermute | solution.py:409
  69.6 2.2 %collective-permute-done.8 = f32[24,96]{1,0:T(8,128)S(1)} collective-permute-done((f32[24,96]{1,0:T(8,128)S(1)}, f32[24,96]{1,0:T(8,128)S(1)}, u32[]{:S(2)}, u32[]{:S(2)}) %collective-permute-start.8) | collective-permute-done | bytes 9248 | tf_op jit(solution)/shard_map/ppermute | solution.py:409
  72.5 0.6 copy.38
  (55 shorter events, 4.0 us)
Async XLA Ops:
  3.3 18.4 %collective-permute-start = (f32[12,96]{1,0:T(8,128)}, f32[12,96]{1,0:T(8,128)S(1)}, u32[]{:S(2)}, u32[]{:S(2)}) collective-permute-start(f32[12,96]{1,0:T(8,128)} %get-tuple-element.13), channel_id=1, source_target_pairs={{4,0},{6,2},{8,4},{10,6},{12,8},{14,10},{16,12},{18,14},{20,16},{2... | collective-permute-start | bytes 13832 | tf_op jit(solution)/shard_map/ppermute | solution.py:27
  6.6 15.1 %collective-permute-start.1 = (f32[12,96]{1,0:T(8,128)}, f32[12,96]{1,0:T(8,128)S(1)}, u32[]{:S(2)}, u32[]{:S(2)}) collective-permute-start(f32[12,96]{1,0:T(8,128)} %get-tuple-element.14), channel_id=1, source_target_pairs={{2,0},{4,2},{6,4},{8,6},{10,8},{12,10},{14,12},{16,14},{18,16},{20... | collective-permute-start | bytes 13832 | tf_op jit(solution)/shard_map/ppermute | solution.py:27
  8.5 13.1 %collective-permute-start.2 = (f32[12,96]{1,0:T(8,128)}, f32[12,96]{1,0:T(8,128)S(1)}, u32[]{:S(2)}, u32[]{:S(2)}) collective-permute-start(f32[12,96]{1,0:T(8,128)} %get-tuple-element.15), channel_id=1, source_target_pairs={{0,2},{2,4},{4,6},{6,8},{8,10},{10,12},{12,14},{14,16},{16,18},{18... | collective-permute-start | bytes 13832 | tf_op jit(solution)/shard_map/ppermute | solution.py:27
  11.0 10.7 %collective-permute-start.3 = (f32[12,96]{1,0:T(8,128)}, f32[12,96]{1,0:T(8,128)S(1)}, u32[]{:S(2)}, u32[]{:S(2)}) collective-permute-start(f32[12,96]{1,0:T(8,128)} %get-tuple-element.16), channel_id=1, source_target_pairs={{0,4},{2,6},{4,8},{6,10},{8,12},{10,14},{12,16},{14,18},{16,20},{1... | collective-permute-start | bytes 13832 | tf_op jit(solution)/shard_map/ppermute | solution.py:27
  16.7 0.9 %copy-start.9 = (bf16[240,240]{1,0:T(8,128)(2,1)S(1)}, bf16[240,240]{1,0:T(8,128)(2,1)}, u32[]{:S(2)}) copy-start(bf16[240,240]{1,0:T(8,128)(2,1)} %param.24) | copy-start | bytes 345604
  19.0 0.9 %copy-start.8 = (bf16[240,240]{1,0:T(8,128)(2,1)S(1)}, bf16[240,240]{1,0:T(8,128)(2,1)}, u32[]{:S(2)}) copy-start(bf16[240,240]{1,0:T(8,128)(2,1)} %copy.42) | copy-start | bytes 345604
  19.9 0.8 %copy-start.11 = (s32[96,64]{0,1:T(8,128)S(1)}, s32[96,64]{0,1:T(8,128)}, u32[]{:S(2)}) copy-start(s32[96,64]{0,1:T(8,128)} %param.16) | copy-start | bytes 73732
  20.8 0.8 %copy-start.12 = (bf16[128,128]{1,0:T(8,128)(2,1)S(1)}, bf16[128,128]{1,0:T(8,128)(2,1)}, u32[]{:S(2)}) copy-start(bf16[128,128]{1,0:T(8,128)(2,1)} %param.20) | copy-start | bytes 98308
  20.8 0.9 %copy-start.3 = (f32[240]{0:T(256)S(1)}, f32[240]{0:T(256)}, u32[]{:S(2)}) copy-start(f32[240]{0:T(256)} %param.23) | copy-start | bytes 2884
  20.8 0.9 %copy-start.4 = (f32[240]{0:T(256)S(1)}, f32[240]{0:T(256)}, u32[]{:S(2)}) copy-start(f32[240]{0:T(256)} %param.25) | copy-start | bytes 2884
  20.8 0.9 %copy-start.5 = (f32[240]{0:T(256)S(1)}, f32[240]{0:T(256)}, u32[]{:S(2)}) copy-start(f32[240]{0:T(256)} %param.26) | copy-start | bytes 2884
  20.8 0.9 %copy-start.7 = (f32[128]{0:T(128)S(1)}, f32[128]{0:T(128)}, u32[]{:S(2)}) copy-start(f32[128]{0:T(128)} %param.21) | copy-start | bytes 1540
  21.7 0.7 copy-start
  48.4 13.4 %copy-start.1 = (f32[12,96]{1,0:T(8,128)}, f32[12,96]{1,0:T(8,128)S(1)}, u32[]{:S(2)}) copy-start(f32[12,96]{1,0:T(8,128)S(1)} %get-tuple-element.17.own_f) | copy-start | bytes 13828
  48.4 12.8 %copy-start.17 = (f32[4,3,96]{2,0,1:T(4,128)S(1)}, f32[4,3,96]{2,0,1:T(4,128)}, u32[]{:S(2)}) copy-start(f32[4,3,96]{2,0,1:T(4,128)} %param.15) | copy-start | bytes 13828
  48.4 13.4 %collective-permute-start.4 = (f32[12,96]{1,0:T(8,128)S(1)}, f32[12,96]{1,0:T(8,128)S(1)}, u32[]{:S(2)}, u32[]{:S(2)}) collective-permute-start(f32[12,96]{1,0:T(8,128)S(1)} %get-tuple-element.18), channel_id=1, source_target_pairs={{0,4},{2,6},{4,8},{6,10},{8,12},{10,14},{12,16},{14,18},{16,20},{1... | collective-permute-start | bytes 13832 | tf_op jit(solution)/shard_map/ppermute | solution.py:27
  52.8 9.0 %collective-permute-start.5 = (f32[12,96]{1,0:T(8,128)S(1)}, f32[12,96]{1,0:T(8,128)S(1)}, u32[]{:S(2)}, u32[]{:S(2)}) collective-permute-start(f32[12,96]{1,0:T(8,128)S(1)} %get-tuple-element.19), channel_id=1, source_target_pairs={{0,2},{2,4},{4,6},{6,8},{8,10},{10,12},{12,14},{14,16},{16,18},{18... | collective-permute-start | bytes 13832 | tf_op jit(solution)/shard_map/ppermute | solution.py:27
  54.9 6.9 %collective-permute-start.6 = (f32[12,96]{1,0:T(8,128)S(1)}, f32[12,96]{1,0:T(8,128)S(1)}, u32[]{:S(2)}, u32[]{:S(2)}) collective-permute-start(f32[12,96]{1,0:T(8,128)S(1)} %get-tuple-element.20), channel_id=1, source_target_pairs={{2,0},{4,2},{6,4},{8,6},{10,8},{12,10},{14,12},{16,14},{18,16},{20... | collective-permute-start | bytes 13832 | tf_op jit(solution)/shard_map/ppermute | solution.py:27
  59.3 5.5 %collective-permute-start.7 = (f32[12,96]{1,0:T(8,128)S(1)}, f32[12,96]{1,0:T(8,128)S(1)}, u32[]{:S(2)}, u32[]{:S(2)}) collective-permute-start(f32[12,96]{1,0:T(8,128)S(1)} %get-tuple-element.21), channel_id=1, source_target_pairs={{4,0},{6,2},{8,4},{10,6},{12,8},{14,10},{16,12},{18,14},{20,16},{2... | collective-permute-start | bytes 13832 | tf_op jit(solution)/shard_map/ppermute | solution.py:27
  61.8 3.0 %copy-start.13 = (f32[12,96]{1,0:T(8,128)}, f32[12,96]{1,0:T(8,128)S(1)}, u32[]{:S(2)}) copy-start(f32[12,96]{1,0:T(8,128)S(1)} %collective-permute-done.4.r0) | copy-start | bytes 13828
  61.8 3.0 %copy-start.14 = (f32[12,96]{1,0:T(8,128)}, f32[12,96]{1,0:T(8,128)S(1)}, u32[]{:S(2)}) copy-start(f32[12,96]{1,0:T(8,128)S(1)} %collective-permute-done.5.r1) | copy-start | bytes 13828
  61.8 3.0 %copy-start.15 = (f32[12,96]{1,0:T(8,128)}, f32[12,96]{1,0:T(8,128)S(1)}, u32[]{:S(2)}) copy-start(f32[12,96]{1,0:T(8,128)S(1)} %collective-permute-done.6.r2) | copy-start | bytes 13828
  67.3 4.5 %copy-start.10 = (f32[48,96]{1,0:T(8,128)S(1)}, f32[48,96]{1,0:T(8,128)}, u32[]{:S(2)}) copy-start(f32[48,96]{1,0:T(8,128)} %propagate.1) | copy-start | bytes 55300
  68.1 3.7 %collective-permute-start.8 = (f32[24,96]{1,0:T(8,128)S(1)}, f32[24,96]{1,0:T(8,128)S(1)}, u32[]{:S(2)}, u32[]{:S(2)}) collective-permute-start(f32[24,96]{1,0:T(8,128)S(1)} %slice.17), channel_id=1, source_target_pairs={{0,1},{1,0},{2,3},{3,2},{4,5},{5,4},{6,7},{7,6},{8,9},{9,8},{10,11... | collective-permute-start | bytes 27656 | tf_op jit(solution)/shard_map/ppermute | solution.py:409
  (3 other events, 1.9 us)

commit v2 on v1

v2 whole, which is shorter than its diff:
```python
import functools

import jax
import jax.numpy as jnp
import numpy as np
from jax import lax
from jax.experimental import pallas as pl
from jax.experimental.pallas import tpu as pltpu
from jax.sharding import PartitionSpec as P

AXIS = 16
LANES = 128
GROUP = 8

cycle_freq = 0.5
time_step = 1.0
soften = 0.25
force_gain = 64.0

f32 = jnp.float32
bf16 = jnp.bfloat16


def passed_along(value, axis, steps):
    count = lax.axis_size(axis)
    first, last = (max(0, -steps), min(count, count - steps))
    return lax.ppermute(value, axis, [(source, source + steps) for source in range(first, last)])


def mode_maps(beads):
    column = np.arange(beads)[None, :]
    bead_row = np.arange(beads)[:, None]
    phases = 2.0 * np.pi * bead_row * column / beads
    mode_basis = np.where(
        column == 0,
        1.0 / np.sqrt(beads),
        np.where(
            2 * column < beads,
            np.sqrt(2.0 / beads) * np.cos(phases),
            np.where(
                2 * column == beads,
                np.cos(phases) / np.sqrt(beads),
                np.sqrt(2.0 / beads) * np.sin(phases),
            ),
        ),
    )
    frequency = 2.0 * cycle_freq * np.sin(np.pi * np.arange(beads) / beads)
    angles = frequency * time_step
    safe_freq = np.where(frequency > 0, frequency, 1.0)
    cosine = np.cos(angles)
    drift = np.where(frequency > 0, np.sin(angles) / safe_freq, time_step)
    pull = -frequency * np.sin(angles)
    keep_map = mode_basis * cosine[None, :] @ mode_basis.T
    drift_map = mode_basis * drift[None, :] @ mode_basis.T
    pull_map = mode_basis * pull[None, :] @ mode_basis.T
    return keep_map, drift_map, pull_map


def propagation_table(groups, bead_dev):
    keep, drift, pull = mode_maps(groups * bead_dev)
    table = np.zeros((groups, groups, 2, bead_dev, 3, 2, 3, bead_dev))
    for source in range(groups):
        cols = slice(source * bead_dev, (source + 1) * bead_dev)
        for target in range(groups):
            rows = slice(target * bead_dev, (target + 1) * bead_dev)
            for c in range(3):
                table[source, target, 0, :, c, 0, c, :] = keep[rows, cols]
                table[source, target, 0, :, c, 1, c, :] = drift[rows, cols]
                table[source, target, 1, :, c, 0, c, :] = pull[rows, cols]
                table[source, target, 1, :, c, 1, c, :] = keep[rows, cols]
    if groups == 2:
        table[1] = table[1, ::-1].copy()
    table = table.reshape(groups, groups * 6 * bead_dev, 6 * bead_dev)
    return np.pad(table, ((0, 0), (0, 0), (0, LANES - table.shape[2]))).astype(np.float32)


def lane_take(values, picked):
    numbers = lax.GatherDimensionNumbers(
        offset_dims=(),
        collapsed_slice_dims=(1,),
        start_index_map=(1,),
        operand_batching_dims=(0,),
        start_indices_batching_dims=(0,),
    )
    return lax.gather(
        values,
        picked[..., None],
        numbers,
        (1, 1),
        mode=lax.GatherScatterMode.PROMISE_IN_BOUNDS,
    )


def dot(a, b):
    return jnp.dot(a, b, preferred_element_type=f32)


def dot_nt(a, b):
    return lax.dot_general(a, b, (((1,), (1,)), ((), ())), preferred_element_type=f32)


def column_of(row, rows):
    wide = jnp.broadcast_to(row, (LANES, rows))
    return jnp.transpose(wide)


def wide_columns(column, width):
    return jnp.concatenate([column] * (width // LANES), axis=1)


def split_dot(a, b):
    high = b.astype(bf16)
    return dot(a, high) + dot(a, (b - high.astype(f32)).astype(bf16))


def prepare_kernel(first, w_embed, e_bias, fit_w, f_bias, fit_w2, f_bias2, f_out,
                   w_embed_t, fit_rows, fit_cols, fit_w2_pad, fit_w2t, columns, fit_columns):
    emb = w_embed.shape[0]
    fit = fit_w.shape[1]
    fit_pad = fit_rows.shape[1]

    def unit(n):
        same = lax.broadcasted_iota(jnp.int32, (n, n), 0) == lax.broadcasted_iota(jnp.int32, (n, n), 1)
        return jnp.where(same, 1.0, 0.0).astype(bf16)

    w_embed_t[...] = dot_nt(unit(emb), w_embed[...]).astype(bf16)
    fit_w2_pad[...] = jnp.zeros_like(fit_w2_pad)
    fit_w2_pad[0:fit, 0:fit] = fit_w2[...]
    fit_w2t[...] = dot_nt(unit(fit_pad), fit_w2_pad[...]).astype(bf16)
    row = lax.broadcasted_iota(jnp.int32, (LANES, LANES), 0)
    source = AXIS * (row % 8) + row // 8
    order = jnp.where(lax.broadcasted_iota(jnp.int32, (LANES, LANES), 1) == source, 1.0, 0.0).astype(bf16)
    fit_rows[:, LANES:] = jnp.zeros((fit_rows.shape[0], fit_pad - LANES), bf16)
    for chunk in range(fit_w.shape[0] // LANES):
        part = slice(chunk * LANES, (chunk + 1) * LANES)
        fit_rows[part, 0:fit] = dot(order, fit_w[part, :]).astype(bf16)
        fit_cols[:, part] = dot_nt(unit(fit_pad), fit_rows[part, :]).astype(bf16)
    columns[0] = column_of(first[0:1, :], emb)
    columns[1] = column_of(first[1:2, :], emb)
    columns[2] = column_of(e_bias[...], emb)
    for at, vector in enumerate((f_bias, f_bias2, f_out)):
        pad = jnp.zeros((1, fit_pad - fit), f32)
        fit_columns[at] = column_of(jnp.concatenate([vector[...], pad], axis=1), fit_pad)


def force_kernel(
    own, core, link, far, idx, cnt, w_embed_t, fit_w, fit_wt, columns, fit_columns, fit_w2, fit_w2t,
    own_f, near_f, link_f,
    table, counts, sent, radial, inverse, offset, second, slope,
    moment, moment_t, desc, d_desc, d_moment_t, d_moment, pair_grad, totals, index,
    rows_here, cols_here, loaded,
):
    beads = 4
    comps = 3
    atoms = own.shape[1]
    blocks, width = idx.shape
    listed = width // GROUP
    emb = w_embed_t.shape[0]
    fit = fit_w2.shape[0]
    rows = beads * comps
    loads = [
        pltpu.make_async_copy(fit_wt, cols_here, loaded.at[0]),
        pltpu.make_async_copy(fit_w, rows_here, loaded.at[1]),
    ]
    for load in loads:
        load.start()

    odd = lax.rem(lax.axis_index("space"), 2) == 1
    block_of = ((2, 1), (1, 2), (0, 3), (3, 0))
    table[...] = jnp.zeros_like(table)
    sent[...] = jnp.zeros_like(sent)
    sources = ((own, 0), (core, 0), (link, 0), (link, own.shape[0]), (far, 0))
    for role, (source, at) in enumerate(sources):
        for c in range(comps):
            table[role, c, 0:beads, 0:atoms] = source[at + c * beads : at + (c + 1) * beads, :]
        if role > 0:
            if_odd, if_even = (
                source[at + rows + j : at + rows + j + 1, :] for j in block_of[role - 1]
            )
            row = jnp.maximum(jnp.where(odd, if_odd, if_even), 0.0).astype(jnp.int32)
            sent[role - 1, :, 0:atoms] = jnp.broadcast_to(row, (8, atoms))
    role_of = [
        jnp.where(odd, 1 + [pair[0] for pair in block_of].index(j), 1 + [pair[1] for pair in block_of].index(j))
        for j in range(4)
    ]
    counts[...] = jnp.zeros_like(counts)
    counts[:, 0:atoms] = jnp.broadcast_to(cnt[...], (8, atoms))
    pair_grad[...] = jnp.zeros_like(pair_grad)
    totals[...] = jnp.zeros_like(totals)
    for i in range(blocks):
        index[i] = jnp.broadcast_to(idx[i : i + 1, :], (8, width))

    lane = lax.broadcasted_iota(jnp.int32, (8, LANES), 1)

    def pairs(i, carry):
        for part in range(width // LANES):
            cols = slice(part * LANES, (part + 1) * LANES)
            ix = index[i, :, cols]
            atom = GROUP * i + part * (LANES // listed) + lane // listed
            entry = lane % listed
            role = jnp.where(ix >= atoms, role_of[0], 0)
            block = jnp.where(ix >= atoms, 1, 0)
            for j in range(1, 4):
                role = jnp.where(ix >= (j + 1) * atoms, role_of[j], role)
                block = jnp.where(ix >= (j + 1) * atoms, j + 1, block)
            slot = ix - atoms * block
            local = slot
            for r in range(1, 5):
                local = jnp.where(role == r, lane_take(sent[r - 1], slot), local)
            index[i, :, cols] = local + role * LANES
            active = entry < lane_take(counts[...], atom)
            offs = []
            for c in range(comps):
                near = lane_take(table[0, c], local)
                for j in range(1, len(sources)):
                    near = jnp.where(role == j, lane_take(table[j, c], local), near)
                offs.append(near - lane_take(table[0, c], atom))
            square = offs[0] * offs[0] + offs[1] * offs[1] + offs[2] * offs[2]
            inv = lax.rsqrt(square + soften)
            smooth = jnp.where(active, inv, 0.0)
            scaled = smooth * inv
            inverse[i, :, cols] = inv
            radial[0, i, :, cols] = smooth
            for c in range(comps):
                offset[c, i, :, cols] = offs[c]
                radial[c + 1, i, :, cols] = scaled * offs[c]
        return carry

    lax.fori_loop(0, blocks, pairs, 0)

    segment = (
        lax.broadcasted_iota(jnp.int32, (GROUP, width), 1) // listed
        == lax.broadcasted_iota(jnp.int32, (GROUP, width), 0)
    )

    def embed(i, carry):
        for b in range(beads):
            w_first = wide_columns(columns[0], width)
            smooth = radial[0, i, b : b + 1, :]
            one = jnp.tanh(smooth * w_first + wide_columns(columns[1], width))
            one_slope = (1.0 - one * one) * w_first
            low = jnp.concatenate([one.astype(bf16), one_slope.astype(bf16)], axis=1)
            product = dot(w_embed_t[...], low)
            two = jnp.tanh(product[:, 0:width] + wide_columns(columns[2], width))
            both = one + two
            total = both.astype(bf16)
            second[b * blocks + i] = total
            slope[b * blocks + i] = (one_slope + (1.0 - two * two) * product[:, width:]).astype(bf16)
            spread = jnp.concatenate(
                [jnp.where(segment, radial[x, i, b : b + 1, :], 0.0) for x in range(4)], axis=0
            )
            high = spread.astype(bf16)
            halves = jnp.concatenate([high, (spread - high.astype(f32)).astype(bf16)], axis=0)
            part = dot_nt(halves, total)
            rest = dot_nt(high, (both - total.astype(f32)).astype(bf16))
            part = (part[0 : 4 * GROUP, :] + part[4 * GROUP :, :] + rest) * (1.0 / listed)
            start = pl.multiple_of(b * atoms + GROUP * i, GROUP)
            for x in range(4):
                moment[x, pl.ds(start, GROUP), :] = part[x * GROUP : (x + 1) * GROUP, :]
        return carry

    lax.fori_loop(0, blocks, embed, 0)

    for x in range(4):
        moment_t[x] = jnp.transpose(moment[x])
    def describe(e, carry):
        mine = [moment_t[x, pl.ds(pl.multiple_of(e * 8, 8), 8), :] for x in range(4)]
        for f in range(0, AXIS, 2):
            values = []
            for g in (f, f + 1):
                value = mine[0] * moment_t[0, g : g + 1, :]
                for x in range(1, 4):
                    value += mine[x] * moment_t[x, g : g + 1, :]
                values.append(value)
            at = pl.ds(pl.multiple_of(e * 8 * AXIS + f * 8, 16), 16)
            desc[at, :] = jnp.concatenate(values, axis=0).astype(bf16)
        return carry

    lax.fori_loop(0, emb // 8, describe, 0)
    for load in loads:
        load.wait()
    many = beads * atoms
    bias, bias2, out_col = (wide_columns(fit_columns[at, 0:fit, :], many) for at in range(3))
    hidden = jnp.tanh(dot(cols_here[...], desc[...]) + bias)
    more = jnp.tanh(dot(fit_w2t[...], hidden.astype(bf16)) + bias2)
    d_more = out_col * (1.0 - more * more)
    d_hidden = out_col + split_dot(fit_w2[...], d_more).astype(bf16).astype(f32)
    d_pre = d_hidden * (1.0 - hidden * hidden)
    d_desc[...] = split_dot(rows_here[...], d_pre).astype(bf16).astype(f32)

    def left(e, carry):
        rows = pl.ds(pl.multiple_of(e * 8, 8), 8)
        sums = [None] * 4
        for f in range(AXIS):
            grad = d_desc[pl.ds(pl.multiple_of((e * AXIS + f) * 8, 8), 8), :]
            for x in range(4):
                term = grad * moment_t[x, f : f + 1, :]
                sums[x] = term if f == 0 else sums[x] + term
        for x in range(4):
            d_moment_t[x, rows, :] = sums[x]
        return carry

    lax.fori_loop(0, emb // 8, left, 0)
    for f in range(AXIS):
        terms = [None] * 4
        for e in range(emb // 8):
            grad = d_desc[(e * AXIS + f) * 8 : (e * AXIS + f + 1) * 8, :]
            for x in range(4):
                term = grad * moment_t[x, e * 8 : (e + 1) * 8, :]
                terms[x] = term if e == 0 else terms[x] + term
        for x in range(4):
            d_moment_t[x, f : f + 1, :] += jnp.sum(terms[x], axis=0, keepdims=True)
    for x in range(4):
        d_moment[x] = jnp.transpose(d_moment_t[x]) * (1.0 / listed)

    row_of = lax.broadcasted_iota(jnp.int32, (atoms, width), 0)
    lane_of = lax.broadcasted_iota(jnp.int32, (atoms, width), 1)

    def backward(i, carry):
        for b in range(beads):
            start = pl.multiple_of(b * atoms + GROUP * i, GROUP)
            left_side = jnp.concatenate(
                [d_moment[x, pl.ds(start, GROUP), :] for x in range(4)], axis=0
            )
            high = left_side.astype(bf16)
            halves = jnp.concatenate([high, (left_side - high.astype(f32)).astype(bf16)], axis=0)
            by_second = dot(halves, second[b * blocks + i])
            by_second = by_second[0 : 4 * GROUP, :] + by_second[4 * GROUP :, :]
            by_slope = dot(halves, slope[b * blocks + i])
            by_slope = by_slope[0 : 4 * GROUP, :] + by_slope[4 * GROUP :, :]
            along = None
            for x in range(4):
                rows = slice(x * GROUP, (x + 1) * GROUP)
                pair_grad[x, b : b + 1, :] = jnp.sum(
                    jnp.where(segment, by_second[rows, :], 0.0), axis=0, keepdims=True
                )
                term = by_slope[rows, :] * radial[x, i, b : b + 1, :]
                along = term if along is None else along + term
            pair_grad[4, b : b + 1, :] = jnp.sum(
                jnp.where(segment, along, 0.0), axis=0, keepdims=True
            )
        inv = inverse[i]
        smooth = radial[0, i]
        offs = [offset[c, i] for c in range(comps)]
        along = pair_grad[1] * offs[0] + pair_grad[2] * offs[1] + pair_grad[3] * offs[2]
        live = jnp.where(smooth > 0.0, 1.0, 0.0)
        d_inv = live * (pair_grad[0] + pair_grad[4]) + 2.0 * smooth * along
        pull = d_inv * inv * inv * inv
        scaled = smooth * inv
        grads = [pair_grad[c + 1] * scaled - pull * offs[c] for c in range(comps)]
        high = [g.astype(bf16) for g in grads]
        low = [(g - h.astype(f32)) for g, h in zip(grads, high)]
        sides = jnp.concatenate(
            [h.astype(f32) for h in high] + low, axis=0
        ).astype(bf16)
        ix = index[i, 0:1, :]
        for j in range(len(sources)):
            hot = jnp.where(row_of == ix - j * LANES, 1.0, 0.0)
            if j == 0:
                hot = hot - jnp.where(row_of == GROUP * i + lane_of // listed, 1.0, 0.0)
            totals[j * LANES : j * LANES + atoms, 0 : 6 * 8] += dot_nt(hot.astype(bf16), sides)
        return carry

    lax.fori_loop(0, blocks, backward, 0)

    targets = ((own_f, 0), (near_f, 0), (link_f, 0), (link_f, rows), (near_f, rows))
    for j, (out, at) in enumerate(targets):
        turned = jnp.transpose(totals[j * LANES : (j + 1) * LANES, :])
        whole = turned[0:24, :] + turned[24:48, :]
        for c in range(comps):
            out[at + c * beads : at + (c + 1) * beads, :] = -whole[c * 8 : c * 8 + beads, 0:atoms]


def finish_kernel(pos, mom, own_f, near, link, far, maps, *outs_and_scratch):
    outs, stacked = outs_and_scratch[:-1], outs_and_scratch[-1]
    beads, comps, atoms = pos.shape
    rows = beads * comps
    force = (own_f[...] + near[0:rows, :]) + (link[0:rows, :] + far[rows : 2 * rows, :])
    stacked[...] = jnp.zeros_like(stacked)
    stacked[rows : 2 * rows, 0:atoms] = force * (time_step * force_gain)
    for b in range(beads):
        for c in range(comps):
            at = c * beads + b
            stacked[at : at + 1, 0:atoms] = pos[b, c : c + 1, :]
            stacked[rows + at : rows + at + 1, 0:atoms] += mom[b, c : c + 1, :]
    shares = jnp.dot(
        maps[lax.axis_index("bead")],
        stacked[...],
        precision=lax.Precision.HIGHEST,
        preferred_element_type=f32,
    )
    for at, out in enumerate(outs):
        out[...] = shares[at * 2 * rows : (at + 1) * 2 * rows, 0:atoms]


def on_device(
    positions, momenta, neighbours, nbr_count, send_rows, embed_first, embed_weight,
    embed_bias, fit_weight, fit_bias, fit_weight2, fit_bias2, fit_out,
):
    bead_dev, comps, atoms = positions.shape
    listed = neighbours.shape[1]
    wide, fit = fit_weight.shape
    emb = embed_weight.shape[0]
    fit_pad = -(-fit // LANES) * LANES
    rows = bead_dev * comps
    blocks = atoms // GROUP
    width = GROUP * listed
    many = bead_dev * atoms
    shape = jax.ShapeDtypeStruct
    big = pltpu.CompilerParams(vmem_limit_bytes=50 * 1024 * 1024)

    domains = lax.axis_size("space")
    pairs = [(d, d + 1) for d in range(0, domains - 1, 2)]
    links = [(d, d + 1) for d in range(1, domains - 1, 2)]

    def swapped(value, which):
        return lax.ppermute(value, "space", which + [(b, a) for a, b in which])

    own = jnp.concatenate(
        [positions.transpose(1, 0, 2).reshape(rows, atoms), send_rows[0].astype(f32)], axis=0
    )
    core = swapped(own, pairs)
    link = swapped(jnp.concatenate([own, core], axis=0), links)
    far = swapped(link, pairs)

    w_embed_t, fit_rows, fit_cols, fit_w2, fit_w2t, columns, fit_columns = pl.pallas_call(
        prepare_kernel,
        out_shape=[
            shape((emb, emb), bf16),
            shape((wide, fit_pad), bf16),
            shape((fit_pad, wide), bf16),
            shape((fit_pad, fit_pad), bf16),
            shape((fit_pad, fit_pad), bf16),
            shape((3, emb, LANES), f32),
            shape((3, fit_pad, LANES), f32),
        ],
        compiler_params=big,
        cost_estimate=pl.CostEstimate(
            flops=2 * wide * fit_pad * (LANES + fit_pad), bytes_accessed=8 * wide * fit_pad, transcendentals=0
        ),
        name="weights",
    )(
        embed_first, embed_weight, embed_bias.reshape(1, emb), fit_weight,
        fit_bias.reshape(1, fit), fit_weight2, fit_bias2.reshape(1, fit), fit_out.reshape(1, fit),
    )
    vmem = pl.BlockSpec(memory_space=pltpu.VMEM)
    anywhere = pl.BlockSpec(memory_space=pl.ANY)
    own_f, near_f, link_f = pl.pallas_call(
        force_kernel,
        out_shape=[shape((rows, atoms), f32), shape((2 * rows, atoms), f32), shape((2 * rows, atoms), f32)],
        in_specs=[vmem] * 7 + [anywhere] * 2 + [vmem] * 4,
        scratch_shapes=[
            pltpu.VMEM((5, comps, 8, LANES), f32),
            pltpu.VMEM((8, LANES), jnp.int32),
            pltpu.VMEM((4, 8, LANES), jnp.int32),
            pltpu.VMEM((4, blocks, 8, width), f32),
            pltpu.VMEM((blocks, 8, width), f32),
            pltpu.VMEM((comps, blocks, 8, width), f32),
            pltpu.VMEM((bead_dev * blocks, emb, width), bf16),
            pltpu.VMEM((bead_dev * blocks, emb, width), bf16),
            pltpu.VMEM((4, many, emb), f32),
            pltpu.VMEM((4, emb, many), f32),
            pltpu.VMEM((wide, many), bf16),
            pltpu.VMEM((wide, many), f32),
            pltpu.VMEM((4, emb, many), f32),
            pltpu.VMEM((4, many, emb), f32),
            pltpu.VMEM((5, 8, width), f32),
            pltpu.VMEM((5 * LANES, LANES), f32),
            pltpu.VMEM((blocks, 8, width), jnp.int32),
            pltpu.VMEM((wide, fit_pad), bf16),
            pltpu.VMEM((fit_pad, wide), bf16),
            pltpu.SemaphoreType.DMA((2,)),
        ],
        compiler_params=big,
        name="forces",
    )(
        own, core, link, far, neighbours.reshape(blocks, width), nbr_count.reshape(1, atoms),
        w_embed_t, fit_rows, fit_cols, columns, fit_columns, fit_w2, fit_w2t,
    )
    near = swapped(near_f, pairs)
    link = swapped(
        jnp.concatenate([link_f[:rows] + near[rows:], link_f[rows:]], axis=0), links
    )
    far = swapped(link, pairs)

    groups = lax.axis_size("bead")
    maps = jnp.asarray(propagation_table(groups, bead_dev))
    shares = pl.pallas_call(
        finish_kernel,
        out_shape=[shape((2 * rows, atoms), f32)] * groups,
        scratch_shapes=[pltpu.VMEM((LANES, LANES), f32)],
        name="propagate",
    )(positions, momenta, own_f, near, link, far, maps)
    if groups == 2:
        result = shares[0] + lax.ppermute(shares[1], "bead", [(0, 1), (1, 0)])
    else:
        parts = lax.all_to_all(jnp.stack(shares), "bead", split_axis=0, concat_axis=0, tiled=True)
        result = parts.sum(axis=0)
    return (result[:rows].reshape(positions.shape), result[rows:].reshape(positions.shape))


def solution(mesh):
    in_specs = (
        P("bead", None, "space"),
        P("bead", None, "space"),
        P("space", None),
        P("space"),
        P("space", None, None),
    ) + (P(),) * 8
    out_specs = (P("bead", None, "space"), P("bead", None, "space"))
    return jax.shard_map(
        on_device, mesh=mesh, in_specs=in_specs, out_specs=out_specs, check_vma=False
    )
```

time: 73.8 us -> 60.6 us (0.82)
  starting transfers between devices: 24.5 us -> 8.42 us
  local copies, waits for them, and re-layouts: 13.1 us -> 8.08 us
  Pallas kernels: 29.3 us -> 33.9 us
  waiting for transfers between devices: 5.2 us -> 7.8 us
    ppermute x9 -> x7, starting transfers between devices: 24.5 us -> 8.42 us  [the longest x6 6.94 us: swapped(): return lax.ppermute(value, 'space', which + [(b, a) for a, b in which])]
    pallas_call x3, Pallas kernels: 29.3 us -> 33.9 us  [the longest x1 28.6 us: on_device(): pl.pallas_call(force_kernel, out_shape=[shape((rows, atoms), f32), shape(...]
    unnamed x47 -> x38, local copies, waits for them, and re-layouts: 10.5 us -> 7.28 us
    ppermute x9 -> x7, waiting for transfers between devices: 5.2 us -> 7.8 us  [the longest x6 5.39 us: swapped(): return lax.ppermute(value, 'space', which + [(b, a) for a, b in which])]
    transpose x3 -> x0, local copies, waits for them, and re-layouts: 1.53 us -> none  [the longest x1 1.4 us: on_device(): fit_weight.reshape(emb, AXIS, fit).transpose(1, 0, 2)]
    slice x1 -> x0, local copies, waits for them, and re-layouts: 0.78 us -> none  [on_device(): other = lax.ppermute(shares[2 * rows:], 'bead', [(0, 1), (1, 0)])]
  transfers between devices with their start and end apart: 9 -> 7, of which waited for: 2 -> 5; matrix products, arithmetic and copies ran while one was open for 8% -> 6% of each run, Pallas kernels for 0% -> 6%
where the time goes in v2:
time: 60.6 us; the launch traced here: 59.8 us
  Pallas kernels  33.9 us (56%)
  starting transfers between devices  8.42 us (14%)
  local copies, waits for them, and re-layouts  8.08 us (13%)
  waiting for transfers between devices  7.8 us (13%)
  between operations  0.81 us (1%)
  other arithmetic  0.74 us (1%)
    pallas_call x1, Pallas kernels, on_device(): pl.pallas_call(force_kernel, out_shape=[shape((rows, atoms), f32), shape(...  28.6 us
    unnamed x38, local copies, waits for them, and re-layouts  7.28 us
    ppermute x6, starting transfers between devices, swapped(): return lax.ppermute(value, 'space', which + [(b, a) for a, b in which])  6.94 us
    ppermute x6, waiting for transfers between devices, swapped(): return lax.ppermute(value, 'space', which + [(b, a) for a, b in which])  5.39 us
    pallas_call x1, Pallas kernels, on_device(): pl.pallas_call(prepare_kernel, out_shape=[shape((emb, emb), bf16), shape(...  3.64 us
    ppermute x1, waiting for transfers between devices, on_device(): result = shares[0] + lax.ppermute(shares[1], 'bead', [(0, 1), (1, 0)])  2.42 us
    pallas_call x1, Pallas kernels, on_device(): pl.pallas_call(finish_kernel, out_shape=[shape((2 * rows, atoms), f32)] *...  1.69 us
    ppermute x1, starting transfers between devices, on_device(): result = shares[0] + lax.ppermute(shares[1], 'bead', [(0, 1), (1, 0)])  1.49 us
  transfers between devices with their start and end apart: 7, of which 5 were waited for; matrix products, arithmetic and copies ran while one was open for 6% of the time, Pallas kernels for 6%

profile of v2, /device:TPU:8, one launch (start us, length us, event | category | flops | bytes accessed | tf_op | source)
XLA Modules:
  0.0 59.8 jit_solution(3389806630553437715)
XLA Ops:
  0.6 0.7 %reshape.32 = f32[12,96]{1,0:T(8,128)S(1)} reshape(f32[3,4,96]{2,1,0:T(4,128)} %bitcast.13) | data formatting | bytes 9216 | tf_op jit(solution)/shard_map/reshape | solution.py:420
  1.4 1.2 %collective-permute-done.core = f32[16,96]{1,0:T(8,128)S(1)} collective-permute-done((f32[16,96]{1,0:T(8,128)S(1)}, f32[16,96]{1,0:T(8,128)S(1)}, u32[]{:S(2)}, u32[]{:S(2)}) %collective-permute-start) | collective-permute-done | bytes 6176 | tf_op jit(solution)/shard_map/ppermute | solution.py:417
  2.6 3.2 %collective-permute-start.1 = (f32[32,96]{1,0:T(8,128)S(1)}, f32[32,96]{1,0:T(8,128)S(1)}, u32[]{:S(2)}, u32[]{:S(2)}) collective-permute-start(f32[32,96]{1,0:T(8,128)S(1)} %pad_maximum_fusion), channel_id=1, source_target_pairs={{2,4},{6,8},{10,12},{14,16},{18,20},{22,24},{26,28},{4,2},{8,6},{1... | collective-permute-start | bytes 36872 | tf_op jit(solution)/shard_map/ppermute | solution.py:417
  5.9 2.3 %copy.23.fit_w = bf16[2048,240]{1,0:T(8,128)(2,1)} copy(bf16[2048,240]{0,1:T(8,128)(2,1)} %param.22) | data formatting | bytes 1966080 | tf_op args[8]
  8.2 0.6 collective-permute-done.1.link
  8.8 0.6 %copy-done.4 = f32[2,128]{1,0:T(2,128)S(1)} copy-done((f32[2,128]{1,0:T(2,128)S(1)}, f32[2,128]{1,0:T(2,128)}, u32[]{:S(2)}) %copy-start.4) | copy-done | bytes 1048
  9.4 3.6 %weights.1 = (bf16[128,128]{1,0:T(8,128)(2,1)S(1)}, bf16[2048,256]{1,0:T(8,128)(2,1)S(1)}, bf16[256,2048]{1,0:T(8,128)(2,1)S(1)}, bf16[256,256]{1,0:T(8,128)(2,1...) custom-call(f32[2,128]{1,0:T(2,128)S(1)} %copy-done.4, ...), custom_call_target="tpu_custom_call" | custom-call | flops 402653184 | bytes 4194304 | tf_op jit(solution)/shard_map/weights/pallas_call | solution.py:426
  13.1 0.1 copy.22
  13.2 0.7 %copy-done.1 = s32[96]{0:T(128)S(1)} copy-done((s32[96]{0:T(128)S(1)}, s32[96]{0:T(128)}, u32[]{:S(2)}) %copy-start.1) | copy-done | bytes 408
  13.9 28.6 %forces.1 = (f32[12,96]{1,0:T(8,128)S(1)}, f32[24,96]{1,0:T(8,128)S(1)}, f32[24,96]{1,0:T(8,128)S(1)}) custom-call(f32[16,96]{1,0:T(8,128)S(1)} %pad_maximum_fusion.2.own, f32[16,96]{1,0:T(8,128)S(1)} %collective-permute-done.core, f32[32,96]{1,0:T(8,128)S(1)} %collective-permute-done.1.link, f32[32,96]{1,0:T(8,128)S(1)} %collective-permute-done.2.far, ...), custom_call_target="tpu_custom_call" | custom-call | tf_op jit(solution)/shard_map/forces/pallas_call | solution.py:448
  42.5 0.6 collective-permute-start.3
  43.1 0.8 %collective-permute-done.3.near = f32[24,96]{1,0:T(8,128)S(1)} collective-permute-done((f32[24,96]{1,0:T(8,128)S(1)}, f32[24,96]{1,0:T(8,128)S(1)}, u32[]{:S(2)}, u32[]{:S(2)}) %collective-permute-start.3) | collective-permute-done | bytes 9248 | tf_op jit(solution)/shard_map/ppermute | solution.py:417
  43.9 0.6 copy-done.9
  44.5 3.1 %collective-permute-start.4 = (f32[24,96]{1,0:T(8,128)S(1)}, f32[24,96]{1,0:T(8,128)S(1)}, u32[]{:S(2)}, u32[]{:S(2)}) collective-permute-start(f32[24,96]{1,0:T(8,128)S(1)} %pad_maximum_fusion.1), channel_id=1, source_target_pairs={{2,4},{6,8},{10,12},{14,16},{18,20},{22,24},{26,28},{4,2},{8,6},{1... | collective-permute-start | bytes 27656 | tf_op jit(solution)/shard_map/ppermute | solution.py:417
  47.6 2.8 %collective-permute-done.4.link = f32[24,96]{1,0:T(8,128)S(1)} collective-permute-done((f32[24,96]{1,0:T(8,128)S(1)}, f32[24,96]{1,0:T(8,128)S(1)}, u32[]{:S(2)}, u32[]{:S(2)}) %collective-permute-start.4) | collective-permute-done | bytes 9248 | tf_op jit(solution)/shard_map/ppermute | solution.py:417
  50.5 0.6 copy.24.pos
  51.1 0.6 copy.25.mom
  51.7 0.6 copy-done.13
  52.3 1.7 %propagate.1 = (f32[24,96]{1,0:T(8,128)}, f32[24,96]{1,0:T(8,128)}) custom-call(f32[4,3,96]{2,1,0:T(4,128)} %copy.24.pos, f32[4,3,96]{2,1,0:T(4,128)} %copy.25.mom, f32[12,96]{1,0:T(8,128)} %copy-done, f32[24,96]{1,0:T(8,128)} %copy-done.9, f32[24,96]{1,0:T(8,128)} %copy-done.12, f32[24,96]{1,0:T(8,128)} %copy-done.13, f32[2,48,128]{2,1,0:T(8,128)} %constant.2.clone.maps), custom_call_target="tpu_custom_call" | custom-call | tf_op jit(solution)/shard_map/propagate/pallas_call | solution.py:488
  54.0 1.5 %collective-permute-start.6 = (f32[24,96]{1,0:T(8,128)}, f32[24,96]{1,0:T(8,128)S(1)}, u32[]{:S(2)}, u32[]{:S(2)}) collective-permute-start(f32[24,96]{1,0:T(8,128)} %get-tuple-element.25), channel_id=1, source_target_pairs={{0,1},{1,0},{2,3},{3,2},{4,5},{5,4},{6,7},{7,6},{8,9},{9,8},{10,11... | collective-permute-start | bytes 27656 | tf_op jit(solution)/shard_map/ppermute | solution.py:495
  55.4 2.4 %collective-permute-done.6 = f32[24,96]{1,0:T(8,128)S(1)} collective-permute-done((f32[24,96]{1,0:T(8,128)}, f32[24,96]{1,0:T(8,128)S(1)}, u32[]{:S(2)}, u32[]{:S(2)}) %collective-permute-start.6) | collective-permute-done | bytes 9248 | tf_op jit(solution)/shard_map/ppermute | solution.py:495
  57.9 0.7 %add.7 = f32[24,96]{1,0:T(8,128)S(1)} add(f32[24,96]{1,0:T(8,128)} %get-tuple-element.24, f32[24,96]{1,0:T(8,128)S(1)} %collective-permute-done.6) | non-fusion elementwise | flops 2304 | bytes 27648 | tf_op jit(solution)/shard_map/add | solution.py:495
  58.6 0.6 copy.26
  59.2 0.6 copy.27
  (42 shorter events, 0.3 us)
Async XLA Ops:
  0.6 0.7 %copy-start.15 = (s32[1,4,96]{2,1,0:T(4,128)S(1)}, s32[1,4,96]{2,1,0:T(4,128)}, u32[]{:S(2)}) copy-start(s32[1,4,96]{2,1,0:T(4,128)} %param.18) | copy-start | bytes 4612
  1.4 1.2 %collective-permute-start = (f32[16,96]{1,0:T(8,128)S(1)}, f32[16,96]{1,0:T(8,128)S(1)}, u32[]{:S(2)}, u32[]{:S(2)}) collective-permute-start(f32[16,96]{1,0:T(8,128)S(1)} %pad_maximum_fusion.2.own), channel_id=1, source_target_pairs={{0,2},{4,6},{8,10},{12,14},{16,18},{20,22},{24,26},{28,30},{2,0},{... | collective-permute-start | bytes 18440 | tf_op jit(solution)/shard_map/ppermute | solution.py:417
  2.6 6.1 %copy-start.2 = (bf16[240,240]{1,0:T(8,128)(2,1)S(1)}, bf16[240,240]{1,0:T(8,128)(2,1)}, u32[]{:S(2)}) copy-start(bf16[240,240]{1,0:T(8,128)(2,1)} %fit_w2.1) | copy-start | bytes 345604
  2.6 6.1 %copy-start.3 = (bf16[128,128]{1,0:T(8,128)(2,1)S(1)}, bf16[128,128]{1,0:T(8,128)(2,1)}, u32[]{:S(2)}) copy-start(bf16[128,128]{1,0:T(8,128)(2,1)} %w_embed.1) | copy-start | bytes 98308
  2.6 6.1 %collective-permute-start.1 = (f32[32,96]{1,0:T(8,128)S(1)}, f32[32,96]{1,0:T(8,128)S(1)}, u32[]{:S(2)}, u32[]{:S(2)}) collective-permute-start(f32[32,96]{1,0:T(8,128)S(1)} %pad_maximum_fusion), channel_id=1, source_target_pairs={{2,4},{6,8},{10,12},{14,16},{18,20},{22,24},{26,28},{4,2},{8,6},{1... | collective-permute-start | bytes 36872 | tf_op jit(solution)/shard_map/ppermute | solution.py:417
  5.9 2.9 %copy-start.5 = (f32[240]{0:T(256)S(1)}, f32[240]{0:T(256)}, u32[]{:S(2)}) copy-start(f32[240]{0:T(256)} %param.23) | copy-start | bytes 2884
  5.9 2.9 %copy-start.6 = (f32[240]{0:T(256)S(1)}, f32[240]{0:T(256)}, u32[]{:S(2)}) copy-start(f32[240]{0:T(256)} %param.25) | copy-start | bytes 2884
  5.9 2.9 %copy-start.7 = (f32[240]{0:T(256)S(1)}, f32[240]{0:T(256)}, u32[]{:S(2)}) copy-start(f32[240]{0:T(256)} %param.26) | copy-start | bytes 2884
  8.7 4.5 %collective-permute-start.2 = (f32[32,96]{1,0:T(8,128)S(1)}, f32[32,96]{1,0:T(8,128)S(1)}, u32[]{:S(2)}, u32[]{:S(2)}) collective-permute-start(f32[32,96]{1,0:T(8,128)S(1)} %collective-permute-done.1.link), channel_id=1, source_target_pairs={{0,2},{4,6},{8,10},{12,14},{16,18},{20,22},{24,26},{28,30},{2,0},{... | collective-permute-start | bytes 36872 | tf_op jit(solution)/shard_map/ppermute | solution.py:417
  8.7 0.7 %copy-start.4 = (f32[2,128]{1,0:T(2,128)S(1)}, f32[2,128]{1,0:T(2,128)}, u32[]{:S(2)}) copy-start(f32[2,128]{1,0:T(2,128)} %first.1) | copy-start | bytes 3076
  8.7 0.7 %copy-start.8 = (f32[128]{0:T(128)S(1)}, f32[128]{0:T(128)}, u32[]{:S(2)}) copy-start(f32[128]{0:T(128)} %param.21) | copy-start | bytes 1540
  9.4 3.7 %copy-start.10 = (s32[96,64]{0,1:T(8,128)S(1)}, s32[96,64]{0,1:T(8,128)}, u32[]{:S(2)}) copy-start(s32[96,64]{0,1:T(8,128)} %param.16) | copy-start | bytes 73732
  13.2 0.7 %copy-start.1 = (s32[96]{0:T(128)S(1)}, s32[96]{0:T(128)}, u32[]{:S(2)}) copy-start(s32[96]{0:T(128)} %param.17) | copy-start | bytes 1156
  42.5 1.4 %copy-start = (f32[12,96]{1,0:T(8,128)}, f32[12,96]{1,0:T(8,128)S(1)}, u32[]{:S(2)}) copy-start(f32[12,96]{1,0:T(8,128)S(1)} %get-tuple-element.21.own_f) | copy-start | bytes 13828
  42.5 1.4 %collective-permute-start.3 = (f32[24,96]{1,0:T(8,128)S(1)}, f32[24,96]{1,0:T(8,128)S(1)}, u32[]{:S(2)}, u32[]{:S(2)}) collective-permute-start(f32[24,96]{1,0:T(8,128)S(1)} %get-tuple-element.22), channel_id=1, source_target_pairs={{0,2},{4,6},{8,10},{12,14},{16,18},{20,22},{24,26},{28,30},{2,0},{... | collective-permute-start | bytes 27656 | tf_op jit(solution)/shard_map/ppermute | solution.py:417
  43.9 0.6 copy-start.9
  44.5 5.9 %copy-start.11 = (f32[4,3,96]{2,0,1:T(4,128)S(1)}, f32[4,3,96]{2,0,1:T(4,128)}, u32[]{:S(2)}) copy-start(f32[4,3,96]{2,0,1:T(4,128)} %param.14) | copy-start | bytes 13828
  44.5 6.5 %copy-start.14 = (f32[4,3,96]{2,0,1:T(4,128)S(1)}, f32[4,3,96]{2,0,1:T(4,128)}, u32[]{:S(2)}) copy-start(f32[4,3,96]{2,0,1:T(4,128)} %param.15) | copy-start | bytes 13828
  44.5 5.9 %collective-permute-start.4 = (f32[24,96]{1,0:T(8,128)S(1)}, f32[24,96]{1,0:T(8,128)S(1)}, u32[]{:S(2)}, u32[]{:S(2)}) collective-permute-start(f32[24,96]{1,0:T(8,128)S(1)} %pad_maximum_fusion.1), channel_id=1, source_target_pairs={{2,4},{6,8},{10,12},{14,16},{18,20},{22,24},{26,28},{4,2},{8,6},{1... | collective-permute-start | bytes 27656 | tf_op jit(solution)/shard_map/ppermute | solution.py:417
  50.5 1.2 %copy-start.12 = (f32[24,96]{1,0:T(8,128)}, f32[24,96]{1,0:T(8,128)S(1)}, u32[]{:S(2)}) copy-start(f32[24,96]{1,0:T(8,128)S(1)} %collective-permute-done.4.link) | copy-start | bytes 27652
  50.5 1.2 %collective-permute-start.5 = (f32[24,96]{1,0:T(8,128)S(1)}, f32[24,96]{1,0:T(8,128)S(1)}, u32[]{:S(2)}, u32[]{:S(2)}) collective-permute-start(f32[24,96]{1,0:T(8,128)S(1)} %collective-permute-done.4.link), channel_id=1, source_target_pairs={{0,2},{4,6},{8,10},{12,14},{16,18},{20,22},{24,26},{28,30},{2,0},{... | collective-permute-start | bytes 27656 | tf_op jit(solution)/shard_map/ppermute | solution.py:417
  51.7 0.6 copy-start.13
  54.0 3.9 %collective-permute-start.6 = (f32[24,96]{1,0:T(8,128)}, f32[24,96]{1,0:T(8,128)S(1)}, u32[]{:S(2)}, u32[]{:S(2)}) collective-permute-start(f32[24,96]{1,0:T(8,128)} %get-tuple-element.25), channel_id=1, source_target_pairs={{0,1},{1,0},{2,3},{3,2},{4,5},{5,4},{6,7},{7,6},{8,9},{9,8},{10,11... | collective-permute-start | bytes 27656 | tf_op jit(solution)/shard_map/ppermute | solution.py:495

commit v3 on v2

--- a/solution.py
+++ b/solution.py
@@ -58,16 +58,16 @@
 
 def propagation_table(groups, bead_dev):
     keep, drift, pull = mode_maps(groups * bead_dev)
-    table = np.zeros((groups, groups, 2, bead_dev, 3, 2, 3, bead_dev))
+    table = np.zeros((groups, groups, 2, 3, bead_dev, 2, 3, bead_dev))
     for source in range(groups):
         cols = slice(source * bead_dev, (source + 1) * bead_dev)
         for target in range(groups):
             rows = slice(target * bead_dev, (target + 1) * bead_dev)
             for c in range(3):
-                table[source, target, 0, :, c, 0, c, :] = keep[rows, cols]
-                table[source, target, 0, :, c, 1, c, :] = drift[rows, cols]
-                table[source, target, 1, :, c, 0, c, :] = pull[rows, cols]
-                table[source, target, 1, :, c, 1, c, :] = keep[rows, cols]
+                table[source, target, 0, c, :, 0, c, :] = keep[rows, cols]
+                table[source, target, 0, c, :, 1, c, :] = drift[rows, cols]
+                table[source, target, 1, c, :, 0, c, :] = pull[rows, cols]
+                table[source, target, 1, c, :, 1, c, :] = keep[rows, cols]
     if groups == 2:
         table[1] = table[1, ::-1].copy()
     table = table.reshape(groups, groups * 6 * bead_dev, 6 * bead_dev)
@@ -113,63 +113,43 @@
     return dot(a, high) + dot(a, (b - high.astype(f32)).astype(bf16))
 
 
-def prepare_kernel(first, w_embed, e_bias, fit_w, f_bias, fit_w2, f_bias2, f_out,
-                   w_embed_t, fit_rows, fit_cols, fit_w2_pad, fit_w2t, columns, fit_columns):
-    emb = w_embed.shape[0]
-    fit = fit_w.shape[1]
-    fit_pad = fit_rows.shape[1]
-
-    def unit(n):
-        same = lax.broadcasted_iota(jnp.int32, (n, n), 0) == lax.broadcasted_iota(jnp.int32, (n, n), 1)
-        return jnp.where(same, 1.0, 0.0).astype(bf16)
-
-    w_embed_t[...] = dot_nt(unit(emb), w_embed[...]).astype(bf16)
-    fit_w2_pad[...] = jnp.zeros_like(fit_w2_pad)
-    fit_w2_pad[0:fit, 0:fit] = fit_w2[...]
-    fit_w2t[...] = dot_nt(unit(fit_pad), fit_w2_pad[...]).astype(bf16)
-    row = lax.broadcasted_iota(jnp.int32, (LANES, LANES), 0)
-    source = AXIS * (row % 8) + row // 8
-    order = jnp.where(lax.broadcasted_iota(jnp.int32, (LANES, LANES), 1) == source, 1.0, 0.0).astype(bf16)
-    fit_rows[:, LANES:] = jnp.zeros((fit_rows.shape[0], fit_pad - LANES), bf16)
-    for chunk in range(fit_w.shape[0] // LANES):
-        part = slice(chunk * LANES, (chunk + 1) * LANES)
-        fit_rows[part, 0:fit] = dot(order, fit_w[part, :]).astype(bf16)
-        fit_cols[:, part] = dot_nt(unit(fit_pad), fit_rows[part, :]).astype(bf16)
-    columns[0] = column_of(first[0:1, :], emb)
-    columns[1] = column_of(first[1:2, :], emb)
-    columns[2] = column_of(e_bias[...], emb)
-    for at, vector in enumerate((f_bias, f_bias2, f_out)):
-        pad = jnp.zeros((1, fit_pad - fit), f32)
-        fit_columns[at] = column_of(jnp.concatenate([vector[...], pad], axis=1), fit_pad)
+def pack_kernel(pos, mom, send, out, mom_out):
+    comps, beads, _ = pos.shape
+    for c in range(comps):
+        out[c * beads : (c + 1) * beads, :] = pos[c]
+        mom_out[c * beads : (c + 1) * beads, :] = mom[c]
+    out[comps * beads : comps * beads + send.shape[1], :] = send[0].astype(f32)
+
+
+def unit(n):
+    same = lax.broadcasted_iota(jnp.int32, (n, n), 0) == lax.broadcasted_iota(jnp.int32, (n, n), 1)
+    return jnp.where(same, 1.0, 0.0).astype(bf16)
 
 
 def force_kernel(
-    own, core, link, far, idx, cnt, w_embed_t, fit_w, fit_wt, columns, fit_columns, fit_w2, fit_w2t,
+    own, mom, core, link, far, idx, cnt, first, w_embed, e_bias, fit_t, f_bias, fit_w2, f_bias2, f_out,
     own_f, near_f, link_f,
     table, counts, sent, radial, inverse, offset, second, slope,
     moment, moment_t, desc, d_desc, d_moment_t, d_moment, pair_grad, totals, index,
-    rows_here, cols_here, loaded,
+    fit_here, rows_here, cols_here, w_embed_t, w2_here, w2_t, columns, fit_columns, loaded,
 ):
     beads = 4
     comps = 3
     atoms = own.shape[1]
     blocks, width = idx.shape
     listed = width // GROUP
-    emb = w_embed_t.shape[0]
-    fit = fit_w2.shape[0]
+    emb = w_embed.shape[0]
+    fit, wide = fit_t.shape
+    fit_pad = rows_here.shape[1]
     rows = beads * comps
-    loads = [
-        pltpu.make_async_copy(fit_wt, cols_here, loaded.at[0]),
-        pltpu.make_async_copy(fit_w, rows_here, loaded.at[1]),
-    ]
-    for load in loads:
-        load.start()
+    load = pltpu.make_async_copy(fit_t, fit_here, loaded)
+    load.start()
 
     odd = lax.rem(lax.axis_index("space"), 2) == 1
     block_of = ((2, 1), (1, 2), (0, 3), (3, 0))
     table[...] = jnp.zeros_like(table)
     sent[...] = jnp.zeros_like(sent)
-    sources = ((own, 0), (core, 0), (link, 0), (link, own.shape[0]), (far, 0))
+    sources = ((own, 0), (core, 0), (link, 0), (link, link.shape[0] // 2), (far, 0))
     for role, (source, at) in enumerate(sources):
         for c in range(comps):
             table[role, c, 0:beads, 0:atoms] = source[at + c * beads : at + (c + 1) * beads, :]
@@ -190,9 +170,34 @@
     for i in range(blocks):
         index[i] = jnp.broadcast_to(idx[i : i + 1, :], (8, width))
 
+    columns[0] = column_of(first[0:1, :], emb)
+    columns[1] = column_of(first[1:2, :], emb)
+    columns[2] = column_of(e_bias[...], emb)
+    for at, vector in enumerate((f_bias, f_bias2, f_out)):
+        pad = jnp.zeros((1, fit_pad - fit), f32)
+        fit_columns[at] = column_of(jnp.concatenate([vector[...], pad], axis=1), fit_pad)
+    w_embed_t[...] = dot_nt(unit(emb), w_embed[...]).astype(bf16)
+    w2_here[...] = jnp.zeros_like(w2_here)
+    w2_here[0:fit, 0:fit] = fit_w2[...]
+    w2_t[...] = dot_nt(unit(fit_pad), w2_here[...]).astype(bf16)
+    cols_here[fit:fit_pad, :] = jnp.zeros((fit_pad - fit, wide), bf16)
+    row = lax.broadcasted_iota(jnp.int32, (LANES, LANES), 0)
+    source = AXIS * (row % 8) + row // 8
+    order = jnp.where(lax.broadcasted_iota(jnp.int32, (LANES, LANES), 1) == source, 1.0, 0.0).astype(bf16)
+    blank = jnp.zeros((LANES, fit_pad - fit), f32)
+    chunks = wide // LANES
+    each = -(-chunks // blocks)
+    load.wait()
+
     lane = lax.broadcasted_iota(jnp.int32, (8, LANES), 1)
 
     def pairs(i, carry):
+        for turn in range(each):
+            chunk = jnp.minimum(each * i + turn, chunks - 1)
+            part = pl.ds(pl.multiple_of(chunk * LANES, LANES), LANES)
+            chunk_t = fit_here[:, part]
+            rows_here[part, :] = jnp.concatenate([dot_nt(order, chunk_t), blank], axis=1).astype(bf16)
+            cols_here[0:fit, part] = dot_nt(chunk_t, order).astype(bf16)
         for part in range(width // LANES):
             cols = slice(part * LANES, (part + 1) * LANES)
             ix = index[i, :, cols]
@@ -277,14 +282,12 @@
         return carry
 
     lax.fori_loop(0, emb // 8, describe, 0)
-    for load in loads:
-        load.wait()
     many = beads * atoms
-    bias, bias2, out_col = (wide_columns(fit_columns[at, 0:fit, :], many) for at in range(3))
+    bias, bias2, out_col = (wide_columns(fit_columns[at], many) for at in range(3))
     hidden = jnp.tanh(dot(cols_here[...], desc[...]) + bias)
-    more = jnp.tanh(dot(fit_w2t[...], hidden.astype(bf16)) + bias2)
+    more = jnp.tanh(dot(w2_t[...], hidden.astype(bf16)) + bias2)
     d_more = out_col * (1.0 - more * more)
-    d_hidden = out_col + split_dot(fit_w2[...], d_more).astype(bf16).astype(f32)
+    d_hidden = out_col + split_dot(w2_here[...], d_more).astype(bf16).astype(f32)
     d_pre = d_hidden * (1.0 - hidden * hidden)
     d_desc[...] = split_dot(rows_here[...], d_pre).astype(bf16).astype(f32)
 
@@ -368,21 +371,19 @@
         turned = jnp.transpose(totals[j * LANES : (j + 1) * LANES, :])
         whole = turned[0:24, :] + turned[24:48, :]
         for c in range(comps):
-            out[at + c * beads : at + (c + 1) * beads, :] = -whole[c * 8 : c * 8 + beads, 0:atoms]
-
-
-def finish_kernel(pos, mom, own_f, near, link, far, maps, *outs_and_scratch):
+            value = -whole[c * 8 : c * 8 + beads, 0:atoms]
+            if j == 0:
+                value = mom[c * beads : (c + 1) * beads, :] + (time_step * force_gain) * value
+            out[at + c * beads : at + (c + 1) * beads, :] = value
+
+
+def finish_kernel(own, kicked, near, link, far, maps, *outs_and_scratch):
     outs, stacked = outs_and_scratch[:-1], outs_and_scratch[-1]
-    beads, comps, atoms = pos.shape
-    rows = beads * comps
-    force = (own_f[...] + near[0:rows, :]) + (link[0:rows, :] + far[rows : 2 * rows, :])
+    rows, atoms = kicked.shape
+    force = near[0:rows, :] + (link[0:rows, :] + far[rows : 2 * rows, :])
     stacked[...] = jnp.zeros_like(stacked)
-    stacked[rows : 2 * rows, 0:atoms] = force * (time_step * force_gain)
-    for b in range(beads):
-        for c in range(comps):
-            at = c * beads + b
-            stacked[at : at + 1, 0:atoms] = pos[b, c : c + 1, :]
-            stacked[rows + at : rows + at + 1, 0:atoms] += mom[b, c : c + 1, :]
+    stacked[0:rows, 0:atoms] = own[0:rows, :]
+    stacked[rows : 2 * rows, 0:atoms] = kicked[...] + force * (time_step * force_gain)
     shares = jnp.dot(
         maps[lax.axis_index("bead")],
         stacked[...],
@@ -390,7 +391,9 @@
         preferred_element_type=f32,
     )
     for at, out in enumerate(outs):
-        out[...] = shares[at * 2 * rows : (at + 1) * 2 * rows, 0:atoms]
+        for k in range(out.shape[0]):
+            start = at * 2 * rows + k * out.shape[1]
+            out[k] = shares[start : start + out.shape[1], 0:atoms]
 
 
 def on_device(
@@ -409,6 +412,9 @@
     shape = jax.ShapeDtypeStruct
     big = pltpu.CompilerParams(vmem_limit_bytes=50 * 1024 * 1024)
 
+    vmem = pl.BlockSpec(memory_space=pltpu.VMEM)
+    anywhere = pl.BlockSpec(memory_space=pl.ANY)
+
     domains = lax.axis_size("space")
     pairs = [(d, d + 1) for d in range(0, domains - 1, 2)]
     links = [(d, d + 1) for d in range(1, domains - 1, 2)]
@@ -416,39 +422,23 @@
     def swapped(value, which):
         return lax.ppermute(value, "space", which + [(b, a) for a, b in which])
 
-    own = jnp.concatenate(
-        [positions.transpose(1, 0, 2).reshape(rows, atoms), send_rows[0].astype(f32)], axis=0
-    )
+    send_blocks = send_rows.shape[1]
+    own, momenta_rows = pl.pallas_call(
+        pack_kernel,
+        out_shape=[shape((rows + send_blocks, atoms), f32), shape((rows, atoms), f32)],
+        in_specs=[vmem] * 3,
+        out_specs=[vmem] * 2,
+        name="pack",
+    )(positions.transpose(1, 0, 2), momenta.transpose(1, 0, 2), send_rows)
     core = swapped(own, pairs)
     link = swapped(jnp.concatenate([own, core], axis=0), links)
     far = swapped(link, pairs)
 
-    w_embed_t, fit_rows, fit_cols, fit_w2, fit_w2t, columns, fit_columns = pl.pallas_call(
-        prepare_kernel,
-        out_shape=[
-            shape((emb, emb), bf16),
-            shape((wide, fit_pad), bf16),
-            shape((fit_pad, wide), bf16),
-            shape((fit_pad, fit_pad), bf16),
-            shape((fit_pad, fit_pad), bf16),
-            shape((3, emb, LANES), f32),
-            shape((3, fit_pad, LANES), f32),
-        ],
-        compiler_params=big,
-        cost_estimate=pl.CostEstimate(
-            flops=2 * wide * fit_pad * (LANES + fit_pad), bytes_accessed=8 * wide * fit_pad, transcendentals=0
-        ),
-        name="weights",
-    )(
-        embed_first, embed_weight, embed_bias.reshape(1, emb), fit_weight,
-        fit_bias.reshape(1, fit), fit_weight2, fit_bias2.reshape(1, fit), fit_out.reshape(1, fit),
-    )
-    vmem = pl.BlockSpec(memory_space=pltpu.VMEM)
-    anywhere = pl.BlockSpec(memory_space=pl.ANY)
     own_f, near_f, link_f = pl.pallas_call(
         force_kernel,
         out_shape=[shape((rows, atoms), f32), shape((2 * rows, atoms), f32), shape((2 * rows, atoms), f32)],
-        in_specs=[vmem] * 7 + [anywhere] * 2 + [vmem] * 4,
+        in_specs=[vmem] * 10 + [anywhere] + [vmem] * 4,
+        out_specs=[vmem] * 3,
         scratch_shapes=[
             pltpu.VMEM((5, comps, 8, LANES), f32),
             pltpu.VMEM((8, LANES), jnp.int32),
@@ -467,15 +457,22 @@
             pltpu.VMEM((5, 8, width), f32),
             pltpu.VMEM((5 * LANES, LANES), f32),
             pltpu.VMEM((blocks, 8, width), jnp.int32),
+            pltpu.VMEM((fit, wide), bf16),
             pltpu.VMEM((wide, fit_pad), bf16),
             pltpu.VMEM((fit_pad, wide), bf16),
-            pltpu.SemaphoreType.DMA((2,)),
+            pltpu.VMEM((emb, emb), bf16),
+            pltpu.VMEM((fit_pad, fit_pad), bf16),
+            pltpu.VMEM((fit_pad, fit_pad), bf16),
+            pltpu.VMEM((3, emb, LANES), f32),
+            pltpu.VMEM((3, fit_pad, LANES), f32),
+            pltpu.SemaphoreType.DMA(()),
         ],
         compiler_params=big,
         name="forces",
     )(
-        own, core, link, far, neighbours.reshape(blocks, width), nbr_count.reshape(1, atoms),
-        w_embed_t, fit_rows, fit_cols, columns, fit_columns, fit_w2, fit_w2t,
+        own, momenta_rows, core, link, far, neighbours.reshape(blocks, width), nbr_count.reshape(1, atoms),
+        embed_first, embed_weight, embed_bias.reshape(1, emb), fit_weight.T,
+        fit_bias.reshape(1, fit), fit_weight2, fit_bias2.reshape(1, fit), fit_out.reshape(1, fit),
     )
     near = swapped(near_f, pairs)
     link = swapped(
@@ -487,16 +484,18 @@
     maps = jnp.asarray(propagation_table(groups, bead_dev))
     shares = pl.pallas_call(
         finish_kernel,
-        out_shape=[shape((2 * rows, atoms), f32)] * groups,
+        out_shape=[shape((2 * comps, bead_dev, atoms), f32)] * groups,
+        in_specs=[vmem] * 6,
+        out_specs=[vmem] * groups,
         scratch_shapes=[pltpu.VMEM((LANES, LANES), f32)],
         name="propagate",
-    )(positions, momenta, own_f, near, link, far, maps)
+    )(own, own_f, near, link, far, maps)
     if groups == 2:
         result = shares[0] + lax.ppermute(shares[1], "bead", [(0, 1), (1, 0)])
     else:
         parts = lax.all_to_all(jnp.stack(shares), "bead", split_axis=0, concat_axis=0, tiled=True)
         result = parts.sum(axis=0)
-    return (result[:rows].reshape(positions.shape), result[rows:].reshape(positions.shape))
+    return (result[:comps].transpose(1, 0, 2), result[comps:].transpose(1, 0, 2))
 
 
 def solution(mesh):

time: 60.6 us -> 59.1 us (0.975)
  waiting for transfers between devices: 7.8 us -> 12.7 us
  local copies, waits for them, and re-layouts: 8.08 us -> 3.85 us
  Pallas kernels: 33.9 us -> 32.1 us
  other arithmetic: 0.74 us -> 1.42 us
    ppermute x6, waiting for transfers between devices: 5.39 us -> 10.2 us  [swapped(): return lax.ppermute(value, 'space', which + [(b, a) for a, b in which])]
    unnamed x38 -> x33, local copies, waits for them, and re-layouts: 7.28 us -> 3.17 us
    pallas_call x2, Pallas kernels: 5.33 us -> 3.02 us  [the longest x1 1.67 us: on_device(): pl.pallas_call(finish_kernel, out_shape=[shape((2 * comps, bead_dev, atom...]
    reshape x3 -> x0, local copies, waits for them, and re-layouts: 0.72 us -> none  [the longest x1 0.71 us: on_device(): positions.transpose(1, 0, 2).reshape(rows, atoms)]
    concatenate x1, other arithmetic: 0.01 us -> 0.7 us  [on_device(): link = swapped(jnp.concatenate([own, core], axis=0), links)]
  transfers between devices with their start and end apart: 7 -> 7, of which waited for: 5 -> 7; matrix products, arithmetic and copies ran while one was open for 6% -> 0% of each run, Pallas kernels for 6% -> 0%
where the time goes in v3:
time: 59.1 us; the launch traced here: 58.7 us
  Pallas kernels  32.1 us (54%)
  waiting for transfers between devices  12.7 us (21%)
  starting transfers between devices  7.88 us (13%)
  local copies, waits for them, and re-layouts  3.85 us (7%)
  other arithmetic  1.42 us (2%)
  between operations  0.77 us (1%)
    pallas_call x1, Pallas kernels, on_device(): pl.pallas_call(force_kernel, out_shape=[shape((rows, atoms), f32), shape(...  29.1 us
    ppermute x6, waiting for transfers between devices, swapped(): return lax.ppermute(value, 'space', which + [(b, a) for a, b in which])  10.2 us
    ppermute x6, starting transfers between devices, swapped(): return lax.ppermute(value, 'space', which + [(b, a) for a, b in which])  6.39 us
    unnamed x33, local copies, waits for them, and re-layouts  3.17 us
    ppermute x1, waiting for transfers between devices, on_device(): result = shares[0] + lax.ppermute(shares[1], 'bead', [(0, 1), (1, 0)])  2.42 us
    pallas_call x1, Pallas kernels, on_device(): pl.pallas_call(finish_kernel, out_shape=[shape((2 * comps, bead_dev, atom...  1.67 us
    ppermute x1, starting transfers between devices, on_device(): result = shares[0] + lax.ppermute(shares[1], 'bead', [(0, 1), (1, 0)])  1.49 us
    pallas_call x1, Pallas kernels, on_device(): pl.pallas_call(pack_kernel, out_shape=[shape((rows + send_blocks, atoms),...  1.36 us
  transfers between devices with their start and end apart: 7, of which 7 were waited for; matrix products, arithmetic and copies ran while one was open for 0% of the time, Pallas kernels for 0%

profile of v3, /device:TPU:8, one launch (start us, length us, event | category | flops | bytes accessed | tf_op | source)
XLA Modules:
  0.0 58.7 jit_solution(1902646759531318502)
XLA Ops:
  0.7 1.4 %pack.1 = (f32[16,96]{1,0:T(8,128)}, f32[12,96]{1,0:T(8,128)}) custom-call(f32[3,4,96]{2,1,0:T(4,128)} %bitcast.18, f32[3,4,96]{2,1,0:T(4,128)} %bitcast.19, s32[1,4,96]{2,1,0:T(4,128)} %send.1), custom_call_target="tpu_custom_call" | custom-call | tf_op jit(solution)/shard_map/pack/pallas_call | solution.py:426
  2.0 1.4 %collective-permute-done.core = f32[16,96]{1,0:T(8,128)S(1)} collective-permute-done((f32[16,96]{1,0:T(8,128)}, f32[16,96]{1,0:T(8,128)S(1)}, u32[]{:S(2)}, u32[]{:S(2)}) %collective-permute-start) | collective-permute-done | bytes 6176 | tf_op jit(solution)/shard_map/ppermute | solution.py:423
  3.4 0.7 %pad_maximum_fusion = f32[32,96]{1,0:T(8,128)S(1)} fusion(f32[16,96]{1,0:T(8,128)S(1)} %collective-permute-done.core, f32[16,96]{1,0:T(8,128)} %get-tuple-element.9.own), kind=kLoop, calls=%fused_computation | loop fusion | flops 3072 | bytes 24576 | tf_op jit(solution)/shard_map/concatenate | solution.py:434
  4.1 3.1 %collective-permute-start.1 = (f32[32,96]{1,0:T(8,128)S(1)}, f32[32,96]{1,0:T(8,128)S(1)}, u32[]{:S(2)}, u32[]{:S(2)}) collective-permute-start(f32[32,96]{1,0:T(8,128)S(1)} %pad_maximum_fusion), channel_id=1, source_target_pairs={{2,4},{6,8},{10,12},{14,16},{18,20},{22,24},{26,28},{4,2},{8,6},{1... | collective-permute-start | bytes 36872 | tf_op jit(solution)/shard_map/ppermute | solution.py:423
  7.2 2.9 %collective-permute-done.1.link = f32[32,96]{1,0:T(8,128)S(1)} collective-permute-done((f32[32,96]{1,0:T(8,128)S(1)}, f32[32,96]{1,0:T(8,128)S(1)}, u32[]{:S(2)}, u32[]{:S(2)}) %collective-permute-start.1) | collective-permute-done | bytes 12320 | tf_op jit(solution)/shard_map/ppermute | solution.py:423
  10.0 0.1 copy.17
  10.2 0.1 reshape.22.idx
  10.2 1.0 %collective-permute-done.2.far = f32[32,96]{1,0:T(8,128)S(1)} collective-permute-done((f32[32,96]{1,0:T(8,128)S(1)}, f32[32,96]{1,0:T(8,128)S(1)}, u32[]{:S(2)}, u32[]{:S(2)}) %collective-permute-start.2) | collective-permute-done | bytes 12320 | tf_op jit(solution)/shard_map/ppermute | solution.py:423
  11.3 0.6 %copy-done.7 = f32[240]{0:T(256)S(1)} copy-done((f32[240]{0:T(256)S(1)}, f32[240]{0:T(256)}, u32[]{:S(2)}) %copy-start.7) | copy-done | bytes 984
  11.9 0.0 copy-done.6
  12.0 1.2 %copy-done = bf16[2048,240]{0,1:T(8,128)(2,1)S(1)} copy-done((bf16[2048,240]{0,1:T(8,128)(2,1)S(1)}, bf16[2048,240]{0,1:T(8,128)(2,1)}, u32[]{:S(2)}) %copy-start) | copy-done | bytes 983064
  13.2 29.1 %forces.1 = (f32[12,96]{1,0:T(8,128)S(1)}, f32[24,96]{1,0:T(8,128)S(1)}, f32[24,96]{1,0:T(8,128)S(1)}) custom-call(f32[16,96]{1,0:T(8,128)S(1)} %copy-done.2, f32[12,96]{1,0:T(8,128)S(1)} %copy-done.4, f32[16,96]{1,0:T(8,128)S(1)} %collective-permute-done.core, f32[32,96]{1,0:T(8,128)S(1)} %collective-permute-done.1.link, ...), custom_call_target="tpu_custom_call" | custom-call | tf_op jit(solution)/shard_map/forces/pallas_call | solution.py:437
  42.2 0.2 collective-permute-start.3
  42.5 1.0 %collective-permute-done.3.near = f32[24,96]{1,0:T(8,128)S(1)} collective-permute-done((f32[24,96]{1,0:T(8,128)S(1)}, f32[24,96]{1,0:T(8,128)S(1)}, u32[]{:S(2)}, u32[]{:S(2)}) %collective-permute-start.3) | collective-permute-done | bytes 9248 | tf_op jit(solution)/shard_map/ppermute | solution.py:423
  43.5 0.6 copy-done.12
  44.1 3.1 %collective-permute-start.4 = (f32[24,96]{1,0:T(8,128)S(1)}, f32[24,96]{1,0:T(8,128)S(1)}, u32[]{:S(2)}, u32[]{:S(2)}) collective-permute-start(f32[24,96]{1,0:T(8,128)S(1)} %pad_maximum_fusion.1), channel_id=1, source_target_pairs={{2,4},{6,8},{10,12},{14,16},{18,20},{22,24},{26,28},{4,2},{8,6},{1... | collective-permute-start | bytes 27656 | tf_op jit(solution)/shard_map/ppermute | solution.py:423
  47.2 2.8 %collective-permute-done.4.link = f32[24,96]{1,0:T(8,128)S(1)} collective-permute-done((f32[24,96]{1,0:T(8,128)S(1)}, f32[24,96]{1,0:T(8,128)S(1)}, u32[]{:S(2)}, u32[]{:S(2)}) %collective-permute-start.4) | collective-permute-done | bytes 9248 | tf_op jit(solution)/shard_map/ppermute | solution.py:423
  50.0 1.2 %collective-permute-done.5.far = f32[24,96]{1,0:T(8,128)S(1)} collective-permute-done((f32[24,96]{1,0:T(8,128)S(1)}, f32[24,96]{1,0:T(8,128)S(1)}, u32[]{:S(2)}, u32[]{:S(2)}) %collective-permute-start.5) | collective-permute-done | bytes 9248 | tf_op jit(solution)/shard_map/ppermute | solution.py:423
  51.2 0.6 %copy-done.15 = f32[24,96]{1,0:T(8,128)} copy-done((f32[24,96]{1,0:T(8,128)}, f32[24,96]{1,0:T(8,128)S(1)}, u32[]{:S(2)}) %copy-start.15) | copy-done | bytes 9240
  51.8 1.7 %propagate.1 = (f32[6,4,96]{2,1,0:T(4,128)}, f32[6,4,96]{2,1,0:T(4,128)}) custom-call(f32[16,96]{1,0:T(8,128)} %get-tuple-element.9.own, f32[12,96]{1,0:T(8,128)} %copy-done.5, f32[24,96]{1,0:T(8,128)} %copy-done.12, f32[24,96]{1,0:T(8,128)} %copy-done.14, f32[24,96]{1,0:T(8,128)} %copy-done.15, f32[2,48,128]{2,1,0:T(8,128)} %constant.2.clone.maps), custom_call_target="tpu_custom_call" | custom-call | tf_op jit(solution)/shard_map/propagate/pallas_call | solution.py:485
  53.4 1.5 %collective-permute-start.6 = (f32[6,4,96]{2,1,0:T(4,128)}, f32[6,4,96]{2,1,0:T(4,128)S(1)}, u32[]{:S(2)}, u32[]{:S(2)}) collective-permute-start(f32[6,4,96]{2,1,0:T(4,128)} %get-tuple-element.15), channel_id=1, source_target_pairs={{0,1},{1,0},{2,3},{3,2},{4,5},{5,4},{6,7},{7,6},{8,9},{9,8},{10,11... | collective-permute-start | bytes 27656 | tf_op jit(solution)/shard_map/ppermute | solution.py:494
  54.9 2.4 %collective-permute-done.6 = f32[6,4,96]{2,1,0:T(4,128)S(1)} collective-permute-done((f32[6,4,96]{2,1,0:T(4,128)}, f32[6,4,96]{2,1,0:T(4,128)S(1)}, u32[]{:S(2)}, u32[]{:S(2)}) %collective-permute-start.6) | collective-permute-done | bytes 9248 | tf_op jit(solution)/shard_map/ppermute | solution.py:494
  57.3 0.7 %add.7 = f32[6,4,96]{2,1,0:T(4,128)S(1)} add(f32[6,4,96]{2,1,0:T(4,128)} %get-tuple-element.14, f32[6,4,96]{2,1,0:T(4,128)S(1)} %collective-permute-done.6) | non-fusion elementwise | flops 2304 | bytes 27648 | tf_op jit(solution)/shard_map/add | solution.py:494
  58.1 0.6 %slice_bitcast_fusion = (f32[4,3,96]{2,0,1:T(4,128)}, f32[4,3,96]{2,0,1:T(4,128)}) fusion(f32[6,4,96]{2,1,0:T(4,128)S(1)} %add.7), kind=kLoop, calls=%fused_computation.3 | loop fusion | bytes 18432 | tf_op jit(solution)/shard_map/transpose | solution.py:498
  (32 shorter events, 0.1 us)
Async XLA Ops:
  0.6 9.4 %copy-start.13 = (s32[96,64]{0,1:T(8,128)S(1)}, s32[96,64]{0,1:T(8,128)}, u32[]{:S(2)}) copy-start(s32[96,64]{0,1:T(8,128)} %param.16) | copy-start | bytes 73732
  0.6 10.6 %copy-start.1 = (bf16[240,240]{1,0:T(8,128)(2,1)S(1)}, bf16[240,240]{1,0:T(8,128)(2,1)}, u32[]{:S(2)}) copy-start(bf16[240,240]{1,0:T(8,128)(2,1)} %fit_w2.1) | copy-start | bytes 345604
  2.0 1.4 %collective-permute-start = (f32[16,96]{1,0:T(8,128)}, f32[16,96]{1,0:T(8,128)S(1)}, u32[]{:S(2)}, u32[]{:S(2)}) collective-permute-start(f32[16,96]{1,0:T(8,128)} %get-tuple-element.9.own), channel_id=1, source_target_pairs={{0,2},{4,6},{8,10},{12,14},{16,18},{20,22},{24,26},{28,30},{2,0},{... | collective-permute-start | bytes 18440 | tf_op jit(solution)/shard_map/ppermute | solution.py:423
  4.1 5.9 %collective-permute-start.1 = (f32[32,96]{1,0:T(8,128)S(1)}, f32[32,96]{1,0:T(8,128)S(1)}, u32[]{:S(2)}, u32[]{:S(2)}) collective-permute-start(f32[32,96]{1,0:T(8,128)S(1)} %pad_maximum_fusion), channel_id=1, source_target_pairs={{2,4},{6,8},{10,12},{14,16},{18,20},{22,24},{26,28},{4,2},{8,6},{1... | collective-permute-start | bytes 36872 | tf_op jit(solution)/shard_map/ppermute | solution.py:423
  10.0 1.2 %collective-permute-start.2 = (f32[32,96]{1,0:T(8,128)S(1)}, f32[32,96]{1,0:T(8,128)S(1)}, u32[]{:S(2)}, u32[]{:S(2)}) collective-permute-start(f32[32,96]{1,0:T(8,128)S(1)} %collective-permute-done.1.link), channel_id=1, source_target_pairs={{0,2},{4,6},{8,10},{12,14},{16,18},{20,22},{24,26},{28,30},{2,0},{... | collective-permute-start | bytes 36872 | tf_op jit(solution)/shard_map/ppermute | solution.py:423
  10.1 1.1 %copy-start.3 = (bf16[128,128]{1,0:T(8,128)(2,1)S(1)}, bf16[128,128]{1,0:T(8,128)(2,1)}, u32[]{:S(2)}) copy-start(bf16[128,128]{1,0:T(8,128)(2,1)} %w_embed.1) | copy-start | bytes 98308
  10.1 1.1 %copy-start.4 = (f32[12,96]{1,0:T(8,128)S(1)}, f32[12,96]{1,0:T(8,128)}, u32[]{:S(2)}) copy-start(f32[12,96]{1,0:T(8,128)} %get-tuple-element.10.mom) | copy-start | bytes 13828
  10.2 1.1 %copy-start.2 = (f32[16,96]{1,0:T(8,128)S(1)}, f32[16,96]{1,0:T(8,128)}, u32[]{:S(2)}) copy-start(f32[16,96]{1,0:T(8,128)} %get-tuple-element.9.own) | copy-start | bytes 18436
  11.2 0.7 %copy-start.7 = (f32[240]{0:T(256)S(1)}, f32[240]{0:T(256)}, u32[]{:S(2)}) copy-start(f32[240]{0:T(256)} %param.23) | copy-start | bytes 2884
  11.2 0.7 %copy-start.8 = (f32[240]{0:T(256)S(1)}, f32[240]{0:T(256)}, u32[]{:S(2)}) copy-start(f32[240]{0:T(256)} %param.25) | copy-start | bytes 2884
  11.2 0.7 %copy-start.9 = (f32[240]{0:T(256)S(1)}, f32[240]{0:T(256)}, u32[]{:S(2)}) copy-start(f32[240]{0:T(256)} %param.26) | copy-start | bytes 2884
  11.2 0.7 %copy-start.11 = (f32[128]{0:T(128)S(1)}, f32[128]{0:T(128)}, u32[]{:S(2)}) copy-start(f32[128]{0:T(128)} %param.21) | copy-start | bytes 1540
  11.2 0.7 %copy-start.6 = (f32[2,128]{1,0:T(2,128)S(1)}, f32[2,128]{1,0:T(2,128)}, u32[]{:S(2)}) copy-start(f32[2,128]{1,0:T(2,128)} %first.1) | copy-start | bytes 3076
  11.2 0.7 %copy-start.10 = (s32[96]{0:T(128)S(1)}, s32[96]{0:T(128)}, u32[]{:S(2)}) copy-start(s32[96]{0:T(128)} %param.17) | copy-start | bytes 1156
  12.0 1.2 %copy-start = (bf16[2048,240]{0,1:T(8,128)(2,1)S(1)}, bf16[2048,240]{0,1:T(8,128)(2,1)}, u32[]{:S(2)}) copy-start(bf16[2048,240]{0,1:T(8,128)(2,1)} %param.22) | copy-start | bytes 2949124
  42.2 1.3 %copy-start.5 = (f32[12,96]{1,0:T(8,128)}, f32[12,96]{1,0:T(8,128)S(1)}, u32[]{:S(2)}) copy-start(f32[12,96]{1,0:T(8,128)S(1)} %get-tuple-element.11.kicked) | copy-start | bytes 13828
  42.2 1.2 %collective-permute-start.3 = (f32[24,96]{1,0:T(8,128)S(1)}, f32[24,96]{1,0:T(8,128)S(1)}, u32[]{:S(2)}, u32[]{:S(2)}) collective-permute-start(f32[24,96]{1,0:T(8,128)S(1)} %get-tuple-element.12), channel_id=1, source_target_pairs={{0,2},{4,6},{8,10},{12,14},{16,18},{20,22},{24,26},{28,30},{2,0},{... | collective-permute-start | bytes 27656 | tf_op jit(solution)/shard_map/ppermute | solution.py:423
  43.5 0.6 %copy-start.12 = (f32[24,96]{1,0:T(8,128)}, f32[24,96]{1,0:T(8,128)S(1)}, u32[]{:S(2)}) copy-start(f32[24,96]{1,0:T(8,128)S(1)} %collective-permute-done.3.near) | copy-start | bytes 27652
  44.1 5.9 %collective-permute-start.4 = (f32[24,96]{1,0:T(8,128)S(1)}, f32[24,96]{1,0:T(8,128)S(1)}, u32[]{:S(2)}, u32[]{:S(2)}) collective-permute-start(f32[24,96]{1,0:T(8,128)S(1)} %pad_maximum_fusion.1), channel_id=1, source_target_pairs={{2,4},{6,8},{10,12},{14,16},{18,20},{22,24},{26,28},{4,2},{8,6},{1... | collective-permute-start | bytes 27656 | tf_op jit(solution)/shard_map/ppermute | solution.py:423
  50.0 1.2 %copy-start.14 = (f32[24,96]{1,0:T(8,128)}, f32[24,96]{1,0:T(8,128)S(1)}, u32[]{:S(2)}) copy-start(f32[24,96]{1,0:T(8,128)S(1)} %collective-permute-done.4.link) | copy-start | bytes 27652
  50.0 1.2 %collective-permute-start.5 = (f32[24,96]{1,0:T(8,128)S(1)}, f32[24,96]{1,0:T(8,128)S(1)}, u32[]{:S(2)}, u32[]{:S(2)}) collective-permute-start(f32[24,96]{1,0:T(8,128)S(1)} %collective-permute-done.4.link), channel_id=1, source_target_pairs={{0,2},{4,6},{8,10},{12,14},{16,18},{20,22},{24,26},{28,30},{2,0},{... | collective-permute-start | bytes 27656 | tf_op jit(solution)/shard_map/ppermute | solution.py:423
  51.2 0.6 %copy-start.15 = (f32[24,96]{1,0:T(8,128)}, f32[24,96]{1,0:T(8,128)S(1)}, u32[]{:S(2)}) copy-start(f32[24,96]{1,0:T(8,128)S(1)} %collective-permute-done.5.far) | copy-start | bytes 27652
  53.4 3.9 %collective-permute-start.6 = (f32[6,4,96]{2,1,0:T(4,128)}, f32[6,4,96]{2,1,0:T(4,128)S(1)}, u32[]{:S(2)}, u32[]{:S(2)}) collective-permute-start(f32[6,4,96]{2,1,0:T(4,128)} %get-tuple-element.15), channel_id=1, source_target_pairs={{0,1},{1,0},{2,3},{3,2},{4,5},{5,4},{6,7},{7,6},{8,9},{9,8},{10,11... | collective-permute-start | bytes 27656 | tf_op jit(solution)/shard_map/ppermute | solution.py:494

commit v4 on v3

--- a/solution.py
+++ b/solution.py
@@ -113,11 +113,10 @@
     return dot(a, high) + dot(a, (b - high.astype(f32)).astype(bf16))
 
 
-def pack_kernel(pos, mom, send, out, mom_out):
+def pack_kernel(pos, send, out):
     comps, beads, _ = pos.shape
     for c in range(comps):
         out[c * beads : (c + 1) * beads, :] = pos[c]
-        mom_out[c * beads : (c + 1) * beads, :] = mom[c]
     out[comps * beads : comps * beads + send.shape[1], :] = send[0].astype(f32)
 
 
@@ -131,7 +130,7 @@
     own_f, near_f, link_f,
     table, counts, sent, radial, inverse, offset, second, slope,
     moment, moment_t, desc, d_desc, d_moment_t, d_moment, pair_grad, totals, index,
-    fit_here, rows_here, cols_here, w_embed_t, w2_here, w2_t, columns, fit_columns, loaded,
+    rows_here, cols_here, w_embed_t, w2_here, w2_t, columns, fit_columns,
 ):
     beads = 4
     comps = 3
@@ -142,9 +141,6 @@
     fit, wide = fit_t.shape
     fit_pad = rows_here.shape[1]
     rows = beads * comps
-    load = pltpu.make_async_copy(fit_t, fit_here, loaded)
-    load.start()
-
     odd = lax.rem(lax.axis_index("space"), 2) == 1
     block_of = ((2, 1), (1, 2), (0, 3), (3, 0))
     table[...] = jnp.zeros_like(table)
@@ -187,7 +183,6 @@
     blank = jnp.zeros((LANES, fit_pad - fit), f32)
     chunks = wide // LANES
     each = -(-chunks // blocks)
-    load.wait()
 
     lane = lax.broadcasted_iota(jnp.int32, (8, LANES), 1)
 
@@ -195,7 +190,7 @@
         for turn in range(each):
             chunk = jnp.minimum(each * i + turn, chunks - 1)
             part = pl.ds(pl.multiple_of(chunk * LANES, LANES), LANES)
-            chunk_t = fit_here[:, part]
+            chunk_t = fit_t[:, part]
             rows_here[part, :] = jnp.concatenate([dot_nt(order, chunk_t), blank], axis=1).astype(bf16)
             cols_here[0:fit, part] = dot_nt(chunk_t, order).astype(bf16)
         for part in range(width // LANES):
@@ -373,7 +368,7 @@
         for c in range(comps):
             value = -whole[c * 8 : c * 8 + beads, 0:atoms]
             if j == 0:
-                value = mom[c * beads : (c + 1) * beads, :] + (time_step * force_gain) * value
+                value = mom[c] + (time_step * force_gain) * value
             out[at + c * beads : at + (c + 1) * beads, :] = value
 
 
@@ -410,10 +405,10 @@
     width = GROUP * listed
     many = bead_dev * atoms
     shape = jax.ShapeDtypeStruct
-    big = pltpu.CompilerParams(vmem_limit_bytes=50 * 1024 * 1024)
+    big = pltpu.CompilerParams(vmem_limit_bytes=44 * 1024 * 1024)
+    small = pltpu.CompilerParams(vmem_limit_bytes=4 * 1024 * 1024)
 
     vmem = pl.BlockSpec(memory_space=pltpu.VMEM)
-    anywhere = pl.BlockSpec(memory_space=pl.ANY)
 
     domains = lax.axis_size("space")
     pairs = [(d, d + 1) for d in range(0, domains - 1, 2)]
@@ -423,13 +418,14 @@
         return lax.ppermute(value, "space", which + [(b, a) for a, b in which])
 
     send_blocks = send_rows.shape[1]
-    own, momenta_rows = pl.pallas_call(
+    own = pl.pallas_call(
         pack_kernel,
-        out_shape=[shape((rows + send_blocks, atoms), f32), shape((rows, atoms), f32)],
-        in_specs=[vmem] * 3,
-        out_specs=[vmem] * 2,
+        out_shape=shape((rows + send_blocks, atoms), f32),
+        in_specs=[vmem] * 2,
+        out_specs=vmem,
+        compiler_params=small,
         name="pack",
-    )(positions.transpose(1, 0, 2), momenta.transpose(1, 0, 2), send_rows)
+    )(positions.transpose(1, 0, 2), send_rows)
     core = swapped(own, pairs)
     link = swapped(jnp.concatenate([own, core], axis=0), links)
     far = swapped(link, pairs)
@@ -437,7 +433,7 @@
     own_f, near_f, link_f = pl.pallas_call(
         force_kernel,
         out_shape=[shape((rows, atoms), f32), shape((2 * rows, atoms), f32), shape((2 * rows, atoms), f32)],
-        in_specs=[vmem] * 10 + [anywhere] + [vmem] * 4,
+        in_specs=[vmem] * 15,
         out_specs=[vmem] * 3,
         scratch_shapes=[
             pltpu.VMEM((5, comps, 8, LANES), f32),
@@ -457,7 +453,6 @@
             pltpu.VMEM((5, 8, width), f32),
             pltpu.VMEM((5 * LANES, LANES), f32),
             pltpu.VMEM((blocks, 8, width), jnp.int32),
-            pltpu.VMEM((fit, wide), bf16),
             pltpu.VMEM((wide, fit_pad), bf16),
             pltpu.VMEM((fit_pad, wide), bf16),
             pltpu.VMEM((emb, emb), bf16),
@@ -465,12 +460,11 @@
             pltpu.VMEM((fit_pad, fit_pad), bf16),
             pltpu.VMEM((3, emb, LANES), f32),
             pltpu.VMEM((3, fit_pad, LANES), f32),
-            pltpu.SemaphoreType.DMA(()),
         ],
         compiler_params=big,
         name="forces",
     )(
-        own, momenta_rows, core, link, far, neighbours.reshape(blocks, width), nbr_count.reshape(1, atoms),
+        own, momenta.transpose(1, 0, 2), core, link, far, neighbours.reshape(blocks, width), nbr_count.reshape(1, atoms),
         embed_first, embed_weight, embed_bias.reshape(1, emb), fit_weight.T,
         fit_bias.reshape(1, fit), fit_weight2, fit_bias2.reshape(1, fit), fit_out.reshape(1, fit),
     )
@@ -488,6 +482,7 @@
         in_specs=[vmem] * 6,
         out_specs=[vmem] * groups,
         scratch_shapes=[pltpu.VMEM((LANES, LANES), f32)],
+        compiler_params=small,
         name="propagate",
     )(own, own_f, near, link, far, maps)
     if groups == 2:

time: 59.1 us -> 54.3 us (0.919)
  Pallas kernels: 32.1 us -> 28.9 us
  other arithmetic: 1.42 us -> 0.03 us
  waiting for transfers between devices: 12.7 us -> 11.4 us
  local copies, waits for them, and re-layouts: 3.85 us -> 4.86 us
    pallas_call x1, Pallas kernels: 1.67 us -> 0.17 us  [on_device(): pl.pallas_call(finish_kernel, out_shape=[shape((2 * comps, bead_dev, atom...]
    pallas_call x1, Pallas kernels: 1.36 us -> 0.01 us  [on_device(): pl.pallas_call(pack_kernel, out_shape=shape((rows + send_blocks, atoms),...]
    ppermute x6, waiting for transfers between devices: 10.2 us -> 9.17 us  [swapped(): return lax.ppermute(value, 'space', which + [(b, a) for a, b in which])]
    unnamed x33 -> x27, local copies, waits for them, and re-layouts: 3.17 us -> 4.18 us
    add x1, other arithmetic: 0.71 us -> 0.01 us  [on_device(): result = shares[0] + lax.ppermute(shares[1], 'bead', [(0, 1), (1, 0)])]
    concatenate x1, other arithmetic: 0.7 us -> 0.01 us  [on_device(): link = swapped(jnp.concatenate([own, core], axis=0), links)]
  transfers between devices with their start and end apart: 7 -> 7, of which waited for: 7 -> 7; matrix products, arithmetic and copies ran while one was open for 0% -> 2% of each run, Pallas kernels for 0% -> 0%
where the time goes in v4:
time: 54.3 us; the launch traced here: 53.9 us
  Pallas kernels  28.9 us (53%)
  waiting for transfers between devices  11.4 us (21%)
  starting transfers between devices  8.04 us (15%)
  local copies, waits for them, and re-layouts  4.86 us (9%)
  between operations  0.73 us (1%)
    pallas_call x1, Pallas kernels, on_device(): pl.pallas_call(force_kernel, out_shape=[shape((rows, atoms), f32), shape(...  28.8 us
    ppermute x6, waiting for transfers between devices, swapped(): return lax.ppermute(value, 'space', which + [(b, a) for a, b in which])  9.17 us
    ppermute x6, starting transfers between devices, swapped(): return lax.ppermute(value, 'space', which + [(b, a) for a, b in which])  6.52 us
    unnamed x27, local copies, waits for them, and re-layouts  4.18 us
    ppermute x1, waiting for transfers between devices, on_device(): result = shares[0] + lax.ppermute(shares[1], 'bead', [(0, 1), (1, 0)])  2.19 us
    ppermute x1, starting transfers between devices, on_device(): result = shares[0] + lax.ppermute(shares[1], 'bead', [(0, 1), (1, 0)])  1.52 us
  transfers between devices with their start and end apart: 7, of which 7 were waited for; matrix products, arithmetic and copies ran while one was open for 2% of the time, Pallas kernels for 0%

profile of v4, /device:TPU:8, one launch (start us, length us, event | category | flops | bytes accessed | tf_op | source)
XLA Modules:
  0.0 53.9 jit_solution(7425355981992530780)
XLA Ops:
  0.6 0.7 %copy-done.5 = f32[4,3,96]{2,0,1:T(4,128)S(1)} copy-done((f32[4,3,96]{2,0,1:T(4,128)S(1)}, f32[4,3,96]{2,0,1:T(4,128)}, u32[]{:S(2)}) %copy-start.5) | copy-done | bytes 4632
  1.4 0.7 %copy-done.6 = s32[1,4,96]{2,1,0:T(4,128)S(1)} copy-done((s32[1,4,96]{2,1,0:T(4,128)S(1)}, s32[1,4,96]{2,1,0:T(4,128)}, u32[]{:S(2)}) %copy-start.6) | copy-done | bytes 1560
  2.1 1.2 %collective-permute-done.core = f32[16,96]{1,0:T(8,128)S(1)} collective-permute-done((f32[16,96]{1,0:T(8,128)S(1)}, f32[16,96]{1,0:T(8,128)S(1)}, u32[]{:S(2)}, u32[]{:S(2)}) %collective-permute-start) | collective-permute-done | bytes 6176 | tf_op jit(solution)/shard_map/ppermute | solution.py:418
  3.2 3.1 %collective-permute-start.1 = (f32[32,96]{1,0:T(8,128)S(1)}, f32[32,96]{1,0:T(8,128)S(1)}, u32[]{:S(2)}, u32[]{:S(2)}) collective-permute-start(f32[32,96]{1,0:T(8,128)S(1)} %pad_maximum_fusion), channel_id=1, source_target_pairs={{2,4},{6,8},{10,12},{14,16},{18,20},{22,24},{26,28},{4,2},{8,6},{1... | collective-permute-start | bytes 36872 | tf_op jit(solution)/shard_map/ppermute | solution.py:418
  6.3 2.9 %collective-permute-done.1.link = f32[32,96]{1,0:T(8,128)S(1)} collective-permute-done((f32[32,96]{1,0:T(8,128)S(1)}, f32[32,96]{1,0:T(8,128)S(1)}, u32[]{:S(2)}, u32[]{:S(2)}) %collective-permute-start.1) | collective-permute-done | bytes 12320 | tf_op jit(solution)/shard_map/ppermute | solution.py:418
  9.2 0.8 %copy.17 = s32[96,64]{1,0:T(8,128)S(1)} copy(s32[96,64]{0,1:T(8,128)} %param.16) | data formatting | bytes 49152 | tf_op args[2]
  10.0 0.1 reshape.22.idx
  10.1 0.2 collective-permute-done.2.far
  10.4 0.4 copy-done.3
  10.8 0.3 copy-done.4
  11.1 0.0 copy-done.9
  11.1 0.0 copy-done.10
  11.1 0.0 copy-done.7
  11.1 1.2 %copy-done = bf16[2048,240]{0,1:T(8,128)(2,1)S(1)} copy-done((bf16[2048,240]{0,1:T(8,128)(2,1)S(1)}, bf16[2048,240]{0,1:T(8,128)(2,1)}, u32[]{:S(2)}) %copy-start) | copy-done | bytes 983064
  12.3 28.8 %forces.1 = (f32[12,96]{1,0:T(8,128)S(1)}, f32[24,96]{1,0:T(8,128)S(1)}, f32[24,96]{1,0:T(8,128)S(1)}) custom-call(f32[16,96]{1,0:T(8,128)S(1)} %pack.1.own, f32[3,4,96]{2,1,0:T(4,128)S(1)} %bitcast.13, f32[16,96]{1,0:T(8,128)S(1)} %collective-permute-done.core, f32[32,96]{1,0:T(8,128)S(1)} %collective-permute-done.1.link, ...), custom_call_target="tpu_custom_call" | custom-call | tf_op jit(solution)/shard_map/forces/pallas_call | solution.py:433
  41.1 0.3 collective-permute-start.3
  41.4 0.9 %collective-permute-done.3.near = f32[24,96]{1,0:T(8,128)S(1)} collective-permute-done((f32[24,96]{1,0:T(8,128)S(1)}, f32[24,96]{1,0:T(8,128)S(1)}, u32[]{:S(2)}, u32[]{:S(2)}) %collective-permute-start.3) | collective-permute-done | bytes 9248 | tf_op jit(solution)/shard_map/ppermute | solution.py:418
  42.4 3.1 %collective-permute-start.4 = (f32[24,96]{1,0:T(8,128)S(1)}, f32[24,96]{1,0:T(8,128)S(1)}, u32[]{:S(2)}, u32[]{:S(2)}) collective-permute-start(f32[24,96]{1,0:T(8,128)S(1)} %pad_maximum_fusion.1), channel_id=1, source_target_pairs={{2,4},{6,8},{10,12},{14,16},{18,20},{22,24},{26,28},{4,2},{8,6},{1... | collective-permute-start | bytes 27656 | tf_op jit(solution)/shard_map/ppermute | solution.py:418
  45.5 2.8 %collective-permute-done.4.link = f32[24,96]{1,0:T(8,128)S(1)} collective-permute-done((f32[24,96]{1,0:T(8,128)S(1)}, f32[24,96]{1,0:T(8,128)S(1)}, u32[]{:S(2)}, u32[]{:S(2)}) %collective-permute-start.4) | collective-permute-done | bytes 9248 | tf_op jit(solution)/shard_map/ppermute | solution.py:418
  48.3 1.2 %collective-permute-done.5.far = f32[24,96]{1,0:T(8,128)S(1)} collective-permute-done((f32[24,96]{1,0:T(8,128)S(1)}, f32[24,96]{1,0:T(8,128)S(1)}, u32[]{:S(2)}, u32[]{:S(2)}) %collective-permute-start.5) | collective-permute-done | bytes 9248 | tf_op jit(solution)/shard_map/ppermute | solution.py:418
  49.5 0.2 propagate.1
  49.6 1.5 %collective-permute-start.6 = (f32[6,4,96]{2,1,0:T(4,128)S(1)}, f32[6,4,96]{2,1,0:T(4,128)S(1)}, u32[]{:S(2)}, u32[]{:S(2)}) collective-permute-start(f32[6,4,96]{2,1,0:T(4,128)S(1)} %get-tuple-element.11), channel_id=1, source_target_pairs={{0,1},{1,0},{2,3},{3,2},{4,5},{5,4},{6,7},{7,6},{8,9},{9,8},{10,11... | collective-permute-start | bytes 27656 | tf_op jit(solution)/shard_map/ppermute | solution.py:489
  51.1 2.2 %collective-permute-done.6 = f32[6,4,96]{2,1,0:T(4,128)S(1)} collective-permute-done((f32[6,4,96]{2,1,0:T(4,128)S(1)}, f32[6,4,96]{2,1,0:T(4,128)S(1)}, u32[]{:S(2)}, u32[]{:S(2)}) %collective-permute-start.6) | collective-permute-done | bytes 9248 | tf_op jit(solution)/shard_map/ppermute | solution.py:489
  53.3 0.6 %slice_bitcast_fusion = (f32[4,3,96]{2,0,1:T(4,128)}, f32[4,3,96]{2,0,1:T(4,128)}) fusion(f32[6,4,96]{2,1,0:T(4,128)S(1)} %add.7), kind=kLoop, calls=%fused_computation.3 | loop fusion | bytes 18432 | tf_op jit(solution)/shard_map/transpose | solution.py:493
  (26 shorter events, 0.1 us)
Async XLA Ops:
  0.6 9.8 %copy-start.1 = (bf16[240,240]{1,0:T(8,128)(2,1)S(1)}, bf16[240,240]{1,0:T(8,128)(2,1)}, u32[]{:S(2)}) copy-start(bf16[240,240]{1,0:T(8,128)(2,1)} %fit_w2.1) | copy-start | bytes 345604
  0.6 0.7 %copy-start.5 = (f32[4,3,96]{2,0,1:T(4,128)S(1)}, f32[4,3,96]{2,0,1:T(4,128)}, u32[]{:S(2)}) copy-start(f32[4,3,96]{2,0,1:T(4,128)} %param.14) | copy-start | bytes 13828
  1.4 0.7 %copy-start.6 = (s32[1,4,96]{2,1,0:T(4,128)S(1)}, s32[1,4,96]{2,1,0:T(4,128)}, u32[]{:S(2)}) copy-start(s32[1,4,96]{2,1,0:T(4,128)} %send.1) | copy-start | bytes 4612
  2.1 1.2 %collective-permute-start = (f32[16,96]{1,0:T(8,128)S(1)}, f32[16,96]{1,0:T(8,128)S(1)}, u32[]{:S(2)}, u32[]{:S(2)}) collective-permute-start(f32[16,96]{1,0:T(8,128)S(1)} %pack.1.own), channel_id=1, source_target_pairs={{0,2},{4,6},{8,10},{12,14},{16,18},{20,22},{24,26},{28,30},{2,0},{... | collective-permute-start | bytes 18440 | tf_op jit(solution)/shard_map/ppermute | solution.py:418
  3.2 5.9 %collective-permute-start.1 = (f32[32,96]{1,0:T(8,128)S(1)}, f32[32,96]{1,0:T(8,128)S(1)}, u32[]{:S(2)}, u32[]{:S(2)}) collective-permute-start(f32[32,96]{1,0:T(8,128)S(1)} %pad_maximum_fusion), channel_id=1, source_target_pairs={{2,4},{6,8},{10,12},{14,16},{18,20},{22,24},{26,28},{4,2},{8,6},{1... | collective-permute-start | bytes 36872 | tf_op jit(solution)/shard_map/ppermute | solution.py:418
  9.2 1.2 %collective-permute-start.2 = (f32[32,96]{1,0:T(8,128)S(1)}, f32[32,96]{1,0:T(8,128)S(1)}, u32[]{:S(2)}, u32[]{:S(2)}) collective-permute-start(f32[32,96]{1,0:T(8,128)S(1)} %collective-permute-done.1.link), channel_id=1, source_target_pairs={{0,2},{4,6},{8,10},{12,14},{16,18},{20,22},{24,26},{28,30},{2,0},{... | collective-permute-start | bytes 36872 | tf_op jit(solution)/shard_map/ppermute | solution.py:418
  10.0 0.8 %copy-start.3 = (bf16[128,128]{1,0:T(8,128)(2,1)S(1)}, bf16[128,128]{1,0:T(8,128)(2,1)}, u32[]{:S(2)}) copy-start(bf16[128,128]{1,0:T(8,128)(2,1)} %w_embed.1) | copy-start | bytes 98308
  10.4 0.7 %copy-start.4 = (f32[4,3,96]{2,0,1:T(4,128)S(1)}, f32[4,3,96]{2,0,1:T(4,128)}, u32[]{:S(2)}) copy-start(f32[4,3,96]{2,0,1:T(4,128)} %param.15) | copy-start | bytes 13828
  10.4 0.7 %copy-start.8 = (f32[240]{0:T(256)S(1)}, f32[240]{0:T(256)}, u32[]{:S(2)}) copy-start(f32[240]{0:T(256)} %param.23) | copy-start | bytes 2884
  10.4 0.7 %copy-start.9 = (f32[240]{0:T(256)S(1)}, f32[240]{0:T(256)}, u32[]{:S(2)}) copy-start(f32[240]{0:T(256)} %param.25) | copy-start | bytes 2884
  10.4 0.7 %copy-start.10 = (f32[240]{0:T(256)S(1)}, f32[240]{0:T(256)}, u32[]{:S(2)}) copy-start(f32[240]{0:T(256)} %param.26) | copy-start | bytes 2884
  10.4 0.7 %copy-start.12 = (f32[128]{0:T(128)S(1)}, f32[128]{0:T(128)}, u32[]{:S(2)}) copy-start(f32[128]{0:T(128)} %param.21) | copy-start | bytes 1540
  10.4 0.7 %copy-start.7 = (f32[2,128]{1,0:T(2,128)S(1)}, f32[2,128]{1,0:T(2,128)}, u32[]{:S(2)}) copy-start(f32[2,128]{1,0:T(2,128)} %first.1) | copy-start | bytes 3076
  10.4 0.7 %copy-start.11 = (s32[96]{0:T(128)S(1)}, s32[96]{0:T(128)}, u32[]{:S(2)}) copy-start(s32[96]{0:T(128)} %param.17) | copy-start | bytes 1156
  11.1 1.2 %copy-start = (bf16[2048,240]{0,1:T(8,128)(2,1)S(1)}, bf16[2048,240]{0,1:T(8,128)(2,1)}, u32[]{:S(2)}) copy-start(bf16[2048,240]{0,1:T(8,128)(2,1)} %param.22) | copy-start | bytes 2949124
  41.1 8.4 %copy-start.2 = (f32[2,48,128]{2,1,0:T(8,128)S(1)}, f32[2,48,128]{2,1,0:T(8,128)}, u32[]{:S(2)}) copy-start(f32[2,48,128]{2,1,0:T(8,128)} %constant.2.clone.maps) | copy-start | bytes 147460
  41.1 1.2 %collective-permute-start.3 = (f32[24,96]{1,0:T(8,128)S(1)}, f32[24,96]{1,0:T(8,128)S(1)}, u32[]{:S(2)}, u32[]{:S(2)}) collective-permute-start(f32[24,96]{1,0:T(8,128)S(1)} %get-tuple-element.8), channel_id=1, source_target_pairs={{0,2},{4,6},{8,10},{12,14},{16,18},{20,22},{24,26},{28,30},{2,0},{... | collective-permute-start | bytes 27656 | tf_op jit(solution)/shard_map/ppermute | solution.py:418
  42.4 5.9 %collective-permute-start.4 = (f32[24,96]{1,0:T(8,128)S(1)}, f32[24,96]{1,0:T(8,128)S(1)}, u32[]{:S(2)}, u32[]{:S(2)}) collective-permute-start(f32[24,96]{1,0:T(8,128)S(1)} %pad_maximum_fusion.1), channel_id=1, source_target_pairs={{2,4},{6,8},{10,12},{14,16},{18,20},{22,24},{26,28},{4,2},{8,6},{1... | collective-permute-start | bytes 27656 | tf_op jit(solution)/shard_map/ppermute | solution.py:418
  48.3 1.2 %collective-permute-start.5 = (f32[24,96]{1,0:T(8,128)S(1)}, f32[24,96]{1,0:T(8,128)S(1)}, u32[]{:S(2)}, u32[]{:S(2)}) collective-permute-start(f32[24,96]{1,0:T(8,128)S(1)} %collective-permute-done.4.link), channel_id=1, source_target_pairs={{0,2},{4,6},{8,10},{12,14},{16,18},{20,22},{24,26},{28,30},{2,0},{... | collective-permute-start | bytes 27656 | tf_op jit(solution)/shard_map/ppermute | solution.py:418
  49.6 3.7 %collective-permute-start.6 = (f32[6,4,96]{2,1,0:T(4,128)S(1)}, f32[6,4,96]{2,1,0:T(4,128)S(1)}, u32[]{:S(2)}, u32[]{:S(2)}) collective-permute-start(f32[6,4,96]{2,1,0:T(4,128)S(1)} %get-tuple-element.11), channel_id=1, source_target_pairs={{0,1},{1,0},{2,3},{3,2},{4,5},{5,4},{6,7},{7,6},{8,9},{9,8},{10,11... | collective-permute-start | bytes 27656 | tf_op jit(solution)/shard_map/ppermute | solution.py:489

commit v5 on v4

--- a/solution.py
+++ b/solution.py
@@ -235,24 +235,28 @@
 
     def embed(i, carry):
         for b in range(beads):
-            w_first = wide_columns(columns[0], width)
-            smooth = radial[0, i, b : b + 1, :]
-            one = jnp.tanh(smooth * w_first + wide_columns(columns[1], width))
-            one_slope = (1.0 - one * one) * w_first
-            low = jnp.concatenate([one.astype(bf16), one_slope.astype(bf16)], axis=1)
-            product = dot(w_embed_t[...], low)
-            two = jnp.tanh(product[:, 0:width] + wide_columns(columns[2], width))
-            both = one + two
-            total = both.astype(bf16)
-            second[b * blocks + i] = total
-            slope[b * blocks + i] = (one_slope + (1.0 - two * two) * product[:, width:]).astype(bf16)
+            totals_here, rests = [], []
+            for at in range(0, width, 2 * LANES):
+                cols = slice(at, at + 2 * LANES)
+                w_first = wide_columns(columns[0], 2 * LANES)
+                one = jnp.tanh(radial[0, i, b : b + 1, cols] * w_first + wide_columns(columns[1], 2 * LANES))
+                one_slope = (1.0 - one * one) * w_first
+                low = jnp.concatenate([one.astype(bf16), one_slope.astype(bf16)], axis=1)
+                product = dot(w_embed_t[...], low)
+                two = jnp.tanh(product[:, 0 : 2 * LANES] + wide_columns(columns[2], 2 * LANES))
+                both = one + two
+                totals_here.append(both.astype(bf16))
+                rests.append((both - totals_here[-1].astype(f32)).astype(bf16))
+                second[b * blocks + i, :, cols] = totals_here[-1]
+                slope[b * blocks + i, :, cols] = (one_slope + (1.0 - two * two) * product[:, 2 * LANES :]).astype(bf16)
+            total = jnp.concatenate(totals_here, axis=1)
             spread = jnp.concatenate(
                 [jnp.where(segment, radial[x, i, b : b + 1, :], 0.0) for x in range(4)], axis=0
             )
             high = spread.astype(bf16)
             halves = jnp.concatenate([high, (spread - high.astype(f32)).astype(bf16)], axis=0)
             part = dot_nt(halves, total)
-            rest = dot_nt(high, (both - total.astype(f32)).astype(bf16))
+            rest = dot_nt(high, jnp.concatenate(rests, axis=1))
             part = (part[0 : 4 * GROUP, :] + part[4 * GROUP :, :] + rest) * (1.0 / listed)
             start = pl.multiple_of(b * atoms + GROUP * i, GROUP)
             for x in range(4):
@@ -311,8 +315,8 @@
     for x in range(4):
         d_moment[x] = jnp.transpose(d_moment_t[x]) * (1.0 / listed)
 
-    row_of = lax.broadcasted_iota(jnp.int32, (atoms, width), 0)
-    lane_of = lax.broadcasted_iota(jnp.int32, (atoms, width), 1)
+    row_of = lax.broadcasted_iota(jnp.int32, (atoms, width), 0).astype(jnp.int16)
+    lane_of = lax.broadcasted_iota(jnp.int32, (1, width), 1)
 
     def backward(i, carry):
         for b in range(beads):
@@ -353,13 +357,15 @@
         ).astype(bf16)
         ix = index[i, 0:1, :]
         for j in range(len(sources)):
-            hot = jnp.where(row_of == ix - j * LANES, 1.0, 0.0)
+            one, none = jnp.ones((), bf16), jnp.zeros((), bf16)
+            hot = jnp.where(row_of == (ix - j * LANES).astype(jnp.int16), one, none)
             if j == 0:
-                hot = hot - jnp.where(row_of == GROUP * i + lane_of // listed, 1.0, 0.0)
-            totals[j * LANES : j * LANES + atoms, 0 : 6 * 8] += dot_nt(hot.astype(bf16), sides)
+                centre = (GROUP * i + lane_of // listed).astype(jnp.int16)
+                hot = hot - jnp.where(row_of == centre, one, none)
+            totals[j * LANES : j * LANES + atoms, 0 : 6 * 8] += dot_nt(hot, sides)
         return carry
 
-    lax.fori_loop(0, blocks, backward, 0)
+    lax.fori_loop(0, blocks, backward, 0, unroll=2)
 
     targets = ((own_f, 0), (near_f, 0), (link_f, 0), (link_f, rows), (near_f, rows))
     for j, (out, at) in enumerate(targets):

time: 54.3 us -> 52.8 us (0.972)
  Pallas kernels: 28.9 us -> 27.4 us
    pallas_call x1, Pallas kernels: 28.8 us -> 27.3 us  [on_device(): pl.pallas_call(force_kernel, out_shape=[shape((rows, atoms), f32), shape(...]
where the time goes in v5:
time: 52.8 us; the launch traced here: 52.4 us
  Pallas kernels  27.4 us (52%)
  waiting for transfers between devices  11.4 us (22%)
  starting transfers between devices  7.99 us (15%)
  local copies, waits for them, and re-layouts  4.86 us (9%)
  between operations  0.73 us (1%)
    pallas_call x1, Pallas kernels, on_device(): pl.pallas_call(force_kernel, out_shape=[shape((rows, atoms), f32), shape(...  27.3 us
    ppermute x6, waiting for transfers between devices, swapped(): return lax.ppermute(value, 'space', which + [(b, a) for a, b in which])  9.2 us
    ppermute x6, starting transfers between devices, swapped(): return lax.ppermute(value, 'space', which + [(b, a) for a, b in which])  6.48 us
    unnamed x27, local copies, waits for them, and re-layouts  4.18 us
    ppermute x1, waiting for transfers between devices, on_device(): result = shares[0] + lax.ppermute(shares[1], 'bead', [(0, 1), (1, 0)])  2.21 us
    ppermute x1, starting transfers between devices, on_device(): result = shares[0] + lax.ppermute(shares[1], 'bead', [(0, 1), (1, 0)])  1.5 us
  transfers between devices with their start and end apart: 7, of which 7 were waited for; matrix products, arithmetic and copies ran while one was open for 2% of the time, Pallas kernels for 0%

profile of v5, /device:TPU:8, one launch (start us, length us, event | category | flops | bytes accessed | tf_op | source)
XLA Modules:
  0.0 52.4 jit_solution(11637300286733196758)
XLA Ops:
  0.6 0.7 %copy-done.5 = f32[4,3,96]{2,0,1:T(4,128)S(1)} copy-done((f32[4,3,96]{2,0,1:T(4,128)S(1)}, f32[4,3,96]{2,0,1:T(4,128)}, u32[]{:S(2)}) %copy-start.5) | copy-done | bytes 4632
  1.4 0.7 %copy-done.6 = s32[1,4,96]{2,1,0:T(4,128)S(1)} copy-done((s32[1,4,96]{2,1,0:T(4,128)S(1)}, s32[1,4,96]{2,1,0:T(4,128)}, u32[]{:S(2)}) %copy-start.6) | copy-done | bytes 1560
  2.1 1.2 %collective-permute-done.core = f32[16,96]{1,0:T(8,128)S(1)} collective-permute-done((f32[16,96]{1,0:T(8,128)S(1)}, f32[16,96]{1,0:T(8,128)S(1)}, u32[]{:S(2)}, u32[]{:S(2)}) %collective-permute-start) | collective-permute-done | bytes 6176 | tf_op jit(solution)/shard_map/ppermute | solution.py:424
  3.2 3.1 %collective-permute-start.1 = (f32[32,96]{1,0:T(8,128)S(1)}, f32[32,96]{1,0:T(8,128)S(1)}, u32[]{:S(2)}, u32[]{:S(2)}) collective-permute-start(f32[32,96]{1,0:T(8,128)S(1)} %pad_maximum_fusion), channel_id=1, source_target_pairs={{2,4},{6,8},{10,12},{14,16},{18,20},{22,24},{26,28},{4,2},{8,6},{1... | collective-permute-start | bytes 36872 | tf_op jit(solution)/shard_map/ppermute | solution.py:424
  6.3 2.9 %collective-permute-done.1.link = f32[32,96]{1,0:T(8,128)S(1)} collective-permute-done((f32[32,96]{1,0:T(8,128)S(1)}, f32[32,96]{1,0:T(8,128)S(1)}, u32[]{:S(2)}, u32[]{:S(2)}) %collective-permute-start.1) | collective-permute-done | bytes 12320 | tf_op jit(solution)/shard_map/ppermute | solution.py:424
  9.2 0.8 %copy.17 = s32[96,64]{1,0:T(8,128)S(1)} copy(s32[96,64]{0,1:T(8,128)} %param.16) | data formatting | bytes 49152 | tf_op args[2]
  10.0 0.1 reshape.22.idx
  10.1 0.2 collective-permute-done.2.far
  10.4 0.4 copy-done.3
  10.8 0.3 copy-done.4
  11.1 0.0 copy-done.9
  11.1 0.0 copy-done.10
  11.1 0.0 copy-done.7
  11.1 1.2 %copy-done = bf16[2048,240]{0,1:T(8,128)(2,1)S(1)} copy-done((bf16[2048,240]{0,1:T(8,128)(2,1)S(1)}, bf16[2048,240]{0,1:T(8,128)(2,1)}, u32[]{:S(2)}) %copy-start) | copy-done | bytes 983064
  12.3 27.3 %forces.1 = (f32[12,96]{1,0:T(8,128)S(1)}, f32[24,96]{1,0:T(8,128)S(1)}, f32[24,96]{1,0:T(8,128)S(1)}) custom-call(f32[16,96]{1,0:T(8,128)S(1)} %pack.1.own, f32[3,4,96]{2,1,0:T(4,128)S(1)} %bitcast.13, f32[16,96]{1,0:T(8,128)S(1)} %collective-permute-done.core, f32[32,96]{1,0:T(8,128)S(1)} %collective-permute-done.1.link, ...), custom_call_target="tpu_custom_call" | custom-call | tf_op jit(solution)/shard_map/forces/pallas_call | solution.py:439
  39.6 0.3 collective-permute-start.3
  39.9 0.9 %collective-permute-done.3.near = f32[24,96]{1,0:T(8,128)S(1)} collective-permute-done((f32[24,96]{1,0:T(8,128)S(1)}, f32[24,96]{1,0:T(8,128)S(1)}, u32[]{:S(2)}, u32[]{:S(2)}) %collective-permute-start.3) | collective-permute-done | bytes 9248 | tf_op jit(solution)/shard_map/ppermute | solution.py:424
  40.9 3.1 %collective-permute-start.4 = (f32[24,96]{1,0:T(8,128)S(1)}, f32[24,96]{1,0:T(8,128)S(1)}, u32[]{:S(2)}, u32[]{:S(2)}) collective-permute-start(f32[24,96]{1,0:T(8,128)S(1)} %pad_maximum_fusion.1), channel_id=1, source_target_pairs={{2,4},{6,8},{10,12},{14,16},{18,20},{22,24},{26,28},{4,2},{8,6},{1... | collective-permute-start | bytes 27656 | tf_op jit(solution)/shard_map/ppermute | solution.py:424
  44.0 2.8 %collective-permute-done.4.link = f32[24,96]{1,0:T(8,128)S(1)} collective-permute-done((f32[24,96]{1,0:T(8,128)S(1)}, f32[24,96]{1,0:T(8,128)S(1)}, u32[]{:S(2)}, u32[]{:S(2)}) %collective-permute-start.4) | collective-permute-done | bytes 9248 | tf_op jit(solution)/shard_map/ppermute | solution.py:424
  46.8 1.2 %collective-permute-done.5.far = f32[24,96]{1,0:T(8,128)S(1)} collective-permute-done((f32[24,96]{1,0:T(8,128)S(1)}, f32[24,96]{1,0:T(8,128)S(1)}, u32[]{:S(2)}, u32[]{:S(2)}) %collective-permute-start.5) | collective-permute-done | bytes 9248 | tf_op jit(solution)/shard_map/ppermute | solution.py:424
  48.0 0.2 propagate.1
  48.1 1.5 %collective-permute-start.6 = (f32[6,4,96]{2,1,0:T(4,128)S(1)}, f32[6,4,96]{2,1,0:T(4,128)S(1)}, u32[]{:S(2)}, u32[]{:S(2)}) collective-permute-start(f32[6,4,96]{2,1,0:T(4,128)S(1)} %get-tuple-element.11), channel_id=1, source_target_pairs={{0,1},{1,0},{2,3},{3,2},{4,5},{5,4},{6,7},{7,6},{8,9},{9,8},{10,11... | collective-permute-start | bytes 27656 | tf_op jit(solution)/shard_map/ppermute | solution.py:495
  49.6 2.2 %collective-permute-done.6 = f32[6,4,96]{2,1,0:T(4,128)S(1)} collective-permute-done((f32[6,4,96]{2,1,0:T(4,128)S(1)}, f32[6,4,96]{2,1,0:T(4,128)S(1)}, u32[]{:S(2)}, u32[]{:S(2)}) %collective-permute-start.6) | collective-permute-done | bytes 9248 | tf_op jit(solution)/shard_map/ppermute | solution.py:495
  51.8 0.6 %slice_bitcast_fusion = (f32[4,3,96]{2,0,1:T(4,128)}, f32[4,3,96]{2,0,1:T(4,128)}) fusion(f32[6,4,96]{2,1,0:T(4,128)S(1)} %add.7), kind=kLoop, calls=%fused_computation.3 | loop fusion | bytes 18432 | tf_op jit(solution)/shard_map/transpose | solution.py:499
  (26 shorter events, 0.1 us)
Async XLA Ops:
  0.6 9.8 %copy-start.1 = (bf16[240,240]{1,0:T(8,128)(2,1)S(1)}, bf16[240,240]{1,0:T(8,128)(2,1)}, u32[]{:S(2)}) copy-start(bf16[240,240]{1,0:T(8,128)(2,1)} %fit_w2.1) | copy-start | bytes 345604
  0.6 0.7 %copy-start.5 = (f32[4,3,96]{2,0,1:T(4,128)S(1)}, f32[4,3,96]{2,0,1:T(4,128)}, u32[]{:S(2)}) copy-start(f32[4,3,96]{2,0,1:T(4,128)} %param.14) | copy-start | bytes 13828
  1.4 0.7 %copy-start.6 = (s32[1,4,96]{2,1,0:T(4,128)S(1)}, s32[1,4,96]{2,1,0:T(4,128)}, u32[]{:S(2)}) copy-start(s32[1,4,96]{2,1,0:T(4,128)} %send.1) | copy-start | bytes 4612
  2.1 1.2 %collective-permute-start = (f32[16,96]{1,0:T(8,128)S(1)}, f32[16,96]{1,0:T(8,128)S(1)}, u32[]{:S(2)}, u32[]{:S(2)}) collective-permute-start(f32[16,96]{1,0:T(8,128)S(1)} %pack.1.own), channel_id=1, source_target_pairs={{0,2},{4,6},{8,10},{12,14},{16,18},{20,22},{24,26},{28,30},{2,0},{... | collective-permute-start | bytes 18440 | tf_op jit(solution)/shard_map/ppermute | solution.py:424
  3.2 5.9 %collective-permute-start.1 = (f32[32,96]{1,0:T(8,128)S(1)}, f32[32,96]{1,0:T(8,128)S(1)}, u32[]{:S(2)}, u32[]{:S(2)}) collective-permute-start(f32[32,96]{1,0:T(8,128)S(1)} %pad_maximum_fusion), channel_id=1, source_target_pairs={{2,4},{6,8},{10,12},{14,16},{18,20},{22,24},{26,28},{4,2},{8,6},{1... | collective-permute-start | bytes 36872 | tf_op jit(solution)/shard_map/ppermute | solution.py:424
  9.2 1.2 %collective-permute-start.2 = (f32[32,96]{1,0:T(8,128)S(1)}, f32[32,96]{1,0:T(8,128)S(1)}, u32[]{:S(2)}, u32[]{:S(2)}) collective-permute-start(f32[32,96]{1,0:T(8,128)S(1)} %collective-permute-done.1.link), channel_id=1, source_target_pairs={{0,2},{4,6},{8,10},{12,14},{16,18},{20,22},{24,26},{28,30},{2,0},{... | collective-permute-start | bytes 36872 | tf_op jit(solution)/shard_map/ppermute | solution.py:424
  10.0 0.8 %copy-start.3 = (bf16[128,128]{1,0:T(8,128)(2,1)S(1)}, bf16[128,128]{1,0:T(8,128)(2,1)}, u32[]{:S(2)}) copy-start(bf16[128,128]{1,0:T(8,128)(2,1)} %w_embed.1) | copy-start | bytes 98308
  10.4 0.7 %copy-start.4 = (f32[4,3,96]{2,0,1:T(4,128)S(1)}, f32[4,3,96]{2,0,1:T(4,128)}, u32[]{:S(2)}) copy-start(f32[4,3,96]{2,0,1:T(4,128)} %param.15) | copy-start | bytes 13828
  10.4 0.7 %copy-start.8 = (f32[240]{0:T(256)S(1)}, f32[240]{0:T(256)}, u32[]{:S(2)}) copy-start(f32[240]{0:T(256)} %param.23) | copy-start | bytes 2884
  10.4 0.7 %copy-start.9 = (f32[240]{0:T(256)S(1)}, f32[240]{0:T(256)}, u32[]{:S(2)}) copy-start(f32[240]{0:T(256)} %param.25) | copy-start | bytes 2884
  10.4 0.7 %copy-start.10 = (f32[240]{0:T(256)S(1)}, f32[240]{0:T(256)}, u32[]{:S(2)}) copy-start(f32[240]{0:T(256)} %param.26) | copy-start | bytes 2884
  10.4 0.7 %copy-start.12 = (f32[128]{0:T(128)S(1)}, f32[128]{0:T(128)}, u32[]{:S(2)}) copy-start(f32[128]{0:T(128)} %param.21) | copy-start | bytes 1540
  10.4 0.7 %copy-start.7 = (f32[2,128]{1,0:T(2,128)S(1)}, f32[2,128]{1,0:T(2,128)}, u32[]{:S(2)}) copy-start(f32[2,128]{1,0:T(2,128)} %first.1) | copy-start | bytes 3076
  10.4 0.7 %copy-start.11 = (s32[96]{0:T(128)S(1)}, s32[96]{0:T(128)}, u32[]{:S(2)}) copy-start(s32[96]{0:T(128)} %param.17) | copy-start | bytes 1156
  11.1 1.2 %copy-start = (bf16[2048,240]{0,1:T(8,128)(2,1)S(1)}, bf16[2048,240]{0,1:T(8,128)(2,1)}, u32[]{:S(2)}) copy-start(bf16[2048,240]{0,1:T(8,128)(2,1)} %param.22) | copy-start | bytes 2949124
  39.6 8.4 %copy-start.2 = (f32[2,48,128]{2,1,0:T(8,128)S(1)}, f32[2,48,128]{2,1,0:T(8,128)}, u32[]{:S(2)}) copy-start(f32[2,48,128]{2,1,0:T(8,128)} %constant.2.clone.maps) | copy-start | bytes 147460
  39.6 1.2 %collective-permute-start.3 = (f32[24,96]{1,0:T(8,128)S(1)}, f32[24,96]{1,0:T(8,128)S(1)}, u32[]{:S(2)}, u32[]{:S(2)}) collective-permute-start(f32[24,96]{1,0:T(8,128)S(1)} %get-tuple-element.8), channel_id=1, source_target_pairs={{0,2},{4,6},{8,10},{12,14},{16,18},{20,22},{24,26},{28,30},{2,0},{... | collective-permute-start | bytes 27656 | tf_op jit(solution)/shard_map/ppermute | solution.py:424
  40.9 5.9 %collective-permute-start.4 = (f32[24,96]{1,0:T(8,128)S(1)}, f32[24,96]{1,0:T(8,128)S(1)}, u32[]{:S(2)}, u32[]{:S(2)}) collective-permute-start(f32[24,96]{1,0:T(8,128)S(1)} %pad_maximum_fusion.1), channel_id=1, source_target_pairs={{2,4},{6,8},{10,12},{14,16},{18,20},{22,24},{26,28},{4,2},{8,6},{1... | collective-permute-start | bytes 27656 | tf_op jit(solution)/shard_map/ppermute | solution.py:424
  46.8 1.2 %collective-permute-start.5 = (f32[24,96]{1,0:T(8,128)S(1)}, f32[24,96]{1,0:T(8,128)S(1)}, u32[]{:S(2)}, u32[]{:S(2)}) collective-permute-start(f32[24,96]{1,0:T(8,128)S(1)} %collective-permute-done.4.link), channel_id=1, source_target_pairs={{0,2},{4,6},{8,10},{12,14},{16,18},{20,22},{24,26},{28,30},{2,0},{... | collective-permute-start | bytes 27656 | tf_op jit(solution)/shard_map/ppermute | solution.py:424
  48.1 3.7 %collective-permute-start.6 = (f32[6,4,96]{2,1,0:T(4,128)S(1)}, f32[6,4,96]{2,1,0:T(4,128)S(1)}, u32[]{:S(2)}, u32[]{:S(2)}) collective-permute-start(f32[6,4,96]{2,1,0:T(4,128)S(1)} %get-tuple-element.11), channel_id=1, source_target_pairs={{0,1},{1,0},{2,3},{3,2},{4,5},{5,4},{6,7},{7,6},{8,9},{9,8},{10,11... | collective-permute-start | bytes 27656 | tf_op jit(solution)/shard_map/ppermute | solution.py:495

commit v6 on v5

--- a/solution.py
+++ b/solution.py
@@ -263,7 +263,7 @@
                 moment[x, pl.ds(start, GROUP), :] = part[x * GROUP : (x + 1) * GROUP, :]
         return carry
 
-    lax.fori_loop(0, blocks, embed, 0)
+    lax.fori_loop(0, blocks, embed, 0, unroll=2)
 
     for x in range(4):
         moment_t[x] = jnp.transpose(moment[x])

time: 52.8 us -> 51.7 us (0.979)
  Pallas kernels: 27.4 us -> 26.3 us
    pallas_call x1, Pallas kernels: 27.3 us -> 26.1 us  [on_device(): pl.pallas_call(force_kernel, out_shape=[shape((rows, atoms), f32), shape(...]
where the time goes in v6:
time: 51.7 us; the launch traced here: 51.3 us
  Pallas kernels  26.3 us (51%)
  waiting for transfers between devices  11.4 us (22%)
  starting transfers between devices  8.01 us (15%)
  local copies, waits for them, and re-layouts  4.86 us (9%)
  between operations  0.73 us (1%)
    pallas_call x1, Pallas kernels, on_device(): pl.pallas_call(force_kernel, out_shape=[shape((rows, atoms), f32), shape(...  26.1 us
    ppermute x6, waiting for transfers between devices, swapped(): return lax.ppermute(value, 'space', which + [(b, a) for a, b in which])  9.19 us
    ppermute x6, starting transfers between devices, swapped(): return lax.ppermute(value, 'space', which + [(b, a) for a, b in which])  6.5 us
    unnamed x27, local copies, waits for them, and re-layouts  4.18 us
    ppermute x1, waiting for transfers between devices, on_device(): result = shares[0] + lax.ppermute(shares[1], 'bead', [(0, 1), (1, 0)])  2.2 us
    ppermute x1, starting transfers between devices, on_device(): result = shares[0] + lax.ppermute(shares[1], 'bead', [(0, 1), (1, 0)])  1.51 us
  transfers between devices with their start and end apart: 7, of which 7 were waited for; matrix products, arithmetic and copies ran while one was open for 2% of the time, Pallas kernels for 0%

profile of v6, /device:TPU:8, one launch (start us, length us, event | category | flops | bytes accessed | tf_op | source)
XLA Modules:
  0.0 51.3 jit_solution(10554073100771968450)
XLA Ops:
  0.6 0.7 %copy-done.5 = f32[4,3,96]{2,0,1:T(4,128)S(1)} copy-done((f32[4,3,96]{2,0,1:T(4,128)S(1)}, f32[4,3,96]{2,0,1:T(4,128)}, u32[]{:S(2)}) %copy-start.5) | copy-done | bytes 4632
  1.4 0.7 %copy-done.6 = s32[1,4,96]{2,1,0:T(4,128)S(1)} copy-done((s32[1,4,96]{2,1,0:T(4,128)S(1)}, s32[1,4,96]{2,1,0:T(4,128)}, u32[]{:S(2)}) %copy-start.6) | copy-done | bytes 1560
  2.1 1.2 %collective-permute-done.core = f32[16,96]{1,0:T(8,128)S(1)} collective-permute-done((f32[16,96]{1,0:T(8,128)S(1)}, f32[16,96]{1,0:T(8,128)S(1)}, u32[]{:S(2)}, u32[]{:S(2)}) %collective-permute-start) | collective-permute-done | bytes 6176 | tf_op jit(solution)/shard_map/ppermute | solution.py:424
  3.2 3.1 %collective-permute-start.1 = (f32[32,96]{1,0:T(8,128)S(1)}, f32[32,96]{1,0:T(8,128)S(1)}, u32[]{:S(2)}, u32[]{:S(2)}) collective-permute-start(f32[32,96]{1,0:T(8,128)S(1)} %pad_maximum_fusion), channel_id=1, source_target_pairs={{2,4},{6,8},{10,12},{14,16},{18,20},{22,24},{26,28},{4,2},{8,6},{1... | collective-permute-start | bytes 36872 | tf_op jit(solution)/shard_map/ppermute | solution.py:424
  6.3 2.9 %collective-permute-done.1.link = f32[32,96]{1,0:T(8,128)S(1)} collective-permute-done((f32[32,96]{1,0:T(8,128)S(1)}, f32[32,96]{1,0:T(8,128)S(1)}, u32[]{:S(2)}, u32[]{:S(2)}) %collective-permute-start.1) | collective-permute-done | bytes 12320 | tf_op jit(solution)/shard_map/ppermute | solution.py:424
  9.2 0.8 %copy.17 = s32[96,64]{1,0:T(8,128)S(1)} copy(s32[96,64]{0,1:T(8,128)} %param.16) | data formatting | bytes 49152 | tf_op args[2]
  10.0 0.1 reshape.22.idx
  10.1 0.2 collective-permute-done.2.far
  10.4 0.4 copy-done.3
  10.8 0.3 copy-done.4
  11.1 0.0 copy-done.9
  11.1 0.0 copy-done.10
  11.1 0.0 copy-done.7
  11.1 1.2 %copy-done = bf16[2048,240]{0,1:T(8,128)(2,1)S(1)} copy-done((bf16[2048,240]{0,1:T(8,128)(2,1)S(1)}, bf16[2048,240]{0,1:T(8,128)(2,1)}, u32[]{:S(2)}) %copy-start) | copy-done | bytes 983064
  12.3 26.1 %forces.1 = (f32[12,96]{1,0:T(8,128)S(1)}, f32[24,96]{1,0:T(8,128)S(1)}, f32[24,96]{1,0:T(8,128)S(1)}) custom-call(f32[16,96]{1,0:T(8,128)S(1)} %pack.1.own, f32[3,4,96]{2,1,0:T(4,128)S(1)} %bitcast.13, f32[16,96]{1,0:T(8,128)S(1)} %collective-permute-done.core, f32[32,96]{1,0:T(8,128)S(1)} %collective-permute-done.1.link, ...), custom_call_target="tpu_custom_call" | custom-call | tf_op jit(solution)/shard_map/forces/pallas_call | solution.py:439
  38.5 0.3 collective-permute-start.3
  38.8 0.9 %collective-permute-done.3.near = f32[24,96]{1,0:T(8,128)S(1)} collective-permute-done((f32[24,96]{1,0:T(8,128)S(1)}, f32[24,96]{1,0:T(8,128)S(1)}, u32[]{:S(2)}, u32[]{:S(2)}) %collective-permute-start.3) | collective-permute-done | bytes 9248 | tf_op jit(solution)/shard_map/ppermute | solution.py:424
  39.7 3.1 %collective-permute-start.4 = (f32[24,96]{1,0:T(8,128)S(1)}, f32[24,96]{1,0:T(8,128)S(1)}, u32[]{:S(2)}, u32[]{:S(2)}) collective-permute-start(f32[24,96]{1,0:T(8,128)S(1)} %pad_maximum_fusion.1), channel_id=1, source_target_pairs={{2,4},{6,8},{10,12},{14,16},{18,20},{22,24},{26,28},{4,2},{8,6},{1... | collective-permute-start | bytes 27656 | tf_op jit(solution)/shard_map/ppermute | solution.py:424
  42.8 2.8 %collective-permute-done.4.link = f32[24,96]{1,0:T(8,128)S(1)} collective-permute-done((f32[24,96]{1,0:T(8,128)S(1)}, f32[24,96]{1,0:T(8,128)S(1)}, u32[]{:S(2)}, u32[]{:S(2)}) %collective-permute-start.4) | collective-permute-done | bytes 9248 | tf_op jit(solution)/shard_map/ppermute | solution.py:424
  45.6 1.2 %collective-permute-done.5.far = f32[24,96]{1,0:T(8,128)S(1)} collective-permute-done((f32[24,96]{1,0:T(8,128)S(1)}, f32[24,96]{1,0:T(8,128)S(1)}, u32[]{:S(2)}, u32[]{:S(2)}) %collective-permute-start.5) | collective-permute-done | bytes 9248 | tf_op jit(solution)/shard_map/ppermute | solution.py:424
  46.8 0.2 propagate.1
  47.0 1.5 %collective-permute-start.6 = (f32[6,4,96]{2,1,0:T(4,128)S(1)}, f32[6,4,96]{2,1,0:T(4,128)S(1)}, u32[]{:S(2)}, u32[]{:S(2)}) collective-permute-start(f32[6,4,96]{2,1,0:T(4,128)S(1)} %get-tuple-element.11), channel_id=1, source_target_pairs={{0,1},{1,0},{2,3},{3,2},{4,5},{5,4},{6,7},{7,6},{8,9},{9,8},{10,11... | collective-permute-start | bytes 27656 | tf_op jit(solution)/shard_map/ppermute | solution.py:495
  48.5 2.2 %collective-permute-done.6 = f32[6,4,96]{2,1,0:T(4,128)S(1)} collective-permute-done((f32[6,4,96]{2,1,0:T(4,128)S(1)}, f32[6,4,96]{2,1,0:T(4,128)S(1)}, u32[]{:S(2)}, u32[]{:S(2)}) %collective-permute-start.6) | collective-permute-done | bytes 9248 | tf_op jit(solution)/shard_map/ppermute | solution.py:495
  50.7 0.6 %slice_bitcast_fusion = (f32[4,3,96]{2,0,1:T(4,128)}, f32[4,3,96]{2,0,1:T(4,128)}) fusion(f32[6,4,96]{2,1,0:T(4,128)S(1)} %add.7), kind=kLoop, calls=%fused_computation.3 | loop fusion | bytes 18432 | tf_op jit(solution)/shard_map/transpose | solution.py:499
  (26 shorter events, 0.1 us)
Async XLA Ops:
  0.6 9.8 %copy-start.1 = (bf16[240,240]{1,0:T(8,128)(2,1)S(1)}, bf16[240,240]{1,0:T(8,128)(2,1)}, u32[]{:S(2)}) copy-start(bf16[240,240]{1,0:T(8,128)(2,1)} %fit_w2.1) | copy-start | bytes 345604
  0.6 0.7 %copy-start.5 = (f32[4,3,96]{2,0,1:T(4,128)S(1)}, f32[4,3,96]{2,0,1:T(4,128)}, u32[]{:S(2)}) copy-start(f32[4,3,96]{2,0,1:T(4,128)} %param.14) | copy-start | bytes 13828
  1.4 0.7 %copy-start.6 = (s32[1,4,96]{2,1,0:T(4,128)S(1)}, s32[1,4,96]{2,1,0:T(4,128)}, u32[]{:S(2)}) copy-start(s32[1,4,96]{2,1,0:T(4,128)} %send.1) | copy-start | bytes 4612
  2.1 1.2 %collective-permute-start = (f32[16,96]{1,0:T(8,128)S(1)}, f32[16,96]{1,0:T(8,128)S(1)}, u32[]{:S(2)}, u32[]{:S(2)}) collective-permute-start(f32[16,96]{1,0:T(8,128)S(1)} %pack.1.own), channel_id=1, source_target_pairs={{0,2},{4,6},{8,10},{12,14},{16,18},{20,22},{24,26},{28,30},{2,0},{... | collective-permute-start | bytes 18440 | tf_op jit(solution)/shard_map/ppermute | solution.py:424
  3.2 5.9 %collective-permute-start.1 = (f32[32,96]{1,0:T(8,128)S(1)}, f32[32,96]{1,0:T(8,128)S(1)}, u32[]{:S(2)}, u32[]{:S(2)}) collective-permute-start(f32[32,96]{1,0:T(8,128)S(1)} %pad_maximum_fusion), channel_id=1, source_target_pairs={{2,4},{6,8},{10,12},{14,16},{18,20},{22,24},{26,28},{4,2},{8,6},{1... | collective-permute-start | bytes 36872 | tf_op jit(solution)/shard_map/ppermute | solution.py:424
  9.2 1.2 %collective-permute-start.2 = (f32[32,96]{1,0:T(8,128)S(1)}, f32[32,96]{1,0:T(8,128)S(1)}, u32[]{:S(2)}, u32[]{:S(2)}) collective-permute-start(f32[32,96]{1,0:T(8,128)S(1)} %collective-permute-done.1.link), channel_id=1, source_target_pairs={{0,2},{4,6},{8,10},{12,14},{16,18},{20,22},{24,26},{28,30},{2,0},{... | collective-permute-start | bytes 36872 | tf_op jit(solution)/shard_map/ppermute | solution.py:424
  10.0 0.8 %copy-start.3 = (bf16[128,128]{1,0:T(8,128)(2,1)S(1)}, bf16[128,128]{1,0:T(8,128)(2,1)}, u32[]{:S(2)}) copy-start(bf16[128,128]{1,0:T(8,128)(2,1)} %w_embed.1) | copy-start | bytes 98308
  10.4 0.7 %copy-start.4 = (f32[4,3,96]{2,0,1:T(4,128)S(1)}, f32[4,3,96]{2,0,1:T(4,128)}, u32[]{:S(2)}) copy-start(f32[4,3,96]{2,0,1:T(4,128)} %param.15) | copy-start | bytes 13828
  10.4 0.7 %copy-start.8 = (f32[240]{0:T(256)S(1)}, f32[240]{0:T(256)}, u32[]{:S(2)}) copy-start(f32[240]{0:T(256)} %param.23) | copy-start | bytes 2884
  10.4 0.7 %copy-start.9 = (f32[240]{0:T(256)S(1)}, f32[240]{0:T(256)}, u32[]{:S(2)}) copy-start(f32[240]{0:T(256)} %param.25) | copy-start | bytes 2884
  10.4 0.7 %copy-start.10 = (f32[240]{0:T(256)S(1)}, f32[240]{0:T(256)}, u32[]{:S(2)}) copy-start(f32[240]{0:T(256)} %param.26) | copy-start | bytes 2884
  10.4 0.7 %copy-start.12 = (f32[128]{0:T(128)S(1)}, f32[128]{0:T(128)}, u32[]{:S(2)}) copy-start(f32[128]{0:T(128)} %param.21) | copy-start | bytes 1540
  10.4 0.7 %copy-start.7 = (f32[2,128]{1,0:T(2,128)S(1)}, f32[2,128]{1,0:T(2,128)}, u32[]{:S(2)}) copy-start(f32[2,128]{1,0:T(2,128)} %first.1) | copy-start | bytes 3076
  10.4 0.7 %copy-start.11 = (s32[96]{0:T(128)S(1)}, s32[96]{0:T(128)}, u32[]{:S(2)}) copy-start(s32[96]{0:T(128)} %param.17) | copy-start | bytes 1156
  11.1 1.2 %copy-start = (bf16[2048,240]{0,1:T(8,128)(2,1)S(1)}, bf16[2048,240]{0,1:T(8,128)(2,1)}, u32[]{:S(2)}) copy-start(bf16[2048,240]{0,1:T(8,128)(2,1)} %param.22) | copy-start | bytes 2949124
  38.5 8.4 %copy-start.2 = (f32[2,48,128]{2,1,0:T(8,128)S(1)}, f32[2,48,128]{2,1,0:T(8,128)}, u32[]{:S(2)}) copy-start(f32[2,48,128]{2,1,0:T(8,128)} %constant.2.clone.maps) | copy-start | bytes 147460
  38.5 1.2 %collective-permute-start.3 = (f32[24,96]{1,0:T(8,128)S(1)}, f32[24,96]{1,0:T(8,128)S(1)}, u32[]{:S(2)}, u32[]{:S(2)}) collective-permute-start(f32[24,96]{1,0:T(8,128)S(1)} %get-tuple-element.8), channel_id=1, source_target_pairs={{0,2},{4,6},{8,10},{12,14},{16,18},{20,22},{24,26},{28,30},{2,0},{... | collective-permute-start | bytes 27656 | tf_op jit(solution)/shard_map/ppermute | solution.py:424
  39.7 5.9 %collective-permute-start.4 = (f32[24,96]{1,0:T(8,128)S(1)}, f32[24,96]{1,0:T(8,128)S(1)}, u32[]{:S(2)}, u32[]{:S(2)}) collective-permute-start(f32[24,96]{1,0:T(8,128)S(1)} %pad_maximum_fusion.1), channel_id=1, source_target_pairs={{2,4},{6,8},{10,12},{14,16},{18,20},{22,24},{26,28},{4,2},{8,6},{1... | collective-permute-start | bytes 27656 | tf_op jit(solution)/shard_map/ppermute | solution.py:424
  45.6 1.2 %collective-permute-start.5 = (f32[24,96]{1,0:T(8,128)S(1)}, f32[24,96]{1,0:T(8,128)S(1)}, u32[]{:S(2)}, u32[]{:S(2)}) collective-permute-start(f32[24,96]{1,0:T(8,128)S(1)} %collective-permute-done.4.link), channel_id=1, source_target_pairs={{0,2},{4,6},{8,10},{12,14},{16,18},{20,22},{24,26},{28,30},{2,0},{... | collective-permute-start | bytes 27656 | tf_op jit(solution)/shard_map/ppermute | solution.py:424
  47.0 3.7 %collective-permute-start.6 = (f32[6,4,96]{2,1,0:T(4,128)S(1)}, f32[6,4,96]{2,1,0:T(4,128)S(1)}, u32[]{:S(2)}, u32[]{:S(2)}) collective-permute-start(f32[6,4,96]{2,1,0:T(4,128)S(1)} %get-tuple-element.11), channel_id=1, source_target_pairs={{0,1},{1,0},{2,3},{3,2},{4,5},{5,4},{6,7},{7,6},{8,9},{9,8},{10,11... | collective-permute-start | bytes 27656 | tf_op jit(solution)/shard_map/ppermute | solution.py:495
